TPU v7x, 128 devices: a whole 4x4x4 slice. The times are simulated.
128 devices in a mesh: sfc: 128 (over z, y, x, core).
Axes of the slice: x: 4, y: 4, z: 4, core: 2. Of those that a mesh axis runs over, the one named last changes fastest.
Arguments:
- state: float32 [5, 512, 16384], P(None, None, 'sfc'), as said below
- register: float32 [5, 512, 16384], P(None, None, 'sfc'), may hold values from -3 to 3
- metric: float32 [16384], P('sfc'), may hold values from 1 to 4
- counts: int32 [128], P('sfc'), may hold values from 96 to 128, as said below
- send_slots: int32 [16384, 16], P('sfc'), may hold values from 0 to 768, as said below
- mortar_refs: int32 [4096, 5], P('sfc'), may hold values from 0 to 2815, as said below
- face_refs: int32 [16384, 2], P('sfc'), may hold values from 0 to 2815, as said below
Outputs:
- state_next: float32 [5, 512, 16384], P(None, None, 'sfc')
- register_next: float32 [5, 512, 16384], P(None, None, 'sfc')
Inputs may be any that keep to these rules, and one draw needn't show every extreme that they name: `counts`: at least 96; some device has exactly that many and some device is full. `send_slots`: row q * 128 + r lists face slots of live elements of device q whose traces device r needs, live entries first and 768 in the unused rest. Rows are nonempty only for r - q equal to 1, -1, 2, -2 or 128 / 2 modulo 128; each such row holds at least half of 16 live entries and every device fills one of its rows completely. No slot appears twice on a device. `mortar_refs`: each entry is a reference of the evaluating device that names a face slot of a live element; over all mortar_refs and face_refs, every face slot of the forest is named at most once, and every live entry of send_slots is named exactly once. `face_refs`: as for mortar_refs. `state`: density and pressure are positive.
All inputs are finite; a program needn't handle non-finite values.
Results may differ from a plain program's by a relative error of at most 0.0003.
Values sent between devices are 32-bit elements; how exact they have to be, the bound alone decides.
No kernel may reach another device: no remote copies, remote signals or barrier semaphores. Data moves between devices by JAX's collectives and lax.ppermute only.
A program may use at most 128 MiB of HBM per device.

v0:
```python
import jax
import jax.numpy as jnp
import numpy as np
from jax import lax
from jax.sharding import PartitionSpec as P

GAMMA = 1.4
LIFT = 28.0
COURANT = 0.02
SECTION_A = -0.4178904745
SECTION_B = 0.3792103129999
HIGHEST = lax.Precision.HIGHEST
GLL_NODES = (
    -1.0,
    -0.8717401485096066,
    -0.5917001814331423,
    -0.2092992179024789,
    0.2092992179024789,
    0.5917001814331423,
    0.8717401485096066,
    1.0,
)
GLL_WEIGHTS = (
    0.03571428571428571,
    0.2107042271435061,
    0.3411226924835044,
    0.4124587946587038,
    0.4124587946587038,
    0.3411226924835044,
    0.2107042271435061,
    0.03571428571428571,
)


def interp_matrix(nodes, points):
    matrix = np.ones((len(points), len(nodes)))
    for source in range(len(nodes)):
        for other in range(len(nodes)):
            if other != source:
                matrix[:, source] *= (points - nodes[other]) / (nodes[source] - nodes[other])
    return matrix


def node_tables():
    number = 8
    nodes = np.array(GLL_NODES)
    weights = np.array(GLL_WEIGHTS)
    differ = nodes[:, None] - nodes[None, :] + np.eye(number)
    barycentric = 1.0 / np.prod(differ, axis=1)
    deriv = barycentric[None, :] / barycentric[:, None] / differ
    deriv = deriv * (1.0 - np.eye(number))
    deriv = deriv - np.eye(number) * deriv.sum(axis=1)[:, None]
    halves = [interp_matrix(nodes, (nodes - 1.0) / 2.0), interp_matrix(nodes, (nodes + 1.0) / 2.0)]
    backs = [0.5 * (half.T * weights[None, :]) / weights[:, None] for half in halves]
    project_cols = []
    back_rows = []
    for first in range(2):
        for second in range(2):
            project_cols.append(np.kron(halves[first], halves[second]).T)
            back_rows.append(np.kron(backs[first], backs[second]).T)
    project_stack = np.concatenate(project_cols, axis=1)
    back_stack = np.concatenate(back_rows, axis=0)
    return (
        jnp.asarray(deriv, jnp.float32),
        jnp.asarray(project_stack, jnp.float32),
        jnp.asarray(back_stack, jnp.float32),
    )


def normal_flux(fields, normal):
    density, mom_one, mom_two, mom_three, energy = fields
    inverse = 1.0 / density
    kinetic = 0.5 * (mom_one * mom_one + mom_two * mom_two + mom_three * mom_three) * inverse
    press = (GAMMA - 1.0) * (energy - kinetic)
    flow = mom_one * normal[0] + mom_two * normal[1] + mom_three * normal[2]
    speed = flow * inverse
    return [
        flow,
        mom_one * speed + press * normal[0],
        mom_two * speed + press * normal[1],
        mom_three * speed + press * normal[2],
        (energy + press) * speed,
    ]


def wave_speed(cube):
    density, mom_one, mom_two, mom_three, energy = [cube[field] for field in range(5)]
    inverse = 1.0 / density
    square = mom_one * mom_one + mom_two * mom_two + mom_three * mom_three
    press = (GAMMA - 1.0) * (energy - 0.5 * square * inverse)
    return jnp.sqrt(square) * inverse + jnp.sqrt(GAMMA * press * inverse)


def volume_terms(cube, metric, deriv):
    fields = [cube[field] for field in range(5)]
    forms = ["ia,fabce->fibce", "ib,fabce->faice", "ic,fabce->fabie"]
    total = jnp.zeros_like(cube)
    for axis in range(3):
        normal = tuple((1.0 if comp == axis else 0.0 for comp in range(3)))
        flux = jnp.stack(normal_flux(fields, normal))
        total = total + jnp.einsum(forms[axis], deriv, flux, precision=HIGHEST)
    return -metric * total


def face_tables(cube):
    tables = []
    for face in range(6):
        axis = face // 2
        side = face % 2
        layer = lax.index_in_dim(cube, 7 * side, axis + 1, keepdims=False)
        flat = layer.reshape(5, 64, layer.shape[-1])
        sign = 2.0 * side - 1.0
        normal = tuple((sign if comp == axis else 0.0 for comp in range(3)))
        flux = jnp.stack(normal_flux([flat[field] for field in range(5)], normal))
        both = jnp.concatenate([flat, flux], axis=0)
        tables.append(both.reshape(640, layer.shape[-1]).T)
    return jnp.concatenate(tables, axis=0)


def lift_faces(rhs_cube, corrections, metric):
    elems = metric.shape[0]
    for face in range(6):
        axis = face // 2
        side = face % 2
        block = corrections[face * elems : (face + 1) * elems]
        layer = block.T.reshape(5, 8, 8, elems)
        index = [slice(None)] * 5
        index[axis + 1] = 7 * side
        rhs_cube = rhs_cube.at[tuple(index)].add(-LIFT * metric * layer)
    return rhs_cube


def mortar_terms(rows, lam, project_stack, back_stack):
    number = rows.shape[0]
    large = rows[:, 0].reshape(number * 10, 64)
    spread = jnp.dot(large, project_stack, precision=HIGHEST).reshape(number, 10, 4, 64)
    spread = jnp.transpose(spread, (0, 2, 1, 3))
    small = rows[:, 1:].reshape(number, 4, 10, 64)
    star = 0.5 * (spread[:, :, 5:] - small[:, :, 5:]) - 0.5 * lam * (
        small[:, :, :5] - spread[:, :, :5]
    )
    child = -star - small[:, :, 5:]
    folded = jnp.transpose(star, (0, 2, 1, 3)).reshape(number * 5, 256)
    large_corr = jnp.dot(folded, back_stack, precision=HIGHEST).reshape(number, 5, 64)
    large_corr = large_corr - rows[:, 0, 320:].reshape(number, 5, 64)
    joined = jnp.concatenate([large_corr[:, None], child], axis=1)
    return joined.reshape(number * 5, 320)


def face_terms(rows, lam):
    left = rows[:, 0]
    right = rows[:, 1]
    star = 0.5 * (left[:, 320:] - right[:, 320:]) - 0.5 * lam * (right[:, :320] - left[:, :320])
    return jnp.stack([star - left[:, 320:], -star - right[:, 320:]], axis=1).reshape(-1, 320)


def per_device(state, register, metric, counts, send_slots, mortar_refs, face_refs):
    deriv, project_stack, back_stack = node_tables()
    elems = metric.shape[0]
    slots = 6 * elems
    width = send_slots.shape[1]
    devices = lax.axis_size("sfc")
    cube = state.reshape(5, 8, 8, 8, elems)
    live = jnp.arange(elems, dtype=jnp.int32) < counts[0]
    fastest = jnp.max(jnp.where(live, wave_speed(cube), jnp.float32(0.0)))
    lam = lax.pmax(fastest, "sfc")
    table = face_tables(cube)
    outgoing = jnp.take(table, send_slots, axis=0, mode="fill", fill_value=0.0)
    incoming = lax.all_to_all(outgoing, "sfc", split_axis=0, concat_axis=0, tiled=True).reshape(
        devices * width, 640
    )
    volume = volume_terms(cube, metric, deriv)
    pool = jnp.concatenate([table, incoming], axis=0)
    corr_m = mortar_terms(pool[mortar_refs], lam, project_stack, back_stack)
    corr_f = face_terms(pool[face_refs], lam)
    corr_pool = jnp.zeros((pool.shape[0], 320), jnp.float32)
    corr_pool = corr_pool.at[mortar_refs.reshape(-1)].add(corr_m)
    corr_pool = corr_pool.at[face_refs.reshape(-1)].add(corr_f)
    local_corr = corr_pool[:slots]
    remote_corr = corr_pool[slots:].reshape(-1, width, 320)
    returned = lax.all_to_all(remote_corr, "sfc", split_axis=0, concat_axis=0, tiled=True)
    local_corr = local_corr.at[send_slots.reshape(-1)].add(returned.reshape(-1, 320), mode="drop")
    rhs = lift_faces(volume, local_corr, metric).reshape(5, 512, elems) * live.astype(jnp.float32)
    step = COURANT / lam
    register_next = SECTION_A * register + step * rhs
    state_next = state + SECTION_B * register_next
    return (state_next, register_next)


def solution(mesh):
    return jax.shard_map(
        per_device,
        mesh=mesh,
        in_specs=(
            P(None, None, "sfc"),
            P(None, None, "sfc"),
            P("sfc"),
            P("sfc"),
            P("sfc", None),
            P("sfc", None),
            P("sfc", None),
        ),
        out_specs=(P(None, None, "sfc"), P(None, None, "sfc")),
        check_vma=False,
    )
```

profile of v0, /device:TPU:0, one launch (start us, length us, event | category | flops | bytes accessed | tf_op | source)
XLA Modules:
  0.0 310.2 jit_solution(16041888985706922029)
XLA Ops:
  0.6 2.0 fusion.21
  10.1 1.7 bitcast_dynamic-update-slice_fusion.11
  11.8 1.9 copy.158
  13.7 1.9 copy.159
  23.3 1.9 copy.160
  31.3 1.9 copy.161
  33.5 1.8 bitcast_dynamic-update-slice_fusion.9
  35.3 1.8 bitcast_dynamic-update-slice_fusion.7
  39.5 9.4 %gather_fusion = f32[2048,640]{1,0:T(8,128)} fusion(f32[768,640]{1,0:T(8,128)S(1)} %get-tuple-element.165, s32[2048]{0:T(1024)S(1)} %broadcast_clamp_fusion), kind=kCustom, calls=%fused_computation | custom fusion | bytes 10493952 | tf_op jit(solution)/shard_map/jit(_take)/gather | solution.py:168
  48.8 4.3 %broadcast_select_fusion = f32[128,16,640]{2,1,0:T(8,128)} fusion(f32[128,16,640]{2,1,0:T(8,128)} %bitcast.371, pred[128,16]{1,0:T(8,128)(4,1)S(1)} %copy.162), kind=kLoop, calls=%fused_computation.6 | loop fusion | flops 1310720 | bytes 10487808 | tf_op jit(solution)/shard_map/jit(_take)/select_n | solution.py:168
  53.1 11.6 %all-to-all-start = ((f32[128,16,640]{2,1,0:T(8,128)}), f32[128,16,640]{2,1,0:T(8,128)}, u32[]{:S(2)}, u32[]{:S(2)}) async-start(f32[128,16,640]{2,1,0:T(8,128)} %broadcast_select_fusion), calls=%async_computation | async-start | bytes 10485760 | tf_op jit(solution)/shard_map/all_to_all | solution.py:169
  66.3 113.0 %pmax.7 = f32[]{:T(128)} all-reduce(f32[]{:T(128)} %get-tuple-element.105), channel_id=1, replica_groups=mesh['sfc'=128] {'sfc'}, use_global_device_ids=true, to_apply=%region_1.2 | all-reduce | flops 1 | bytes 8 | tf_op jit(solution)/shard_map/pmax | solution.py:166
  185.9 5.1 %constant_dynamic-update-slice_fusion.35 = f32[2816,640]{1,0:T(8,128)} fusion(f32[2816,640]{1,0:T(8,128)} %get-tuple-element.166, f32[2048,640]{1,0:T(8,128)} %bitcast.63), kind=kLoop, calls=%fused_computation.135 | loop fusion | bytes 10485760 | tf_op jit(solution)/shard_map/concatenate | solution.py:173
  191.0 4.1 %gather_fusion.1 = f32[160,640]{1,0:T(8,128)S(1)} fusion(f32[2816,640]{1,0:T(8,128)} %constant_dynamic-update-slice_fusion.35, s32[1024]{0:T(1024)S(1)} %get-tuple-element.180), kind=kCustom, calls=%fused_computation.1 | custom fusion | bytes 819840 | tf_op jit(solution)/shard_map/gather | solution.py:174
  196.0 1.9 slice.564
  200.4 4.3 %gather_fusion.2 = f32[256,640]{1,0:T(8,128)S(1)} fusion(f32[2816,640]{1,0:T(8,128)} %constant_dynamic-update-slice_fusion.35, s32[1024]{0:T(1024)S(1)} %get-tuple-element.179), kind=kCustom, calls=%fused_computation.2 | custom fusion | bytes 1311744 | tf_op jit(solution)/shard_map/gather | solution.py:175
  206.0 1.9 fusion.48
  216.6 3.9 %scatter_custom_fusion = f32[2816,320]{1,0:T(8,128)} fusion(s32[160]{0:T(256)} %bitcast.428, f32[160,320]{1,0:T(8,128)S(1)} %reshape.2706, f32[]{:T(128)} %constant.219.clone.1), kind=kCustom, calls=%fused_computation.7 | custom fusion | flops 51200 | bytes 3604992 | tf_op jit(solution)/shard_map/scatter-add | solution.py:177
  220.5 6.3 %scatter_fusion = f32[2816,320]{1,0:T(8,128)} fusion(f32[2816,320]{1,0:T(8,128)} %scatter_custom_fusion, s32[256]{0:T(256)S(1)} %bitcast.427, f32[256,320]{1,0:T(8,128)S(1)} %copy-done.9), kind=kCustom, calls=%fused_computation.4 | custom fusion | flops 81920 | bytes 984064 | tf_op jit(solution)/shard_map/scatter-add | solution.py:178
  226.8 3.8 %slice.576 = f32[2048,320]{1,0:T(8,128)} slice(f32[2816,320]{1,0:T(8,128)} %scatter_fusion), slice={[768:2816], [0:320]} | slice | bytes 5242880 | tf_op jit(solution)/shard_map/slice | solution.py:180
  230.6 7.0 %all-to-all-start.1 = ((f32[128,16,320]{2,1,0:T(8,128)}), f32[128,16,320]{2,1,0:T(8,128)}, u32[]{:S(2)}, u32[]{:S(2)}) async-start(f32[128,16,320]{2,1,0:T(8,128)} %bitcast.372), calls=%async_computation.1 | async-start | bytes 6291456 | tf_op jit(solution)/shard_map/all_to_all | solution.py:181
  237.6 1.7 add_dynamic-update-slice_fusion.2
  242.5 2.7 fusion.7
  245.2 3.4 %fusion.9 = f32[5,8,8,128,8]{3,4,2,1,0:T(8,128)S(1)} fusion(f32[8,8,1,1,1]{1,0,4,3,2:T(8,128)S(1)} %copy-done.18, f32[5,8,8,8,128]{4,1,3,2,0:T(8,128)} %get-tuple-element.156), kind=kOutput, calls=%fused_computation.18 | convolution fusion | flops 31457280 | bytes 2621696 | tf_op jit(solution)/shard_map/ib,fabce->faice/dot_general | solution.py:101
  248.6 3.6 %fusion.4 = f32[5,8,8,8,128]{4,1,3,2,0:T(8,128)} fusion(f32[5,8,8,8,128]{4,1,3,2,0:T(8,128)S(1)} %copy-done.8, f32[8,8,1,1,1]{1,0,4,3,2:T(8,128)S(1)} %copy-done.18, f32[5,8,8,128,8]{3,4,2,1,0:T(8,128)S(1)} %fusion.7, f32[5,8,8,128,8]{3,4,2,1,0:T(8,128)S(1)} %fusion.9, f32[128]{0:T(128)S(1)} %copy-done.22), kind=kOutput, calls=%fused_computation.12 | convolution fusion | flops 32440320 | bytes 5243648 | tf_op jit(solution)/shard_map/ia,fabce->fibce/dot_general | solution.py:101
  253.6 25.3 %all-to-all-done.1 = f32[128,16,320]{2,1,0:T(8,128)} async-done(((f32[128,16,320]{2,1,0:T(8,128)}), f32[128,16,320]{2,1,0:T(8,128)}, u32[]{:S(2)}, u32[]{:S(2)}) %all-to-all-start.1) | async-done | bytes 2621472 | tf_op jit(solution)/shard_map/all_to_all | solution.py:181
  278.9 13.8 %scatter_fusion.1 = f32[768,320]{1,0:T(8,128)S(1)} fusion(f32[768,320]{1,0:T(8,128)S(1)} %slice.575, s32[2048]{0:T(1024)S(1)} %bitcast.426, f32[2048,320]{1,0:T(8,128)} %bitcast.77), kind=kCustom, calls=%fused_computation.5 | custom fusion | flops 655360 | bytes 7872512 | tf_op jit(solution)/shard_map/scatter-add | solution.py:182
  293.5 1.8 copy.178
  295.3 1.7 copy.179
  299.3 3.2 %scatter-add.54 = f32[5,8,8,8,128]{4,1,3,2,0:T(8,128)S(1)} dynamic-update-slice(f32[5,8,8,8,128]{4,1,3,2,0:T(8,128)S(1)} %copy-done.1, f32[5,1,8,8,128]{4,1,3,2,0:T(1,128)S(1)} %slice_add_fusion.5, s32[]{:T(128)} %constant.223.clone.1, s32[]{:T(128)} %constant.223.clone.1, s32[]{:T(128)} %constant.223.clone.1, s32[]{:T(128)} %constant.223.clone.1, s32[]{:T(128)} %constant.223.clone.1) | dynamic-update-slice | bytes 327684 | tf_op jit(solution)/shard_map/scatter-add | solution.py:129
  303.6 3.2 %scatter-add.55 = f32[5,8,8,8,128]{4,1,3,2,0:T(8,128)S(1)} dynamic-update-slice(f32[5,8,8,8,128]{4,1,3,2,0:T(8,128)S(1)} %scatter-add.54, f32[5,1,8,8,128]{4,1,3,2,0:T(1,128)S(1)} %slice_add_fusion.4, s32[]{:T(128)} %constant.223.clone.1, s32[]{:T(128)} %constant.229.clone.1, s32[]{:T(128)} %constant.223.clone.1, s32[]{:T(128)} %constant.223.clone.1, s32[]{:T(128)} %constant.223.clone.1) | dynamic-update-slice | bytes 327684 | tf_op jit(solution)/shard_map/scatter-add | solution.py:129
  308.4 1.8 multiply_add_fusion
  (144 shorter events, 53.4 us)
Async XLA Ops:
  0.6 2.0 copy-start
  0.6 3.7 %copy-start.16 = (s32[128,16]{0,1:T(8,128)S(1)}, s32[128,16]{0,1:T(8,128)}, u32[]{:S(2)}) copy-start(s32[128,16]{0,1:T(8,128)} %param.26) | copy-start | bytes 24580
  6.3 2.0 copy-start.14
  23.3 10.0 %copy-start.20 = (pred[128,16]{0,1:T(8,128)(4,1)S(1)}, pred[128,16]{0,1:T(8,128)(4,1)}, u32[]{:S(2)}) copy-start(pred[128,16]{0,1:T(8,128)(4,1)} %compare_and_fusion) | copy-start | bytes 6148
  33.5 3.6 %copy-start.10 = (f32[640,128]{0,1:T(8,128)S(1)}, f32[640,128]{0,1:T(8,128)}, u32[]{:S(2)}) copy-start(f32[640,128]{0,1:T(8,128)} %copy.159) | copy-start | bytes 983044
  33.5 4.4 %copy-start.11 = (f32[640,128]{0,1:T(8,128)S(1)}, f32[640,128]{0,1:T(8,128)}, u32[]{:S(2)}) copy-start(f32[640,128]{0,1:T(8,128)} %copy.160) | copy-start | bytes 983044
  35.3 3.4 %copy-start.12 = (f32[640,128]{0,1:T(8,128)S(1)}, f32[640,128]{0,1:T(8,128)}, u32[]{:S(2)}) copy-start(f32[640,128]{0,1:T(8,128)} %copy.161) | copy-start | bytes 983044
  53.1 132.8 %all-to-all-start = ((f32[128,16,640]{2,1,0:T(8,128)}), f32[128,16,640]{2,1,0:T(8,128)}, u32[]{:S(2)}, u32[]{:S(2)}) async-start(f32[128,16,640]{2,1,0:T(8,128)} %broadcast_select_fusion), calls=%async_computation | async-start | bytes 10485760 | tf_op jit(solution)/shard_map/all_to_all | solution.py:169
  65.4 114.0 %copy-start.21 = (s32[128,2]{0,1:T(2,128)S(1)}, s32[128,2]{0,1:T(2,128)}, u32[]{:S(2)}) copy-start(s32[128,2]{0,1:T(2,128)} %param.28) | copy-start | bytes 3076
  65.4 114.4 %copy-start.19 = (s32[32,5]{0,1:T(8,128)S(1)}, s32[32,5]{0,1:T(8,128)}, u32[]{:S(2)}) copy-start(s32[32,5]{0,1:T(8,128)} %param.27) | copy-start | bytes 1924
  65.4 116.4 %copy-start.23 = (f32[128]{0:T(128)S(1)}, f32[128]{0:T(128)}, u32[]{:S(2)}) copy-start(f32[128]{0:T(128)} %param.24) | copy-start | bytes 1540
  66.3 119.6 %copy-start.3 = (f32[1,512,128]{2,1,0:T(8,128)}, f32[1,512,128]{2,1,0:T(8,128)S(1)}, u32[]{:S(2)}) copy-start(f32[1,512,128]{2,1,0:T(8,128)S(1)} %get-tuple-element.106) | copy-start | bytes 786436
  66.3 119.6 %copy-start.5 = (f32[1,512,128]{2,1,0:T(8,128)}, f32[1,512,128]{2,1,0:T(8,128)S(1)}, u32[]{:S(2)}) copy-start(f32[1,512,128]{2,1,0:T(8,128)S(1)} %get-tuple-element.107) | copy-start | bytes 786436
  212.1 1.7 copy-start.7
  213.8 2.0 copy-start.17
  216.6 3.9 %copy-start.9 = (f32[256,320]{1,0:T(8,128)S(1)}, f32[256,320]{1,0:T(8,128)}, u32[]{:S(2)}) copy-start(f32[256,320]{1,0:T(8,128)} %reshape.2714) | copy-start | bytes 983044
  230.6 7.0 %copy-start.2 = (f32[1,8,8,8,128]{4,1,3,2,0:T(8,128)S(1)}, f32[1,8,8,8,128]{4,1,3,2,0:T(8,128)}, u32[]{:S(2)}) copy-start(f32[1,8,8,8,128]{4,1,3,2,0:T(8,128)} %get-tuple-element.99) | copy-start | bytes 786436
  230.6 7.0 %copy-start.6 = (f32[1,512,128]{2,1,0:T(8,128)S(1)}, f32[1,512,128]{2,1,0:T(8,128)}, u32[]{:S(2)}) copy-start(f32[1,512,128]{2,1,0:T(8,128)} %copy-done.5) | copy-start | bytes 786436
  230.6 48.2 %all-to-all-start.1 = ((f32[128,16,320]{2,1,0:T(8,128)}), f32[128,16,320]{2,1,0:T(8,128)}, u32[]{:S(2)}, u32[]{:S(2)}) async-start(f32[128,16,320]{2,1,0:T(8,128)} %bitcast.372), calls=%async_computation.1 | async-start | bytes 6291456 | tf_op jit(solution)/shard_map/all_to_all | solution.py:181
  240.3 1.1 copy-start.4
  241.4 1.1 copy-start.18
  245.1 3.4 %copy-start.8 = (f32[5,8,8,8,128]{4,1,3,2,0:T(8,128)S(1)}, f32[5,8,8,8,128]{4,1,3,2,0:T(8,128)}, u32[]{:S(2)}) copy-start(f32[5,8,8,8,128]{4,1,3,2,0:T(8,128)} %get-tuple-element.158) | copy-start | bytes 3932164
  245.2 3.4 %copy-start.22 = (f32[128]{0:T(128)S(1)}, f32[128]{0:T(128)}, u32[]{:S(2)}) copy-start(f32[128]{0:T(128)} %get-tuple-element.178) | copy-start | bytes 1540
  293.5 4.6 %copy-start.1 = (f32[5,8,8,8,128]{4,1,3,2,0:T(8,128)S(1)}, f32[5,8,8,8,128]{4,1,3,2,0:T(8,128)}, u32[]{:S(2)}) copy-start(f32[5,8,8,8,128]{4,1,3,2,0:T(8,128)} %fusion.4) | copy-start | bytes 3932164
  297.8 9.0 %copy-start.15 = (f32[320,128]{1,0:T(8,128)S(1)}, f32[320,128]{1,0:T(8,128)}, u32[]{:S(2)}) copy-start(f32[320,128]{1,0:T(8,128)} %copy.180) | copy-start | bytes 491524
  307.1 1.3 copy-start.13
where the time goes:
time: 312 us; the launch traced here: 310 us
  blocking collectives  113 us (36%)
  local copies, waits for them, and re-layouts  78.2 us (25%)
  other arithmetic  60.2 us (19%)
  waiting for transfers between devices  25.3 us (8%)
  starting transfers between devices  18.6 us (6%)
  matrix products  11.6 us (4%)
  between operations  3.16 us (1%)
    pmax x1, blocking collectives, per_device(): lam = lax.pmax(fastest, 'sfc')  113 us
    all_to_all x1, waiting for transfers between devices, per_device(): lax.all_to_all(remote_corr, 'sfc', split_axis=0, concat_axis=0, tiled=True)  25.3 us
    unnamed x20, other arithmetic  18.2 us
    scatter-add x1, other arithmetic, per_device(): local_corr.at[send_slots.reshape(-1)]  13.8 us
    unnamed x61, local copies, waits for them, and re-layouts  13 us
    all_to_all x1, starting transfers between devices, per_device(): lax.all_to_all(outgoing, 'sfc', split_axis=0, concat_axis=0, tiled=True)  11.6 us
    dot_general x3, matrix products, volume_terms(): total = total + jnp.einsum(forms[axis], deriv, flux, precision=HIGHEST)  9.68 us
    gather x1, local copies, waits for them, and re-layouts, per_device(): outgoing = jnp.take(table, send_slots, axis=0, mode='fill', fill_value=0.0)  9.36 us
  transfers between devices with their start and end apart: 2, of which 1 were waited for; matrix products, arithmetic and copies ran while one was open for 7% of the time, Pallas kernels for 0%

commit v1 on v0

v1 whole, which is shorter than its diff:
```python
import functools
import jax
import jax.numpy as jnp
import numpy as np
from jax import lax
from jax.experimental import pallas as pl
from jax.experimental.pallas import tpu as pltpu
from jax.sharding import PartitionSpec as P

GAMMA = 1.4
LIFT = 28.0
COURANT = 0.02
SECTION_A = -0.4178904745
SECTION_B = 0.3792103129999
HIGHEST = lax.Precision.HIGHEST
F32 = jnp.float32
BF16 = jnp.bfloat16
ELEMS = 128
SLOTS = 6 * ELEMS
WIDTH = 16
PEERS = 5
MORTARS = 32
FACES = 128
ROWS = 320
GLL_NODES = (
    -1.0,
    -0.8717401485096066,
    -0.5917001814331423,
    -0.2092992179024789,
    0.2092992179024789,
    0.5917001814331423,
    0.8717401485096066,
    1.0,
)
GLL_WEIGHTS = (
    0.03571428571428571,
    0.2107042271435061,
    0.3411226924835044,
    0.4124587946587038,
    0.4124587946587038,
    0.3411226924835044,
    0.2107042271435061,
    0.03571428571428571,
)


def interp_matrix(nodes, points):
    matrix = np.ones((len(points), len(nodes)))
    for source in range(len(nodes)):
        for other in range(len(nodes)):
            if other != source:
                matrix[:, source] *= (points - nodes[other]) / (nodes[source] - nodes[other])
    return matrix


def node_tables():
    number = 8
    nodes = np.array(GLL_NODES)
    weights = np.array(GLL_WEIGHTS)
    differ = nodes[:, None] - nodes[None, :] + np.eye(number)
    barycentric = 1.0 / np.prod(differ, axis=1)
    deriv = barycentric[None, :] / barycentric[:, None] / differ
    deriv = deriv * (1.0 - np.eye(number))
    deriv = deriv - np.eye(number) * deriv.sum(axis=1)[:, None]
    halves = [interp_matrix(nodes, (nodes - 1.0) / 2.0), interp_matrix(nodes, (nodes + 1.0) / 2.0)]
    backs = [0.5 * (half.T * weights[None, :]) / weights[:, None] for half in halves]
    project = np.concatenate([np.kron(halves[c // 2], halves[c % 2]) for c in range(4)], axis=0)
    back = np.concatenate([np.kron(backs[c // 2], backs[c % 2]) for c in range(4)], axis=0)
    return (
        deriv.astype(np.float32),
        project.astype(np.float32),
        back.astype(np.float32),
        np.kron(np.eye(32), deriv).astype(np.float32),
    )


def pairings(devices):
    index = np.arange(devices)
    low = index % 4 < 2
    partners = [
        index ^ 1,
        np.where(index % 2 == 1, index + 1, index - 1) % devices,
        np.where(low, index + 2, index - 2) % devices,
        np.where(low, index - 2, index + 2) % devices,
        (index + devices // 2) % devices,
    ]
    return [[(int(d), int(p)) for d, p in enumerate(side)] for side in partners]


def partner_of(me, devices):
    odd = me % 2
    low = jnp.where(me % 4 < 2, 2, -2)
    steps = [1 - 2 * odd, 2 * odd - 1, low, -low, devices // 2]
    return [lax.rem(me + step + devices, devices) for step in steps]


def split3(value):
    high = value.astype(BF16)
    rest = value - high.astype(F32)
    mid = rest.astype(BF16)
    low = (rest - mid.astype(F32)).astype(BF16)
    return high, mid, low


def iota(shape, dim):
    return lax.broadcasted_iota(jnp.int32, shape, dim)


def dot_nt(left, right):
    return lax.dot_general(left, right, (((1,), (1,)), ((), ())), preferred_element_type=F32)


def one_hot(mask):
    return jnp.where(mask, F32(1.0), F32(0.0)).astype(BF16)


def thirds(value, size):
    return value[:size] + value[size : 2 * size] + value[2 * size : 3 * size]


def face_layer(ref, field, face):
    axis, side = face // 2, face % 2
    if axis == 0:
        return ref[field, 448 * side : 448 * side + 64, :]
    if axis == 1:
        return jnp.concatenate(
            [ref[field, a * 64 + 56 * side : a * 64 + 56 * side + 8, :] for a in range(8)], axis=0
        )
    return ref[field, pl.ds(7 * side, 64, stride=8), :]


def add_layer(ref, field, face, value):
    axis, side = face // 2, face % 2
    if axis == 0:
        ref[field, 448 * side : 448 * side + 64, :] += value
    elif axis == 1:
        for a in range(8):
            ref[field, a * 64 + 56 * side : a * 64 + 56 * side + 8, :] += value[8 * a : 8 * a + 8]
    else:
        place = pl.ds(7 * side, 64, stride=8)
        ref[field, place, :] = ref[field, place, :] + value


def out_columns(send_ref, partners):
    eye = iota((WIDTH, WIDTH), 0) == iota((WIDTH, WIDTH), 1)
    columns = []
    for peer in range(PEERS):
        row = send_ref[pl.ds(partners[peer], 1), :]
        columns.append(jnp.sum(jnp.where(eye, row, 0), axis=1, keepdims=True))
    columns.append(jnp.full((ELEMS - PEERS * WIDTH, 1), SLOTS, jnp.int32))
    return jnp.concatenate(columns, axis=0)


def ref_columns(mortar_ref, face_ref):
    large = mortar_ref[:, 0:1]
    return jnp.concatenate(
        [large] * 4 + [face_ref[:, 0:1]] + [mortar_ref[:, c : c + 1] for c in range(1, 5)] + [face_ref[:, 1:2]],
        axis=0,
    )


def remote_targets(partners):
    lane = iota((1, ELEMS), 1)
    target = jnp.full((1, ELEMS), -1, jnp.int32)
    for peer in range(PEERS):
        inside = (lane >= peer * WIDTH) & (lane < (peer + 1) * WIDTH)
        target = jnp.where(inside, SLOTS + partners[peer] * WIDTH + lane - peer * WIDTH, target)
    return target


def send_kernel(devices, state_ref, count_ref, send_ref, m0, m1, m2, m3, m4, split_ref, fast_ref):
    partners = partner_of(lax.axis_index("sfc"), devices)
    fastest = jnp.zeros((8, ELEMS), F32)
    for a in range(8):
        part = slice(64 * a, 64 * a + 64)
        density, one, two, three, energy = [state_ref[field, part, :] for field in range(5)]
        inverse = 1.0 / density
        square = one * one + two * two + three * three
        press = (GAMMA - 1.0) * (energy - 0.5 * square * inverse)
        speed = jnp.sqrt(square) * inverse + jnp.sqrt(GAMMA * press * inverse)
        fastest = jnp.maximum(fastest, jnp.max(speed.reshape(8, 8, ELEMS), axis=0))
    fastest = jnp.where(iota((8, ELEMS), 1) < count_ref[0], fastest, 0.0)
    fast_ref[...] = fastest
    for face in range(6):
        lanes = slice(face * ELEMS, (face + 1) * ELEMS)
        for field in range(5):
            parts = split3(face_layer(state_ref, field, face))
            for term in range(3):
                split_ref[term * ROWS + field * 64 : term * ROWS + field * 64 + 64, lanes] = parts[term]
    row = iota((16, SLOTS), 0)
    face = iota((16, SLOTS), 1) // ELEMS
    sign = jnp.where(face % 2 == 1, F32(1.0), F32(-1.0))
    split_ref[3 * ROWS : 3 * ROWS + 16, :] = jnp.where(row == face // 2, sign, 0.0).astype(BF16)
    chosen = one_hot(out_columns(send_ref, partners) == iota((ELEMS, SLOTS), 1))
    picked = dot_nt(split_ref[...], chosen)
    rows = jnp.concatenate(
        [thirds(picked, ROWS), picked[3 * ROWS : 3 * ROWS + 16], jnp.zeros((48, ELEMS), F32)], axis=0
    )
    message = rows.T
    for peer, ref in enumerate((m0, m1, m2, m3, m4)):
        ref[0:WIDTH, :] = message[peer * WIDTH : (peer + 1) * WIDTH]
        ref[WIDTH : WIDTH + 8, 0:ELEMS] = fastest
        ref[WIDTH : WIDTH + 8, ELEMS:] = jnp.zeros((8, 256), F32)


def local_kernel(deriv, state_ref, split_ref, mortar_ref, face_ref, mix_ref, gather_ref, volume_ref, fa, fb, fc):
    columns = ref_columns(mortar_ref, face_ref)
    chosen = one_hot(columns == iota((512, SLOTS), 1))
    picked = dot_nt(split_ref[...], chosen)
    gather_ref[0:ROWS, :] = thirds(picked, ROWS)
    gather_ref[ROWS : ROWS + 16, :] = picked[3 * ROWS : 3 * ROWS + 16]
    for a in range(8):
        part = slice(64 * a, 64 * a + 64)
        density, one, two, three, energy = [state_ref[field, part, :] for field in range(5)]
        inverse = 1.0 / density
        press = (GAMMA - 1.0) * (energy - 0.5 * (one * one + two * two + three * three) * inverse)
        total = energy + press
        for axis, ref in enumerate((fa, fb, fc)):
            flow = (one, two, three)[axis]
            speed = flow * inverse
            terms = [one * speed, two * speed, three * speed]
            terms[axis] = terms[axis] + press
            for field, value in enumerate([flow] + terms + [total * speed]):
                ref[field, part, :] = value

    def body(field, carry):
        for half in range(2):
            part = slice(256 * half, 256 * half + 256)
            volume_ref[field, part, :] = jnp.dot(
                mix_ref[...], fc[field, part, :], precision=HIGHEST, preferred_element_type=F32
            )
        for b in range(8):
            values = [fa[field, a * 64 + 8 * b : a * 64 + 8 * b + 8, :] for a in range(8)]
            for i in range(8):
                place = slice(i * 64 + 8 * b, i * 64 + 8 * b + 8)
                total = volume_ref[field, place, :]
                for j in range(8):
                    total = total + float(deriv[i, j]) * values[j]
                volume_ref[field, place, :] = total
        for a in range(8):
            values = [fb[field, a * 64 + 8 * b : a * 64 + 8 * b + 8, :] for b in range(8)]
            for i in range(8):
                place = slice(a * 64 + 8 * i, a * 64 + 8 * i + 8)
                total = volume_ref[field, place, :]
                for j in range(8):
                    total = total + float(deriv[i, j]) * values[j]
                volume_ref[field, place, :] = total
        return carry

    lax.fori_loop(0, 5, body, 0)


def trace_flux(fields, normal):
    density, one, two, three, energy = fields
    inverse = 1.0 / density
    press = (GAMMA - 1.0) * (energy - 0.5 * (one * one + two * two + three * three) * inverse)
    flow = one * normal[0] + two * normal[1] + three * normal[2]
    speed = flow * inverse
    return [
        flow,
        one * speed + press * normal[0],
        two * speed + press * normal[1],
        three * speed + press * normal[2],
        (energy + press) * speed,
    ]


def child_select(stack, index):
    lanes = slice(index * ELEMS, (index + 1) * ELEMS)
    lane = iota((64, ELEMS), 1)
    value = stack[192:256, lanes]
    for child in (2, 1, 0):
        value = jnp.where(lane < 32 * (child + 1), stack[64 * child : 64 * child + 64, lanes], value)
    return value


def by_child(matrix_ref, values):
    stack = jnp.dot(
        matrix_ref[...], jnp.concatenate(values, axis=1), precision=HIGHEST, preferred_element_type=F32
    )
    return [child_select(stack, index) for index in range(len(values))]


def face_kernel(
    devices, own_ref, gather_ref, i0, i1, i2, i3, i4, mortar_ref, face_ref, project_ref, back_ref,
    corr_ref, m0, m1, m2, m3, m4, fast_ref, pool_ref
):
    partners = partner_of(lax.axis_index("sfc"), devices)
    incoming = (i0, i1, i2, i3, i4)
    fast = own_ref[...]
    for ref in incoming[0:4]:
        fast = jnp.maximum(fast, ref[WIDTH : WIDTH + 8, 0:ELEMS])
    fast_ref[...] = fast
    columns = ref_columns(mortar_ref, face_ref)
    remote = one_hot(columns == remote_targets(partners))
    arrived = jnp.concatenate(
        [ref[0:WIDTH, :] for ref in incoming] + [jnp.zeros((ELEMS - PEERS * WIDTH, 384), F32)], axis=0
    ).T
    high, mid, low = split3(arrived[:ROWS])
    picked = dot_nt(jnp.concatenate([high, mid, low, arrived[ROWS : ROWS + 16].astype(BF16)], axis=0), remote)
    pool_ref[0:ROWS, :] = gather_ref[0:ROWS, :] + thirds(picked, ROWS)
    normals = gather_ref[ROWS : ROWS + 8, :] + picked[3 * ROWS : 3 * ROWS + 8]
    sides = []
    for side in range(4):
        lanes = slice(side * ELEMS, (side + 1) * ELEMS)
        fields = [pool_ref[64 * field : 64 * field + 64, lanes] for field in range(5)]
        normal = [normals[axis : axis + 1, lanes] for axis in range(3)]
        sides.append((fields, trace_flux(fields, normal)))
    (large_u, large_f), (left_u, left_f), (child_u, child_f), (right_u, right_f) = sides
    spread = by_child(project_ref, large_u + large_f)
    steady = [0.5 * (spread[5 + k] - child_f[k]) for k in range(5)]
    moving = [0.5 * (spread[k] - child_u[k]) for k in range(5)]
    folded = by_child(back_ref, steady + moving)
    for k in range(5):
        rows = slice(64 * k, 64 * k + 64)
        more = slice(ROWS + 64 * k, ROWS + 64 * k + 64)
        corr_ref[rows, 0:128] = folded[k] - 0.25 * large_f[k]
        corr_ref[more, 0:128] = folded[5 + k]
        corr_ref[rows, 256:384] = -steady[k] - child_f[k]
        corr_ref[more, 256:384] = -moving[k]
        even = 0.5 * (left_f[k] - right_f[k])
        jump = 0.5 * (left_u[k] - right_u[k])
        corr_ref[rows, 128:256] = even - left_f[k]
        corr_ref[more, 128:256] = jump
        corr_ref[rows, 384:512] = -even - right_f[k]
        corr_ref[more, 384:512] = -jump
    parts = split3(corr_ref[...])
    back = sum(jnp.dot(part, remote, preferred_element_type=F32) for part in parts).T
    for peer, ref in enumerate((m0, m1, m2, m3, m4)):
        ref[...] = back[peer * WIDTH : (peer + 1) * WIDTH]


def lift_kernel(
    corr_ref, mortar_ref, face_ref, volume_ref, register_ref, metric_ref, count_ref, steady_ref, rate_ref
):
    columns = ref_columns(mortar_ref, face_ref)
    chosen = one_hot(columns == iota((512, SLOTS), 1))
    live = iota((1, ELEMS), 1) < count_ref[0]
    scale = jnp.where(live, COURANT * metric_ref[...], 0.0)
    for field in range(5):
        steady_ref[field] = SECTION_A * register_ref[field]
        rate_ref[field] = -scale * volume_ref[field]
    parts = split3(corr_ref[...])
    layers = sum(jnp.dot(part, chosen, preferred_element_type=F32) for part in parts)
    lift = -LIFT * scale
    for face in range(6):
        lanes = slice(face * ELEMS, (face + 1) * ELEMS)
        for field in range(5):
            add_layer(rate_ref, field, face, lift * layers[64 * field : 64 * field + 64, lanes])
            add_layer(
                steady_ref, field, face, lift * layers[ROWS + 64 * field : ROWS + 64 * field + 64, lanes]
            )


def finish_kernel(
    devices, steady_ref, rate_ref, state_ref, i0, i1, i2, i3, i4, fast_ref, send_ref, metric_ref, count_ref,
    state_out, register_out
):
    partners = partner_of(lax.axis_index("sfc"), devices)
    lam = jnp.max(jnp.max(fast_ref[...], axis=0, keepdims=True), axis=1, keepdims=True)
    inverse = 1.0 / lam
    live = iota((1, ELEMS), 1) < count_ref[0]
    lift = jnp.where(live, -LIFT * COURANT * metric_ref[...], 0.0) * inverse
    chosen = one_hot(out_columns(send_ref, partners) == iota((ELEMS, SLOTS), 1))
    arrived = jnp.concatenate(
        [ref[:, 0:ROWS] + lam * ref[:, ROWS : 2 * ROWS] for ref in (i0, i1, i2, i3, i4)]
        + [jnp.zeros((ELEMS - PEERS * WIDTH, ROWS), F32)],
        axis=0,
    ).T
    layers = sum(jnp.dot(part, chosen, preferred_element_type=F32) for part in split3(arrived))
    for field in range(5):
        register_out[field] = steady_ref[field] + inverse * rate_ref[field]
    for face in range(6):
        lanes = slice(face * ELEMS, (face + 1) * ELEMS)
        for field in range(5):
            add_layer(register_out, field, face, lift * layers[64 * field : 64 * field + 64, lanes])
    for field in range(5):
        state_out[field] = state_ref[field] + SECTION_B * register_out[field]


VMEM = pl.BlockSpec(memory_space=pltpu.VMEM)
SMEM = pl.BlockSpec(memory_space=pltpu.SMEM)


def call(kernel, name, outs, specs, cost, scratch=()):
    return pl.pallas_call(
        kernel,
        name=name,
        out_shape=[jax.ShapeDtypeStruct(shape, dtype) for shape, dtype in outs],
        in_specs=specs,
        out_specs=[VMEM] * len(outs),
        scratch_shapes=list(scratch),
        compiler_params=pltpu.CompilerParams(vmem_limit_bytes=40 * 1024 * 1024),
        cost_estimate=pl.CostEstimate(flops=cost[0], bytes_accessed=cost[1], transcendentals=0),
    )


def per_device(state, register, metric, counts, send_slots, mortar_refs, face_refs):
    devices = lax.axis_size("sfc")
    deriv, project, back, mix = node_tables()
    metric = metric.reshape(1, ELEMS)
    pairs = pairings(devices)
    cube = (5, 512, ELEMS)
    first = call(
        functools.partial(send_kernel, devices), "send",
        [((WIDTH + 8, 384), F32)] * 5 + [((3 * ROWS + 16, SLOTS), BF16), ((8, ELEMS), F32)],
        [VMEM, SMEM, VMEM], (200_000_000, 3_000_000),
    )(state, counts, send_slots)
    messages, split, own = first[:5], first[5], first[6]
    incoming = [lax.ppermute(message, "sfc", pair) for message, pair in zip(messages, pairs)]
    gathered, volume = call(
        functools.partial(local_kernel, deriv), "local",
        [((ROWS + 16, 512), F32), (cube, F32)],
        [VMEM] * 5, (2_000_000_000, 5_000_000),
        [pltpu.VMEM(cube, F32)] * 3,
    )(state, split, mortar_refs, face_refs, jnp.asarray(mix))
    second = call(
        functools.partial(face_kernel, devices), "faces",
        [((2 * ROWS, 512), F32)] + [((WIDTH, 2 * ROWS), F32)] * 5 + [((8, ELEMS), F32)],
        [VMEM] * 11, (1_000_000_000, 3_000_000),
        [pltpu.VMEM((ROWS, 512), F32)],
    )(own, gathered, *incoming, mortar_refs, face_refs, jnp.asarray(project), jnp.asarray(back))
    corrections, replies, fast = second[0], second[1:6], second[6]
    returned = [lax.ppermute(reply, "sfc", pair) for reply, pair in zip(replies, pairs)]
    shift = 4
    while shift < devices:
        pair = [(d, d ^ shift) for d in range(devices)]
        fast = jnp.maximum(fast, lax.ppermute(fast, "sfc", pair))
        shift *= 2
    steady, rate = call(
        lift_kernel, "lift", [(cube, F32)] * 2, [VMEM] * 6 + [SMEM], (1_500_000_000, 6_000_000)
    )(corrections, mortar_refs, face_refs, volume, register, metric, counts)
    return tuple(
        call(
            functools.partial(finish_kernel, devices), "finish", [(cube, F32)] * 2,
            [VMEM] * 11 + [SMEM], (200_000_000, 6_000_000),
        )(steady, rate, state, *returned, fast, send_slots, metric, counts)
    )


def solution(mesh):
    return jax.shard_map(
        per_device,
        mesh=mesh,
        in_specs=(
            P(None, None, "sfc"),
            P(None, None, "sfc"),
            P("sfc"),
            P("sfc"),
            P("sfc", None),
            P("sfc", None),
            P("sfc", None),
        ),
        out_specs=(P(None, None, "sfc"), P(None, None, "sfc")),
        check_vma=False,
    )
```

time: 312 us -> 64.5 us (0.21)
  blocking collectives: 113 us -> 0 us
  local copies, waits for them, and re-layouts: 78.2 us -> 3.28 us
  other arithmetic: 60.2 us -> 0.02 us
  Pallas kernels: 0 us -> 14.6 us
  matrix products: 11.6 us -> 0 us
    pmax x1 -> x0, blocking collectives: 113 us -> none  [per_device(): lam = lax.pmax(fastest, 'sfc')]
    all_to_all x2 -> x0, waiting for transfers between devices: 25.3 us -> none  [the longest x1 25.3 us: per_device(): lax.all_to_all(remote_corr, 'sfc', split_axis=0, concat_axis=0, tiled=True)]
    ppermute x0 -> x15, waiting for transfers between devices: none -> 24.8 us  [the longest x5 16.2 us: per_device(): fast = jnp.maximum(fast, lax.ppermute(fast, 'sfc', pair))]
    scatter-add x7 -> x0, other arithmetic: 24.2 us -> none  [the longest x1 13.8 us: per_device(): local_corr.at[send_slots.reshape(-1)]]
    ppermute x0 -> x15, starting transfers between devices: none -> 20.2 us  [the longest x5 10.3 us: per_device(): lax.ppermute(message, 'sfc', pair)]
    gather x5 -> x0, local copies, waits for them, and re-layouts: 19.9 us -> none  [the longest x1 9.36 us: per_device(): outgoing = jnp.take(table, send_slots, axis=0, mode='fill', fill_value=0.0)]
    all_to_all x2 -> x0, starting transfers between devices: 18.6 us -> none  [the longest x1 11.6 us: per_device(): lax.all_to_all(outgoing, 'sfc', split_axis=0, concat_axis=0, tiled=True)]
    unnamed x20 -> x0, other arithmetic: 18.2 us -> none
  transfers between devices with their start and end apart: 2 -> 15, of which waited for: 1 -> 8; matrix products, arithmetic and copies ran while one was open for 7% -> 0% of each run, Pallas kernels for 0% -> 11%
where the time goes in v1:
time: 64.5 us; the launch traced here: 64.2 us
  waiting for transfers between devices  24.8 us (38%)
  starting transfers between devices  20.2 us (31%)
  Pallas kernels  14.6 us (23%)
  local copies, waits for them, and re-layouts  3.28 us (5%)
  between operations  1.47 us (2%)
    ppermute x5, waiting for transfers between devices, per_device(): fast = jnp.maximum(fast, lax.ppermute(fast, 'sfc', pair))  16.2 us
    ppermute x5, starting transfers between devices, per_device(): lax.ppermute(message, 'sfc', pair)  10.3 us
    ppermute x5, waiting for transfers between devices, per_device(): lax.ppermute(reply, 'sfc', pair)  7.02 us
    ppermute x5, starting transfers between devices, per_device(): lax.ppermute(reply, 'sfc', pair)  6.5 us
    pallas_call x1, Pallas kernels, per_device(): call(functools.partial(local_kernel, deriv), 'local', [((ROWS + 16, 512),...  5.28 us
    pallas_call x1, Pallas kernels, per_device(): call(functools.partial(face_kernel, devices), 'faces', [((2 * ROWS, 512),...  3.73 us
    ppermute x5, starting transfers between devices, per_device(): fast = jnp.maximum(fast, lax.ppermute(fast, 'sfc', pair))  3.34 us
    unnamed x21, local copies, waits for them, and re-layouts  3.28 us
  transfers between devices with their start and end apart: 15, of which 8 were waited for; matrix products, arithmetic and copies ran while one was open for 0% of the time, Pallas kernels for 11%

profile of v1, /device:TPU:0, one launch (start us, length us, event | category | flops | bytes accessed | tf_op | source)
XLA Modules:
  0.0 64.2 jit_solution(15443401954411807458)
XLA Ops:
  1.3 0.8 %copy.12.send_ref = s32[128,16]{1,0:T(8,128)S(1)} copy(s32[128,16]{0,1:T(8,128)} %param.14) | data formatting | bytes 16384 | tf_op args[4]
  2.1 1.3 %copy-done = f32[5,512,128]{2,1,0:T(8,128)S(1)} copy-done((f32[5,512,128]{2,1,0:T(8,128)S(1)}, f32[5,512,128]{2,1,0:T(8,128)}, u32[]{:S(2)}) %copy-start) | copy-done | bytes 1310744
  3.4 1.0 %send.1 = (f32[24,384]{1,0:T(8,128)S(1)}, f32[24,384]{1,0:T(8,128)S(1)}, f32[24,384]{1,0:T(8,128)S(1)}, f32[24,384]{1,0:T(8,128)S(1)}, f32[24,384]{1,0:T(8,128)S...) custom-call(f32[5,512,128]{2,1,0:T(8,128)S(1)} %copy-done, s32[1]{0:T(128)S(6)} %copy.20.count_ref, ...), custom_call_target="tpu_custom_call" | custom-call | flops 200000000 | bytes 3000000 | tf_op jit(solution)/shard_map/send/pallas_call | solution.py:404
  4.4 0.1 collective-permute-start
  4.5 8.9 %collective-permute-start.1 = (f32[24,384]{1,0:T(8,128)S(1)}, f32[24,384]{1,0:T(8,128)S(1)}, u32[]{:S(2)}, u32[]{:S(2)}) collective-permute-start(f32[24,384]{1,0:T(8,128)S(1)} %get-tuple-element.24), channel_id=1, source_target_pairs={{0,127},{1,2},{2,1},{3,4},{4,3},{5,6},{6,5},{7,8},{8,7},{9,10},{10... | collective-permute-start | bytes 110600 | tf_op jit(solution)/shard_map/ppermute | solution.py:410
  13.4 0.0 collective-permute-start.2
  13.4 1.4 %collective-permute-start.3 = (f32[24,384]{1,0:T(8,128)S(1)}, f32[24,384]{1,0:T(8,128)S(1)}, u32[]{:S(2)}, u32[]{:S(2)}) collective-permute-start(f32[24,384]{1,0:T(8,128)S(1)} %get-tuple-element.26), channel_id=1, source_target_pairs={{0,126},{1,127},{2,4},{3,5},{4,2},{5,3},{6,8},{7,9},{8,6},{9,7},{1... | collective-permute-start | bytes 110600 | tf_op jit(solution)/shard_map/ppermute | solution.py:410
  14.7 0.1 copy.13.mortar_ref
  14.8 0.1 copy.14.face_ref
  14.9 0.0 copy-start.4
  14.9 0.9 %copy-done.4 = f32[256,256]{1,0:T(8,128)S(1)} copy-done((f32[256,256]{1,0:T(8,128)S(1)}, f32[256,256]{1,0:T(8,128)}, u32[]{:S(2)}) %copy-start.4) | copy-done | bytes 262168
  15.9 5.3 %local.1 = (f32[336,512]{1,0:T(8,128)S(1)}, f32[5,512,128]{2,1,0:T(8,128)S(1)}) custom-call(f32[5,512,128]{2,1,0:T(8,128)S(1)} %copy-done.1, bf16[976,768]{1,0:T(8,128)(2,1)S(1)} %get-tuple-element.21.split_ref, s32[32,5]{1,0:T(8,128)S(1)} %copy.13.mortar_ref, s32[128,2]{1,0:T(8,128)S(1)} %copy.14.face_ref, f32[256,256]{1,0:T(8,128)S(1)} %copy-done.4), custom_call_target="tpu_custom_call" | custom-call | flops 2000000000 | bytes 5000000 | tf_op jit(solution)/shard_map/local/pallas_call | solution.py:411
  21.2 0.0 collective-permute-done.1.i1
  21.2 0.0 collective-permute-done.2.i2
  21.2 1.5 %collective-permute-done.3.i3 = f32[24,384]{1,0:T(8,128)S(1)} collective-permute-done((f32[24,384]{1,0:T(8,128)S(1)}, f32[24,384]{1,0:T(8,128)S(1)}, u32[]{:S(2)}, u32[]{:S(2)}) %collective-permute-start.3) | collective-permute-done | bytes 36896 | tf_op jit(solution)/shard_map/ppermute | solution.py:410
  22.7 0.0 collective-permute-done.4.i4
  22.8 0.0 copy-start.2
  22.8 0.0 copy-start.3
  22.8 3.7 %faces.1 = (f32[640,512]{1,0:T(8,128)S(1)}, f32[16,640]{1,0:T(8,128)S(1)}, f32[16,640]{1,0:T(8,128)S(1)}, f32[16,640]{1,0:T(8,128)S(1)}, f32[16,640]{1,0:T(8,128...) custom-call(f32[8,128]{1,0:T(8,128)S(1)} %get-tuple-element.20.own_ref, f32[336,512]{1,0:T(8,128)S(1)} %get-tuple-element.22.gather_ref, ...), custom_call_target="tpu_custom_call" | custom-call | flops 1000000000 | bytes 3000000 | tf_op jit(solution)/shard_map/faces/pallas_call | solution.py:417
  26.5 1.3 %collective-permute-start.10 = (f32[8,128]{1,0:T(8,128)S(1)}, f32[8,128]{1,0:T(8,128)S(1)}, u32[]{:S(2)}, u32[]{:S(2)}) collective-permute-start(f32[8,128]{1,0:T(8,128)S(1)} %get-tuple-element.37), channel_id=1, source_target_pairs={{0,4},{1,5},{2,6},{3,7},{4,0},{5,1},{6,2},{7,3},{8,12},{9,13},{10,... | collective-permute-start | bytes 12296 | tf_op jit(solution)/shard_map/ppermute | solution.py:428
  27.8 3.9 %collective-permute-done.10 = f32[8,128]{1,0:T(8,128)S(1)} collective-permute-done((f32[8,128]{1,0:T(8,128)S(1)}, f32[8,128]{1,0:T(8,128)S(1)}, u32[]{:S(2)}, u32[]{:S(2)}) %collective-permute-start.10) | collective-permute-done | bytes 4128 | tf_op jit(solution)/shard_map/ppermute | solution.py:428
  31.7 3.6 %collective-permute-done.11 = f32[8,128]{1,0:T(8,128)S(1)} collective-permute-done((f32[8,128]{1,0:T(8,128)S(1)}, f32[8,128]{1,0:T(8,128)S(1)}, u32[]{:S(2)}, u32[]{:S(2)}) %collective-permute-start.11) | collective-permute-done | bytes 4128 | tf_op jit(solution)/shard_map/ppermute | solution.py:428
  35.3 5.1 %collective-permute-done.12 = f32[8,128]{1,0:T(8,128)S(1)} collective-permute-done((f32[8,128]{1,0:T(8,128)S(1)}, f32[8,128]{1,0:T(8,128)S(1)}, u32[]{:S(2)}, u32[]{:S(2)}) %collective-permute-start.12) | collective-permute-done | bytes 4128 | tf_op jit(solution)/shard_map/ppermute | solution.py:428
  40.4 3.6 %collective-permute-done.13 = f32[8,128]{1,0:T(8,128)S(1)} collective-permute-done((f32[8,128]{1,0:T(8,128)S(1)}, f32[8,128]{1,0:T(8,128)S(1)}, u32[]{:S(2)}, u32[]{:S(2)}) %collective-permute-start.13) | collective-permute-done | bytes 4128 | tf_op jit(solution)/shard_map/ppermute | solution.py:428
  44.1 2.0 %collective-permute-start.14 = (f32[8,128]{1,0:T(8,128)S(1)}, f32[8,128]{1,0:T(8,128)S(1)}, u32[]{:S(2)}, u32[]{:S(2)}) collective-permute-start(f32[8,128]{1,0:T(8,128)S(1)} %max.18), channel_id=1, source_target_pairs={{0,64},{1,65},{2,66},{3,67},{4,68},{5,69},{6,70},{7,71},{8,72},{9,... | collective-permute-start | bytes 12296 | tf_op jit(solution)/shard_map/ppermute | solution.py:428
  46.1 6.2 %collective-permute-start.6 = (f32[16,640]{1,0:T(8,128)S(1)}, f32[16,640]{1,0:T(8,128)S(1)}, u32[]{:S(2)}, u32[]{:S(2)}) collective-permute-start(f32[16,640]{1,0:T(8,128)S(1)} %get-tuple-element.33), channel_id=1, source_target_pairs={{0,127},{1,2},{2,1},{3,4},{4,3},{5,6},{6,5},{7,8},{8,7},{9,10},{10... | collective-permute-start | bytes 122888 | tf_op jit(solution)/shard_map/ppermute | solution.py:424
  52.3 0.3 collective-permute-start.9
  52.6 2.1 %lift.1 = (f32[5,512,128]{2,1,0:T(8,128)S(1)}, f32[5,512,128]{2,1,0:T(8,128)S(1)}) custom-call(f32[640,512]{1,0:T(8,128)S(1)} %get-tuple-element.28.corr_ref, s32[32,5]{1,0:T(8,128)S(1)} %copy.13.mortar_ref, s32[128,2]{1,0:T(8,128)S(1)} %copy.14.face_ref, f32[5,512,128]{2,1,0:T(8,128)S(1)} %get-tuple-element.29.volume_ref, f32[5,512,128]{2,1,0:T(8,128)S(1)} %copy-done.3, ...), custom_call_target="tpu_custom_call" | custom-call | flops 1500000000 | bytes 6000000 | tf_op jit(solution)/shard_map/lift/pallas_call | solution.py:430
  54.7 0.2 collective-permute-done.6.i1
  54.9 1.4 %collective-permute-done.7.i2 = f32[16,640]{1,0:T(8,128)S(1)} collective-permute-done((f32[16,640]{1,0:T(8,128)S(1)}, f32[16,640]{1,0:T(8,128)S(1)}, u32[]{:S(2)}, u32[]{:S(2)}) %collective-permute-start.7) | collective-permute-done | bytes 40992 | tf_op jit(solution)/shard_map/ppermute | solution.py:424
  56.3 5.4 %collective-permute-done.8.i3 = f32[16,640]{1,0:T(8,128)S(1)} collective-permute-done((f32[16,640]{1,0:T(8,128)S(1)}, f32[16,640]{1,0:T(8,128)S(1)}, u32[]{:S(2)}, u32[]{:S(2)}) %collective-permute-start.8) | collective-permute-done | bytes 40992 | tf_op jit(solution)/shard_map/ppermute | solution.py:424
  61.7 2.5 %finish.1 = (f32[5,512,128]{2,1,0:T(8,128)}, f32[5,512,128]{2,1,0:T(8,128)}) custom-call(f32[5,512,128]{2,1,0:T(8,128)S(1)} %get-tuple-element.30.steady_ref, f32[5,512,128]{2,1,0:T(8,128)S(1)} %get-tuple-element.31.rate_ref, f32[5,512,128]{2,1,0:T(8,128)S(1)} %copy-done.1, f32[16,640]{1,0:T(8,128)S(1)} %collective-permute-done.5.i0, ...), custom_call_target="tpu_custom_call" | custom-call | flops 200000000 | bytes 6000000 | tf_op jit(solution)/shard_map/finish/pallas_call | solution.py:434
  (29 shorter events, 0.1 us)
Async XLA Ops:
  0.6 14.1 %copy-start.7 = (s32[32,5]{0,1:T(8,128)S(1)}, s32[32,5]{0,1:T(8,128)}, u32[]{:S(2)}) copy-start(s32[32,5]{0,1:T(8,128)} %param.15) | copy-start | bytes 1924
  0.6 14.2 %copy-start.8 = (s32[128,2]{0,1:T(2,128)S(1)}, s32[128,2]{0,1:T(2,128)}, u32[]{:S(2)}) copy-start(s32[128,2]{0,1:T(2,128)} %param.16) | copy-start | bytes 3076
  2.1 1.3 %copy-start = (f32[5,512,128]{2,1,0:T(8,128)S(1)}, f32[5,512,128]{2,1,0:T(8,128)}, u32[]{:S(2)}) copy-start(f32[5,512,128]{2,1,0:T(8,128)} %state_ref.5) | copy-start | bytes 3932164
  3.4 11.5 %copy-start.1 = (f32[5,512,128]{2,1,0:T(8,128)S(1)}, f32[5,512,128]{2,1,0:T(8,128)}, u32[]{:S(2)}) copy-start(f32[5,512,128]{2,1,0:T(8,128)} %state_ref.5) | copy-start | bytes 3932164
  4.4 16.8 %collective-permute-start = (f32[24,384]{1,0:T(8,128)S(1)}, f32[24,384]{1,0:T(8,128)S(1)}, u32[]{:S(2)}, u32[]{:S(2)}) collective-permute-start(f32[24,384]{1,0:T(8,128)S(1)} %get-tuple-element.23), channel_id=1, source_target_pairs={{0,1},{1,0},{2,3},{3,2},{4,5},{5,4},{6,7},{7,6},{8,9},{9,8},{10,11... | collective-permute-start | bytes 110600 | tf_op jit(solution)/shard_map/ppermute | solution.py:410
  4.5 16.7 %collective-permute-start.1 = (f32[24,384]{1,0:T(8,128)S(1)}, f32[24,384]{1,0:T(8,128)S(1)}, u32[]{:S(2)}, u32[]{:S(2)}) collective-permute-start(f32[24,384]{1,0:T(8,128)S(1)} %get-tuple-element.24), channel_id=1, source_target_pairs={{0,127},{1,2},{2,1},{3,4},{4,3},{5,6},{6,5},{7,8},{8,7},{9,10},{10... | collective-permute-start | bytes 110600 | tf_op jit(solution)/shard_map/ppermute | solution.py:410
  13.4 7.8 %collective-permute-start.2 = (f32[24,384]{1,0:T(8,128)S(1)}, f32[24,384]{1,0:T(8,128)S(1)}, u32[]{:S(2)}, u32[]{:S(2)}) collective-permute-start(f32[24,384]{1,0:T(8,128)S(1)} %get-tuple-element.25), channel_id=1, source_target_pairs={{0,2},{1,3},{2,0},{3,1},{4,6},{5,7},{6,4},{7,5},{8,10},{9,11},{10,... | collective-permute-start | bytes 110600 | tf_op jit(solution)/shard_map/ppermute | solution.py:410
  13.4 9.4 %collective-permute-start.3 = (f32[24,384]{1,0:T(8,128)S(1)}, f32[24,384]{1,0:T(8,128)S(1)}, u32[]{:S(2)}, u32[]{:S(2)}) collective-permute-start(f32[24,384]{1,0:T(8,128)S(1)} %get-tuple-element.26), channel_id=1, source_target_pairs={{0,126},{1,127},{2,4},{3,5},{4,2},{5,3},{6,8},{7,9},{8,6},{9,7},{1... | collective-permute-start | bytes 110600 | tf_op jit(solution)/shard_map/ppermute | solution.py:410
  14.7 8.0 %collective-permute-start.4 = (f32[24,384]{1,0:T(8,128)S(1)}, f32[24,384]{1,0:T(8,128)S(1)}, u32[]{:S(2)}, u32[]{:S(2)}) collective-permute-start(f32[24,384]{1,0:T(8,128)S(1)} %get-tuple-element.27), channel_id=1, source_target_pairs={{0,64},{1,65},{2,66},{3,67},{4,68},{5,69},{6,70},{7,71},{8,72},{9,... | collective-permute-start | bytes 110600 | tf_op jit(solution)/shard_map/ppermute | solution.py:410
  14.9 1.0 %copy-start.4 = (f32[256,256]{1,0:T(8,128)S(1)}, f32[256,256]{1,0:T(8,128)}, u32[]{:S(2)}) copy-start(f32[256,256]{1,0:T(8,128)} %constant.6.clone.mix_ref) | copy-start | bytes 786436
  15.9 6.9 %copy-start.5 = (f32[256,64]{1,0:T(8,128)S(1)}, f32[256,64]{1,0:T(8,128)}, u32[]{:S(2)}) copy-start(f32[256,64]{1,0:T(8,128)} %constant.8.clone.back_ref) | copy-start | bytes 196612
  15.9 6.9 %copy-start.6 = (f32[256,64]{1,0:T(8,128)S(1)}, f32[256,64]{1,0:T(8,128)}, u32[]{:S(2)}) copy-start(f32[256,64]{1,0:T(8,128)} %constant.7.clone.project_ref) | copy-start | bytes 196612
  22.8 29.8 %copy-start.2 = (f32[128]{0:T(128)S(1)}, f32[128]{0:T(128)}, u32[]{:S(2)}) copy-start(f32[128]{0:T(128)} %param.12) | copy-start | bytes 1540
  22.8 29.8 %copy-start.3 = (f32[5,512,128]{2,1,0:T(8,128)S(1)}, f32[5,512,128]{2,1,0:T(8,128)}, u32[]{:S(2)}) copy-start(f32[5,512,128]{2,1,0:T(8,128)} %register_ref.1) | copy-start | bytes 3932164
  26.5 5.2 %collective-permute-start.10 = (f32[8,128]{1,0:T(8,128)S(1)}, f32[8,128]{1,0:T(8,128)S(1)}, u32[]{:S(2)}, u32[]{:S(2)}) collective-permute-start(f32[8,128]{1,0:T(8,128)S(1)} %get-tuple-element.37), channel_id=1, source_target_pairs={{0,4},{1,5},{2,6},{3,7},{4,0},{5,1},{6,2},{7,3},{8,12},{9,13},{10,... | collective-permute-start | bytes 12296 | tf_op jit(solution)/shard_map/ppermute | solution.py:428
  31.7 3.6 %collective-permute-start.11 = (f32[8,128]{1,0:T(8,128)S(1)}, f32[8,128]{1,0:T(8,128)S(1)}, u32[]{:S(2)}, u32[]{:S(2)}) collective-permute-start(f32[8,128]{1,0:T(8,128)S(1)} %max.15), channel_id=1, source_target_pairs={{0,8},{1,9},{2,10},{3,11},{4,12},{5,13},{6,14},{7,15},{8,0},{9,1},... | collective-permute-start | bytes 12296 | tf_op jit(solution)/shard_map/ppermute | solution.py:428
  35.3 5.1 %collective-permute-start.12 = (f32[8,128]{1,0:T(8,128)S(1)}, f32[8,128]{1,0:T(8,128)S(1)}, u32[]{:S(2)}, u32[]{:S(2)}) collective-permute-start(f32[8,128]{1,0:T(8,128)S(1)} %max.16), channel_id=1, source_target_pairs={{0,16},{1,17},{2,18},{3,19},{4,20},{5,21},{6,22},{7,23},{8,24},{9,... | collective-permute-start | bytes 12296 | tf_op jit(solution)/shard_map/ppermute | solution.py:428
  40.4 3.6 %collective-permute-start.13 = (f32[8,128]{1,0:T(8,128)S(1)}, f32[8,128]{1,0:T(8,128)S(1)}, u32[]{:S(2)}, u32[]{:S(2)}) collective-permute-start(f32[8,128]{1,0:T(8,128)S(1)} %max.17), channel_id=1, source_target_pairs={{0,32},{1,33},{2,34},{3,35},{4,36},{5,37},{6,38},{7,39},{8,40},{9,... | collective-permute-start | bytes 12296 | tf_op jit(solution)/shard_map/ppermute | solution.py:428
  44.1 8.3 %collective-permute-start.14 = (f32[8,128]{1,0:T(8,128)S(1)}, f32[8,128]{1,0:T(8,128)S(1)}, u32[]{:S(2)}, u32[]{:S(2)}) collective-permute-start(f32[8,128]{1,0:T(8,128)S(1)} %max.18), channel_id=1, source_target_pairs={{0,64},{1,65},{2,66},{3,67},{4,68},{5,69},{6,70},{7,71},{8,72},{9,... | collective-permute-start | bytes 12296 | tf_op jit(solution)/shard_map/ppermute | solution.py:428
  46.1 8.6 %collective-permute-start.5 = (f32[16,640]{1,0:T(8,128)S(1)}, f32[16,640]{1,0:T(8,128)S(1)}, u32[]{:S(2)}, u32[]{:S(2)}) collective-permute-start(f32[16,640]{1,0:T(8,128)S(1)} %get-tuple-element.32), channel_id=1, source_target_pairs={{0,1},{1,0},{2,3},{3,2},{4,5},{5,4},{6,7},{7,6},{8,9},{9,8},{10,11... | collective-permute-start | bytes 122888 | tf_op jit(solution)/shard_map/ppermute | solution.py:424
  46.1 8.9 %collective-permute-start.6 = (f32[16,640]{1,0:T(8,128)S(1)}, f32[16,640]{1,0:T(8,128)S(1)}, u32[]{:S(2)}, u32[]{:S(2)}) collective-permute-start(f32[16,640]{1,0:T(8,128)S(1)} %get-tuple-element.33), channel_id=1, source_target_pairs={{0,127},{1,2},{2,1},{3,4},{4,3},{5,6},{6,5},{7,8},{8,7},{9,10},{10... | collective-permute-start | bytes 122888 | tf_op jit(solution)/shard_map/ppermute | solution.py:424
  52.3 4.0 %collective-permute-start.7 = (f32[16,640]{1,0:T(8,128)S(1)}, f32[16,640]{1,0:T(8,128)S(1)}, u32[]{:S(2)}, u32[]{:S(2)}) collective-permute-start(f32[16,640]{1,0:T(8,128)S(1)} %get-tuple-element.34), channel_id=1, source_target_pairs={{0,2},{1,3},{2,0},{3,1},{4,6},{5,7},{6,4},{7,5},{8,10},{9,11},{10,... | collective-permute-start | bytes 122888 | tf_op jit(solution)/shard_map/ppermute | solution.py:424
  52.3 9.4 %collective-permute-start.8 = (f32[16,640]{1,0:T(8,128)S(1)}, f32[16,640]{1,0:T(8,128)S(1)}, u32[]{:S(2)}, u32[]{:S(2)}) collective-permute-start(f32[16,640]{1,0:T(8,128)S(1)} %get-tuple-element.35), channel_id=1, source_target_pairs={{0,126},{1,127},{2,4},{3,5},{4,2},{5,3},{6,8},{7,9},{8,6},{9,7},{1... | collective-permute-start | bytes 122888 | tf_op jit(solution)/shard_map/ppermute | solution.py:424
  52.3 9.4 %collective-permute-start.9 = (f32[16,640]{1,0:T(8,128)S(1)}, f32[16,640]{1,0:T(8,128)S(1)}, u32[]{:S(2)}, u32[]{:S(2)}) collective-permute-start(f32[16,640]{1,0:T(8,128)S(1)} %get-tuple-element.36), channel_id=1, source_target_pairs={{0,64},{1,65},{2,66},{3,67},{4,68},{5,69},{6,70},{7,71},{8,72},{9,... | collective-permute-start | bytes 122888 | tf_op jit(solution)/shard_map/ppermute | solution.py:424

commit v2 on v1

--- a/solution.py
+++ b/solution.py
@@ -142,30 +142,34 @@
 
 
 def out_columns(send_ref, partners):
-    eye = iota((WIDTH, WIDTH), 0) == iota((WIDTH, WIDTH), 1)
-    columns = []
-    for peer in range(PEERS):
-        row = send_ref[pl.ds(partners[peer], 1), :]
-        columns.append(jnp.sum(jnp.where(eye, row, 0), axis=1, keepdims=True))
+    lane = iota((WIDTH, ELEMS), 1)
+    slots = send_ref[...]
+    columns = [
+        jnp.sum(jnp.where(lane == partners[peer], slots, 0), axis=1, keepdims=True) for peer in range(PEERS)
+    ]
     columns.append(jnp.full((ELEMS - PEERS * WIDTH, 1), SLOTS, jnp.int32))
     return jnp.concatenate(columns, axis=0)
 
 
-def ref_columns(mortar_ref, face_ref):
-    large = mortar_ref[:, 0:1]
+def ref_rows(mortar_ref, face_ref):
+    large = mortar_ref[0:1, :]
     return jnp.concatenate(
-        [large] * 4 + [face_ref[:, 0:1]] + [mortar_ref[:, c : c + 1] for c in range(1, 5)] + [face_ref[:, 1:2]],
-        axis=0,
-    )
-
-
-def remote_targets(partners):
-    lane = iota((1, ELEMS), 1)
-    target = jnp.full((1, ELEMS), -1, jnp.int32)
+        [large] * 4 + [face_ref[0:1, :]] + [mortar_ref[c : c + 1, :] for c in range(1, 5)] + [face_ref[1:2, :]],
+        axis=1,
+    )
+
+
+def own_choice(mortar_ref, face_ref):
+    return one_hot(ref_rows(mortar_ref, face_ref) == iota((SLOTS, 512), 0))
+
+
+def remote_choice(mortar_ref, face_ref, partners):
+    place = iota((ELEMS, 1), 0)
+    target = jnp.full((ELEMS, 1), -1, jnp.int32)
     for peer in range(PEERS):
-        inside = (lane >= peer * WIDTH) & (lane < (peer + 1) * WIDTH)
-        target = jnp.where(inside, SLOTS + partners[peer] * WIDTH + lane - peer * WIDTH, target)
-    return target
+        inside = (place >= peer * WIDTH) & (place < (peer + 1) * WIDTH)
+        target = jnp.where(inside, SLOTS + partners[peer] * WIDTH + place - peer * WIDTH, target)
+    return one_hot(ref_rows(mortar_ref, face_ref) == target)
 
 
 def send_kernel(devices, state_ref, count_ref, send_ref, m0, m1, m2, m3, m4, split_ref, fast_ref):
@@ -203,51 +207,68 @@
         ref[WIDTH : WIDTH + 8, ELEMS:] = jnp.zeros((8, 256), F32)
 
 
-def local_kernel(deriv, state_ref, split_ref, mortar_ref, face_ref, mix_ref, gather_ref, volume_ref, fa, fb, fc):
-    columns = ref_columns(mortar_ref, face_ref)
-    chosen = one_hot(columns == iota((512, SLOTS), 1))
-    picked = dot_nt(split_ref[...], chosen)
-    gather_ref[0:ROWS, :] = thirds(picked, ROWS)
-    gather_ref[ROWS : ROWS + 16, :] = picked[3 * ROWS : 3 * ROWS + 16]
+def axis_flux(state_ref, axis, ref):
     for a in range(8):
         part = slice(64 * a, 64 * a + 64)
         density, one, two, three, energy = [state_ref[field, part, :] for field in range(5)]
         inverse = 1.0 / density
         press = (GAMMA - 1.0) * (energy - 0.5 * (one * one + two * two + three * three) * inverse)
-        total = energy + press
-        for axis, ref in enumerate((fa, fb, fc)):
-            flow = (one, two, three)[axis]
-            speed = flow * inverse
-            terms = [one * speed, two * speed, three * speed]
-            terms[axis] = terms[axis] + press
-            for field, value in enumerate([flow] + terms + [total * speed]):
-                ref[field, part, :] = value
+        flow = (one, two, three)[axis]
+        speed = flow * inverse
+        terms = [one * speed, two * speed, three * speed]
+        terms[axis] = terms[axis] + press
+        for field, value in enumerate([flow] + terms + [(energy + press) * speed]):
+            ref[field, part, :] = value
+
+
+def first_kernel(deriv, turn_ref, state_ref, volume_ref, flux):
+    axis_flux(state_ref, 0, flux)
 
     def body(field, carry):
-        for half in range(2):
-            part = slice(256 * half, 256 * half + 256)
-            volume_ref[field, part, :] = jnp.dot(
-                mix_ref[...], fc[field, part, :], precision=HIGHEST, preferred_element_type=F32
-            )
         for b in range(8):
-            values = [fa[field, a * 64 + 8 * b : a * 64 + 8 * b + 8, :] for a in range(8)]
+            values = [flux[field, a * 64 + 8 * b : a * 64 + 8 * b + 8, :] for a in range(8)]
             for i in range(8):
-                place = slice(i * 64 + 8 * b, i * 64 + 8 * b + 8)
-                total = volume_ref[field, place, :]
-                for j in range(8):
+                total = float(deriv[i, 0]) * values[0]
+                for j in range(1, 8):
                     total = total + float(deriv[i, j]) * values[j]
-                volume_ref[field, place, :] = total
+                volume_ref[field, i * 64 + 8 * b : i * 64 + 8 * b + 8, :] = total
+        return carry
+
+    lax.fori_loop(0, 5, body, 0)
+
+
+def second_kernel(deriv, turn_ref, state_ref, before_ref, volume_ref, flux):
+    axis_flux(state_ref, 1, flux)
+
+    def body(field, carry):
         for a in range(8):
-            values = [fb[field, a * 64 + 8 * b : a * 64 + 8 * b + 8, :] for b in range(8)]
+            values = [flux[field, a * 64 + 8 * b : a * 64 + 8 * b + 8, :] for b in range(8)]
             for i in range(8):
                 place = slice(a * 64 + 8 * i, a * 64 + 8 * i + 8)
-                total = volume_ref[field, place, :]
+                total = before_ref[field, place, :]
                 for j in range(8):
                     total = total + float(deriv[i, j]) * values[j]
                 volume_ref[field, place, :] = total
         return carry
 
     lax.fori_loop(0, 5, body, 0)
+
+
+def third_kernel(turn_ref, state_ref, before_ref, split_ref, mortar_ref, face_ref, mix_ref, gather_ref, volume_ref, flux):
+    axis_flux(state_ref, 2, flux)
+    picked = jnp.dot(split_ref[...], own_choice(mortar_ref, face_ref), preferred_element_type=F32)
+    gather_ref[0:ROWS, :] = thirds(picked, ROWS)
+    gather_ref[ROWS : ROWS + 16, :] = picked[3 * ROWS : 3 * ROWS + 16]
+    for half in range(2):
+        part = slice(256 * half, 256 * half + 256)
+        mixed = jnp.dot(
+            mix_ref[...],
+            jnp.concatenate([flux[field, part, :] for field in range(5)], axis=1),
+            precision=HIGHEST,
+            preferred_element_type=F32,
+        )
+        for field in range(5):
+            volume_ref[field, part, :] = before_ref[field, part, :] + mixed[:, field * ELEMS : (field + 1) * ELEMS]
 
 
 def trace_flux(fields, normal):
@@ -282,22 +303,20 @@
 
 
 def face_kernel(
-    devices, own_ref, gather_ref, i0, i1, i2, i3, i4, mortar_ref, face_ref, project_ref, back_ref,
-    corr_ref, m0, m1, m2, m3, m4, fast_ref, pool_ref
+    devices, turn_ref, gather_ref, i0, i1, i2, i3, i4, mortar_ref, face_ref, project_ref, back_ref, corr_ref, pool_ref
 ):
     partners = partner_of(lax.axis_index("sfc"), devices)
     incoming = (i0, i1, i2, i3, i4)
-    fast = own_ref[...]
-    for ref in incoming[0:4]:
-        fast = jnp.maximum(fast, ref[WIDTH : WIDTH + 8, 0:ELEMS])
-    fast_ref[...] = fast
-    columns = ref_columns(mortar_ref, face_ref)
-    remote = one_hot(columns == remote_targets(partners))
+    remote = remote_choice(mortar_ref, face_ref, partners)
     arrived = jnp.concatenate(
         [ref[0:WIDTH, :] for ref in incoming] + [jnp.zeros((ELEMS - PEERS * WIDTH, 384), F32)], axis=0
     ).T
     high, mid, low = split3(arrived[:ROWS])
-    picked = dot_nt(jnp.concatenate([high, mid, low, arrived[ROWS : ROWS + 16].astype(BF16)], axis=0), remote)
+    picked = jnp.dot(
+        jnp.concatenate([high, mid, low, arrived[ROWS : ROWS + 16].astype(BF16)], axis=0),
+        remote,
+        preferred_element_type=F32,
+    )
     pool_ref[0:ROWS, :] = gather_ref[0:ROWS, :] + thirds(picked, ROWS)
     normals = gather_ref[ROWS : ROWS + 8, :] + picked[3 * ROWS : 3 * ROWS + 8]
     sides = []
@@ -324,24 +343,31 @@
         corr_ref[more, 128:256] = jump
         corr_ref[rows, 384:512] = -even - right_f[k]
         corr_ref[more, 384:512] = -jump
-    parts = split3(corr_ref[...])
-    back = sum(jnp.dot(part, remote, preferred_element_type=F32) for part in parts).T
+
+
+def reply_kernel(devices, corr_ref, mortar_ref, face_ref, turn_ref, last_ref, m0, m1, m2, m3, m4, fast_ref):
+    partners = partner_of(lax.axis_index("sfc"), devices)
+    remote = remote_choice(mortar_ref, face_ref, partners)
+    fast = jnp.maximum(turn_ref[...], last_ref[...])
+    fast_ref[...] = fast
+    back = sum(dot_nt(part, remote) for part in split3(corr_ref[...])).T
     for peer, ref in enumerate((m0, m1, m2, m3, m4)):
-        ref[...] = back[peer * WIDTH : (peer + 1) * WIDTH]
+        ref[0:WIDTH, :] = back[peer * WIDTH : (peer + 1) * WIDTH]
+        ref[WIDTH : WIDTH + 8, 0:ELEMS] = fast
+        ref[WIDTH : WIDTH + 8, ELEMS:] = jnp.zeros((8, 512), F32)
 
 
 def lift_kernel(
-    corr_ref, mortar_ref, face_ref, volume_ref, register_ref, metric_ref, count_ref, steady_ref, rate_ref
+    turn_ref, corr_ref, mortar_ref, face_ref, volume_ref, register_ref, metric_ref, count_ref, steady_ref, rate_ref
 ):
-    columns = ref_columns(mortar_ref, face_ref)
-    chosen = one_hot(columns == iota((512, SLOTS), 1))
+    chosen = own_choice(mortar_ref, face_ref)
     live = iota((1, ELEMS), 1) < count_ref[0]
     scale = jnp.where(live, COURANT * metric_ref[...], 0.0)
     for field in range(5):
         steady_ref[field] = SECTION_A * register_ref[field]
         rate_ref[field] = -scale * volume_ref[field]
     parts = split3(corr_ref[...])
-    layers = sum(jnp.dot(part, chosen, preferred_element_type=F32) for part in parts)
+    layers = sum(dot_nt(part, chosen) for part in parts)
     lift = -LIFT * scale
     for face in range(6):
         lanes = slice(face * ELEMS, (face + 1) * ELEMS)
@@ -357,13 +383,16 @@
     state_out, register_out
 ):
     partners = partner_of(lax.axis_index("sfc"), devices)
-    lam = jnp.max(jnp.max(fast_ref[...], axis=0, keepdims=True), axis=1, keepdims=True)
+    fast = fast_ref[...]
+    for ref in (i0, i1, i2, i3):
+        fast = jnp.maximum(fast, ref[WIDTH : WIDTH + 8, 0:ELEMS])
+    lam = jnp.max(jnp.max(fast, axis=0, keepdims=True), axis=1, keepdims=True)
     inverse = 1.0 / lam
     live = iota((1, ELEMS), 1) < count_ref[0]
     lift = jnp.where(live, -LIFT * COURANT * metric_ref[...], 0.0) * inverse
     chosen = one_hot(out_columns(send_ref, partners) == iota((ELEMS, SLOTS), 1))
     arrived = jnp.concatenate(
-        [ref[:, 0:ROWS] + lam * ref[:, ROWS : 2 * ROWS] for ref in (i0, i1, i2, i3, i4)]
+        [ref[0:WIDTH, 0:ROWS] + lam * ref[0:WIDTH, ROWS : 2 * ROWS] for ref in (i0, i1, i2, i3, i4)]
         + [jnp.zeros((ELEMS - PEERS * WIDTH, ROWS), F32)],
         axis=0,
     ).T
@@ -399,42 +428,61 @@
     devices = lax.axis_size("sfc")
     deriv, project, back, mix = node_tables()
     metric = metric.reshape(1, ELEMS)
+    sends, mortars, faces = send_slots.T, mortar_refs.T, face_refs.T
     pairs = pairings(devices)
     cube = (5, 512, ELEMS)
+    flux = [pltpu.VMEM(cube, F32)]
+
+    def exchange(value, shift):
+        return lax.ppermute(value, "sfc", [(d, d ^ shift) for d in range(devices)])
+
     first = call(
         functools.partial(send_kernel, devices), "send",
         [((WIDTH + 8, 384), F32)] * 5 + [((3 * ROWS + 16, SLOTS), BF16), ((8, ELEMS), F32)],
         [VMEM, SMEM, VMEM], (200_000_000, 3_000_000),
-    )(state, counts, send_slots)
-    messages, split, own = first[:5], first[5], first[6]
-    incoming = [lax.ppermute(message, "sfc", pair) for message, pair in zip(messages, pairs)]
+    )(state, counts, sends)
+    messages, split, fast = first[:5], first[5], first[6]
+    far = lax.ppermute(messages[4], "sfc", pairs[4])
+    near = [lax.ppermute(message, "sfc", pair) for message, pair in zip(messages[:4], pairs[:4])]
+    fast = jnp.maximum(fast, far[WIDTH : WIDTH + 8, 0:ELEMS])
+    came = exchange(fast, 32)
+    (volume,) = call(
+        functools.partial(first_kernel, deriv), "volume_first", [(cube, F32)], [VMEM] * 2,
+        (1_000_000_000, 2_600_000), flux,
+    )(fast, state)
+    fast = jnp.maximum(fast, came)
+    came = exchange(fast, 16)
+    (volume,) = call(
+        functools.partial(second_kernel, deriv), "volume_second", [(cube, F32)], [VMEM] * 3,
+        (1_000_000_000, 3_900_000), flux,
+    )(fast, state, volume)
+    fast = jnp.maximum(fast, came)
+    came = exchange(fast, 8)
     gathered, volume = call(
-        functools.partial(local_kernel, deriv), "local",
-        [((ROWS + 16, 512), F32), (cube, F32)],
-        [VMEM] * 5, (2_000_000_000, 5_000_000),
-        [pltpu.VMEM(cube, F32)] * 3,
-    )(state, split, mortar_refs, face_refs, jnp.asarray(mix))
+        third_kernel, "volume_third_gather", [((ROWS + 16, 512), F32), (cube, F32)], [VMEM] * 7,
+        (2_000_000_000, 6_000_000), flux,
+    )(fast, state, volume, split, mortars, faces, jnp.asarray(mix))
+    fast = jnp.maximum(fast, came)
+    came = exchange(fast, 4)
+    (corrections,) = call(
+        functools.partial(face_kernel, devices), "faces", [((2 * ROWS, 512), F32)], [VMEM] * 11,
+        (1_000_000_000, 3_000_000), [pltpu.VMEM((ROWS, 512), F32)],
+    )(fast, gathered, *near, far, mortars, faces, jnp.asarray(project), jnp.asarray(back))
     second = call(
-        functools.partial(face_kernel, devices), "faces",
-        [((2 * ROWS, 512), F32)] + [((WIDTH, 2 * ROWS), F32)] * 5 + [((8, ELEMS), F32)],
-        [VMEM] * 11, (1_000_000_000, 3_000_000),
-        [pltpu.VMEM((ROWS, 512), F32)],
-    )(own, gathered, *incoming, mortar_refs, face_refs, jnp.asarray(project), jnp.asarray(back))
-    corrections, replies, fast = second[0], second[1:6], second[6]
+        functools.partial(reply_kernel, devices), "reply",
+        [((WIDTH + 8, 2 * ROWS), F32)] * 5 + [((8, ELEMS), F32)],
+        [VMEM] * 5, (500_000_000, 2_000_000),
+    )(corrections, mortars, faces, fast, came)
+    replies, fast = second[:5], second[5]
     returned = [lax.ppermute(reply, "sfc", pair) for reply, pair in zip(replies, pairs)]
-    shift = 4
-    while shift < devices:
-        pair = [(d, d ^ shift) for d in range(devices)]
-        fast = jnp.maximum(fast, lax.ppermute(fast, "sfc", pair))
-        shift *= 2
     steady, rate = call(
-        lift_kernel, "lift", [(cube, F32)] * 2, [VMEM] * 6 + [SMEM], (1_500_000_000, 6_000_000)
-    )(corrections, mortar_refs, face_refs, volume, register, metric, counts)
+        lift_kernel, "lift", [(cube, F32)] * 2, [VMEM] * 7 + [SMEM], (1_500_000_000, 6_000_000)
+    )(fast, corrections, mortars, faces, volume, register, metric, counts)
     return tuple(
         call(
             functools.partial(finish_kernel, devices), "finish", [(cube, F32)] * 2,
             [VMEM] * 11 + [SMEM], (200_000_000, 6_000_000),
-        )(steady, rate, state, *returned, fast, send_slots, metric, counts)
+        )(steady, rate, state, *returned, fast, sends, metric, counts)
     )
 
 

time: 64.5 us -> 52.2 us (0.81)
  waiting for transfers between devices: 24.8 us -> 11.5 us
  starting transfers between devices: 20.2 us -> 23.7 us
  Pallas kernels: 14.6 us -> 13.2 us
  local copies, waits for them, and re-layouts: 3.28 us -> 2.05 us
    ppermute x5, waiting for transfers between devices: 16.2 us -> 6.34 us  [the longest x4 6.34 us: exchange(): return lax.ppermute(value, 'sfc', [(d, d ^ shift) for d in range(devices)])]
    ppermute x5, starting transfers between devices: 3.34 us -> 8.69 us  [the longest x4 4.65 us: exchange(): return lax.ppermute(value, 'sfc', [(d, d ^ shift) for d in range(devices)])]
    ppermute x5 -> x4, starting transfers between devices: 10.3 us -> 6.84 us  [per_device(): lax.ppermute(message, 'sfc', pair)]
    ppermute x5, waiting for transfers between devices: 7.02 us -> 5.13 us  [per_device(): lax.ppermute(reply, 'sfc', pair)]
    ppermute x5, starting transfers between devices: 6.5 us -> 8.2 us  [per_device(): lax.ppermute(reply, 'sfc', pair)]
    ppermute x5 -> x4, waiting for transfers between devices: 1.55 us -> 0.01 us  [per_device(): lax.ppermute(message, 'sfc', pair)]
    unnamed x21 -> x22, local copies, waits for them, and re-layouts: 3.28 us -> 2.05 us
    pallas_call x1, Pallas kernels: 3.73 us -> 2.78 us  [per_device(): call(functools.partial(face_kernel, devices), 'faces', [((2 * ROWS, 512),...]
  transfers between devices with their start and end apart: 15 -> 14, of which waited for: 8 -> 4; matrix products, arithmetic and copies ran while one was open for 0% -> 0% of each run, Pallas kernels for 11% -> 17%
where the time goes in v2:
time: 52.2 us; the launch traced here: 52 us
  starting transfers between devices  23.7 us (45%)
  Pallas kernels  13.2 us (25%)
  waiting for transfers between devices  11.5 us (22%)
  local copies, waits for them, and re-layouts  2.05 us (4%)
  between operations  1.47 us (3%)
    ppermute x5, starting transfers between devices, per_device(): lax.ppermute(reply, 'sfc', pair)  8.2 us
    ppermute x4, starting transfers between devices, per_device(): lax.ppermute(message, 'sfc', pair)  6.84 us
    ppermute x4, waiting for transfers between devices, exchange(): return lax.ppermute(value, 'sfc', [(d, d ^ shift) for d in range(devices)])  6.34 us
    ppermute x5, waiting for transfers between devices, per_device(): lax.ppermute(reply, 'sfc', pair)  5.13 us
    ppermute x4, starting transfers between devices, exchange(): return lax.ppermute(value, 'sfc', [(d, d ^ shift) for d in range(devices)])  4.65 us
    ppermute x1, starting transfers between devices, per_device(): far = lax.ppermute(messages[4], 'sfc', pairs[4])  4.04 us
    pallas_call x1, Pallas kernels, per_device(): call(functools.partial(face_kernel, devices), 'faces', [((2 * ROWS, 512),...  2.78 us
    pallas_call x1, Pallas kernels, per_device(): call(functools.partial(finish_kernel, devices), 'finish', [(cube, F32)] *...  2.5 us
  transfers between devices with their start and end apart: 14, of which 4 were waited for; matrix products, arithmetic and copies ran while one was open for 0% of the time, Pallas kernels for 17%

profile of v2, /device:TPU:0, one launch (start us, length us, event | category | flops | bytes accessed | tf_op | source)
XLA Modules:
  0.0 52.0 jit_solution(14374463639006860365)
XLA Ops:
  1.3 0.0 copy-start
  1.3 1.3 %copy-done = f32[5,512,128]{2,1,0:T(8,128)S(1)} copy-done((f32[5,512,128]{2,1,0:T(8,128)S(1)}, f32[5,512,128]{2,1,0:T(8,128)}, u32[]{:S(2)}) %copy-start) | copy-done | bytes 1310744
  2.6 0.7 %copy-done.2 = s32[128,16]{0,1:T(8,128)S(1)} copy-done((s32[128,16]{0,1:T(8,128)S(1)}, s32[128,16]{0,1:T(8,128)}, u32[]{:S(2)}) %copy-start.2) | copy-done | bytes 8216
  3.3 1.0 %send.1 = (f32[24,384]{1,0:T(8,128)S(1)}, f32[24,384]{1,0:T(8,128)S(1)}, f32[24,384]{1,0:T(8,128)S(1)}, f32[24,384]{1,0:T(8,128)S(1)}, f32[24,384]{1,0:T(8,128)S...) custom-call(f32[5,512,128]{2,1,0:T(8,128)S(1)} %copy-done, s32[1]{0:T(128)S(6)} %copy.12.count_ref, ...), custom_call_target="tpu_custom_call" | custom-call | flops 200000000 | bytes 3000000 | tf_op jit(solution)/shard_map/send/pallas_call | solution.py:439
  4.3 4.0 %collective-permute-start = (f32[24,384]{1,0:T(8,128)S(1)}, f32[24,384]{1,0:T(8,128)S(1)}, u32[]{:S(2)}, u32[]{:S(2)}) collective-permute-start(f32[24,384]{1,0:T(8,128)S(1)} %get-tuple-element.20), channel_id=1, source_target_pairs={{0,64},{1,65},{2,66},{3,67},{4,68},{5,69},{6,70},{7,71},{8,72},{9,... | collective-permute-start | bytes 110600 | tf_op jit(solution)/shard_map/ppermute | solution.py:445
  8.3 0.0 collective-permute-start.4
  8.3 5.5 %collective-permute-start.5 = (f32[24,384]{1,0:T(8,128)S(1)}, f32[24,384]{1,0:T(8,128)S(1)}, u32[]{:S(2)}, u32[]{:S(2)}) collective-permute-start(f32[24,384]{1,0:T(8,128)S(1)} %get-tuple-element.24), channel_id=1, source_target_pairs={{0,127},{1,2},{2,1},{3,4},{4,3},{5,6},{6,5},{7,8},{8,7},{9,10},{10... | collective-permute-start | bytes 110600 | tf_op jit(solution)/shard_map/ppermute | solution.py:446
  13.8 0.0 collective-permute-start.6
  13.8 1.4 %collective-permute-start.7 = (f32[24,384]{1,0:T(8,128)S(1)}, f32[24,384]{1,0:T(8,128)S(1)}, u32[]{:S(2)}, u32[]{:S(2)}) collective-permute-start(f32[24,384]{1,0:T(8,128)S(1)} %get-tuple-element.26), channel_id=1, source_target_pairs={{0,126},{1,127},{2,4},{3,5},{4,2},{5,3},{6,8},{7,9},{8,6},{9,7},{1... | collective-permute-start | bytes 110600 | tf_op jit(solution)/shard_map/ppermute | solution.py:446
  15.2 0.0 collective-permute-done.i4
  15.2 1.3 %collective-permute-start.1 = (f32[8,128]{1,0:T(8,128)S(1)}, f32[8,128]{1,0:T(8,128)S(1)}, u32[]{:S(2)}, u32[]{:S(2)}) collective-permute-start(f32[8,128]{1,0:T(8,128)S(1)} %slice_maximum_fusion.turn_ref), channel_id=1, source_target_pairs={{0,32},{1,33},{2,34},{3,35},{4,36},{5,37},{6,38},{7,39},{8,40},{9,... | collective-permute-start | bytes 12296 | tf_op jit(solution)/shard_map/ppermute | solution.py:437
  16.5 0.8 %volume_first.1.before_ref = f32[5,512,128]{2,1,0:T(8,128)S(1)} custom-call(f32[8,128]{1,0:T(8,128)S(1)} %slice_maximum_fusion.turn_ref, f32[5,512,128]{2,1,0:T(8,128)S(1)} %copy-done), custom_call_target="tpu_custom_call" | custom-call | flops 1000000000 | bytes 2600000 | tf_op jit(solution)/shard_map/volume_first/pallas_call | solution.py:449
  17.3 1.4 %collective-permute-done.1 = f32[8,128]{1,0:T(8,128)S(1)} collective-permute-done((f32[8,128]{1,0:T(8,128)S(1)}, f32[8,128]{1,0:T(8,128)S(1)}, u32[]{:S(2)}, u32[]{:S(2)}) %collective-permute-start.1) | collective-permute-done | bytes 4128 | tf_op jit(solution)/shard_map/ppermute | solution.py:437
  18.8 0.6 %collective-permute-start.2 = (f32[8,128]{1,0:T(8,128)S(1)}, f32[8,128]{1,0:T(8,128)S(1)}, u32[]{:S(2)}, u32[]{:S(2)}) collective-permute-start(f32[8,128]{1,0:T(8,128)S(1)} %max.13.turn_ref), channel_id=1, source_target_pairs={{0,16},{1,17},{2,18},{3,19},{4,20},{5,21},{6,22},{7,23},{8,24},{9,... | collective-permute-start | bytes 12296 | tf_op jit(solution)/shard_map/ppermute | solution.py:437
  19.4 0.9 %volume_second.1.before_ref = f32[5,512,128]{2,1,0:T(8,128)S(1)} custom-call(f32[8,128]{1,0:T(8,128)S(1)} %max.13.turn_ref, f32[5,512,128]{2,1,0:T(8,128)S(1)} %copy-done, f32[5,512,128]{2,1,0:T(8,128)S(1)} %volume_first.1.before_ref), custom_call_target="tpu_custom_call" | custom-call | flops 1000000000 | bytes 3900000 | tf_op jit(solution)/shard_map/volume_second/pallas_call | solution.py:455
  20.2 3.7 %collective-permute-done.2 = f32[8,128]{1,0:T(8,128)S(1)} collective-permute-done((f32[8,128]{1,0:T(8,128)S(1)}, f32[8,128]{1,0:T(8,128)S(1)}, u32[]{:S(2)}, u32[]{:S(2)}) %collective-permute-start.2) | collective-permute-done | bytes 4128 | tf_op jit(solution)/shard_map/ppermute | solution.py:437
  24.0 0.0 copy-start.9
  24.0 0.0 copy-start.10
  24.0 2.4 %volume_third_gather.1 = (f32[336,512]{1,0:T(8,128)S(1)}, f32[5,512,128]{2,1,0:T(8,128)S(1)}) custom-call(f32[8,128]{1,0:T(8,128)S(1)} %max.14.turn_ref, f32[5,512,128]{2,1,0:T(8,128)S(1)} %copy-done, f32[5,512,128]{2,1,0:T(8,128)S(1)} %volume_second.1.before_ref, bf16[976,768]{1,0:T(8,128)(2,1)S(1)} %get-tuple-element.21.split_ref, s32[5,32]{1,0:T(8,128)S(1)} %bitcast.8, ...), custom_call_target="tpu_custom_call" | custom-call | flops 2000000000 | bytes 6000000 | tf_op jit(solution)/shard_map/volume_third_gather/pallas_call | solution.py:461
  26.4 1.2 %collective-permute-done.3 = f32[8,128]{1,0:T(8,128)S(1)} collective-permute-done((f32[8,128]{1,0:T(8,128)S(1)}, f32[8,128]{1,0:T(8,128)S(1)}, u32[]{:S(2)}, u32[]{:S(2)}) %collective-permute-start.3) | collective-permute-done | bytes 4128 | tf_op jit(solution)/shard_map/ppermute | solution.py:437
  27.6 2.7 %collective-permute-start.8 = (f32[8,128]{1,0:T(8,128)S(1)}, f32[8,128]{1,0:T(8,128)S(1)}, u32[]{:S(2)}, u32[]{:S(2)}) collective-permute-start(f32[8,128]{1,0:T(8,128)S(1)} %max.15.turn_ref), channel_id=1, source_target_pairs={{0,4},{1,5},{2,6},{3,7},{4,0},{5,1},{6,2},{7,3},{8,12},{9,13},{10,... | collective-permute-start | bytes 12296 | tf_op jit(solution)/shard_map/ppermute | solution.py:437
  30.4 2.8 %faces.1.corr_ref = f32[640,512]{1,0:T(8,128)S(1)} custom-call(f32[8,128]{1,0:T(8,128)S(1)} %max.15.turn_ref, f32[336,512]{1,0:T(8,128)S(1)} %get-tuple-element.22.gather_ref, f32[24,384]{1,0:T(8,128)S(1)} %collective-permute-done.4.i0, f32[24,384]{1,0:T(8,128)S(1)} %collective-permute-done.5.i1, f32[24,384]{1,0:T(8,128)S(1)} %collective-permute-done.6.i2, ...), custom_call_target="tpu_custom_call" | custom-call | flops 1000000000 | bytes 3000000 | tf_op jit(solution)/shard_map/faces/pallas_call | solution.py:467
  33.2 0.0 copy-start.4
  33.2 0.0 copy-start.5
  33.2 0.8 %reply.1 = (f32[24,640]{1,0:T(8,128)S(1)}, f32[24,640]{1,0:T(8,128)S(1)}, f32[24,640]{1,0:T(8,128)S(1)}, f32[24,640]{1,0:T(8,128)S(1)}, f32[24,640]{1,0:T(8,128)S(1)}, /*index=5*/f32[8,128]{1,0:T(8,128)S(1)}) custom-call(f32[640,512]{1,0:T(8,128)S(1)} %faces.1.corr_ref, s32[5,32]{1,0:T(8,128)S(1)} %bitcast.10, s32[2,128]{1,0:T(2,128)S(1)} %bitcast.14, ...), custom_call_target="tpu_custom_call" | custom-call | flops 500000000 | bytes 2000000 | tf_op jit(solution)/shard_map/reply/pallas_call | solution.py:471
  34.0 0.1 collective-permute-start.9
  34.1 5.7 %collective-permute-start.10 = (f32[24,640]{1,0:T(8,128)S(1)}, f32[24,640]{1,0:T(8,128)S(1)}, u32[]{:S(2)}, u32[]{:S(2)}) collective-permute-start(f32[24,640]{1,0:T(8,128)S(1)} %get-tuple-element.32), channel_id=1, source_target_pairs={{0,127},{1,2},{2,1},{3,4},{4,3},{5,6},{6,5},{7,8},{8,7},{9,10},{10... | collective-permute-start | bytes 184328 | tf_op jit(solution)/shard_map/ppermute | solution.py:477
  39.8 1.2 %collective-permute-start.12 = (f32[24,640]{1,0:T(8,128)S(1)}, f32[24,640]{1,0:T(8,128)S(1)}, u32[]{:S(2)}, u32[]{:S(2)}) collective-permute-start(f32[24,640]{1,0:T(8,128)S(1)} %get-tuple-element.34), channel_id=1, source_target_pairs={{0,126},{1,127},{2,4},{3,5},{4,2},{5,3},{6,8},{7,9},{8,6},{9,7},{1... | collective-permute-start | bytes 184328 | tf_op jit(solution)/shard_map/ppermute | solution.py:477
  41.1 1.2 %collective-permute-start.13 = (f32[24,640]{1,0:T(8,128)S(1)}, f32[24,640]{1,0:T(8,128)S(1)}, u32[]{:S(2)}, u32[]{:S(2)}) collective-permute-start(f32[24,640]{1,0:T(8,128)S(1)} %get-tuple-element.35), channel_id=1, source_target_pairs={{0,64},{1,65},{2,66},{3,67},{4,68},{5,69},{6,70},{7,71},{8,72},{9,... | collective-permute-start | bytes 184328 | tf_op jit(solution)/shard_map/ppermute | solution.py:477
  42.2 2.1 %lift.1 = (f32[5,512,128]{2,1,0:T(8,128)S(1)}, f32[5,512,128]{2,1,0:T(8,128)S(1)}) custom-call(f32[8,128]{1,0:T(8,128)S(1)} %get-tuple-element.27.turn_ref.fast_ref, f32[640,512]{1,0:T(8,128)S(1)} %faces.1.corr_ref, s32[5,32]{1,0:T(8,128)S(1)} %bitcast.11, s32[2,128]{1,0:T(2,128)S(1)} %bitcast.15, f32[5,512,128]{2,1,0:T(8,128)S(1)} %get-tuple-element.28.volume_ref, ...), custom_call_target="tpu_custom_call" | custom-call | flops 1500000000 | bytes 6000000 | tf_op jit(solution)/shard_map/lift/pallas_call | solution.py:478
  44.4 5.1 %collective-permute-done.12.i3 = f32[24,640]{1,0:T(8,128)S(1)} collective-permute-done((f32[24,640]{1,0:T(8,128)S(1)}, f32[24,640]{1,0:T(8,128)S(1)}, u32[]{:S(2)}, u32[]{:S(2)}) %collective-permute-start.12) | collective-permute-done | bytes 61472 | tf_op jit(solution)/shard_map/ppermute | solution.py:477
  49.5 2.5 %finish.1 = (f32[5,512,128]{2,1,0:T(8,128)}, f32[5,512,128]{2,1,0:T(8,128)}) custom-call(f32[5,512,128]{2,1,0:T(8,128)S(1)} %get-tuple-element.29.steady_ref, f32[5,512,128]{2,1,0:T(8,128)S(1)} %get-tuple-element.30.rate_ref, f32[5,512,128]{2,1,0:T(8,128)S(1)} %copy-done.1, f32[24,640]{1,0:T(8,128)S(1)} %collective-permute-done.9.i0, ...), custom_call_target="tpu_custom_call" | custom-call | flops 200000000 | bytes 6000000 | tf_op jit(solution)/shard_map/finish/pallas_call | solution.py:482
  (30 shorter events, 0.1 us)
Async XLA Ops:
  1.3 1.3 %copy-start = (f32[5,512,128]{2,1,0:T(8,128)S(1)}, f32[5,512,128]{2,1,0:T(8,128)}, u32[]{:S(2)}) copy-start(f32[5,512,128]{2,1,0:T(8,128)} %state_ref.9) | copy-start | bytes 3932164
  2.6 0.7 %copy-start.2 = (s32[128,16]{0,1:T(8,128)S(1)}, s32[128,16]{0,1:T(8,128)}, u32[]{:S(2)}) copy-start(s32[128,16]{0,1:T(8,128)} %param.14) | copy-start | bytes 24580
  4.3 10.9 %collective-permute-start = (f32[24,384]{1,0:T(8,128)S(1)}, f32[24,384]{1,0:T(8,128)S(1)}, u32[]{:S(2)}, u32[]{:S(2)}) collective-permute-start(f32[24,384]{1,0:T(8,128)S(1)} %get-tuple-element.20), channel_id=1, source_target_pairs={{0,64},{1,65},{2,66},{3,67},{4,68},{5,69},{6,70},{7,71},{8,72},{9,... | collective-permute-start | bytes 110600 | tf_op jit(solution)/shard_map/ppermute | solution.py:445
  8.3 22.0 %collective-permute-start.4 = (f32[24,384]{1,0:T(8,128)S(1)}, f32[24,384]{1,0:T(8,128)S(1)}, u32[]{:S(2)}, u32[]{:S(2)}) collective-permute-start(f32[24,384]{1,0:T(8,128)S(1)} %get-tuple-element.23), channel_id=1, source_target_pairs={{0,1},{1,0},{2,3},{3,2},{4,5},{5,4},{6,7},{7,6},{8,9},{9,8},{10,11... | collective-permute-start | bytes 110600 | tf_op jit(solution)/shard_map/ppermute | solution.py:446
  8.3 22.0 %collective-permute-start.5 = (f32[24,384]{1,0:T(8,128)S(1)}, f32[24,384]{1,0:T(8,128)S(1)}, u32[]{:S(2)}, u32[]{:S(2)}) collective-permute-start(f32[24,384]{1,0:T(8,128)S(1)} %get-tuple-element.24), channel_id=1, source_target_pairs={{0,127},{1,2},{2,1},{3,4},{4,3},{5,6},{6,5},{7,8},{8,7},{9,10},{10... | collective-permute-start | bytes 110600 | tf_op jit(solution)/shard_map/ppermute | solution.py:446
  13.8 16.5 %collective-permute-start.6 = (f32[24,384]{1,0:T(8,128)S(1)}, f32[24,384]{1,0:T(8,128)S(1)}, u32[]{:S(2)}, u32[]{:S(2)}) collective-permute-start(f32[24,384]{1,0:T(8,128)S(1)} %get-tuple-element.25), channel_id=1, source_target_pairs={{0,2},{1,3},{2,0},{3,1},{4,6},{5,7},{6,4},{7,5},{8,10},{9,11},{10,... | collective-permute-start | bytes 110600 | tf_op jit(solution)/shard_map/ppermute | solution.py:446
  13.8 16.5 %collective-permute-start.7 = (f32[24,384]{1,0:T(8,128)S(1)}, f32[24,384]{1,0:T(8,128)S(1)}, u32[]{:S(2)}, u32[]{:S(2)}) collective-permute-start(f32[24,384]{1,0:T(8,128)S(1)} %get-tuple-element.26), channel_id=1, source_target_pairs={{0,126},{1,127},{2,4},{3,5},{4,2},{5,3},{6,8},{7,9},{8,6},{9,7},{1... | collective-permute-start | bytes 110600 | tf_op jit(solution)/shard_map/ppermute | solution.py:446
  15.2 3.6 %collective-permute-start.1 = (f32[8,128]{1,0:T(8,128)S(1)}, f32[8,128]{1,0:T(8,128)S(1)}, u32[]{:S(2)}, u32[]{:S(2)}) collective-permute-start(f32[8,128]{1,0:T(8,128)S(1)} %slice_maximum_fusion.turn_ref), channel_id=1, source_target_pairs={{0,32},{1,33},{2,34},{3,35},{4,36},{5,37},{6,38},{7,39},{8,40},{9,... | collective-permute-start | bytes 12296 | tf_op jit(solution)/shard_map/ppermute | solution.py:437
  18.8 5.2 %copy-start.6 = (s32[32,5]{0,1:T(8,128)S(1)}, s32[32,5]{0,1:T(8,128)}, u32[]{:S(2)}) copy-start(s32[32,5]{0,1:T(8,128)} %param.15) | copy-start | bytes 1924
  18.8 5.2 %copy-start.7 = (s32[128,2]{0,1:T(2,128)S(1)}, s32[128,2]{0,1:T(2,128)}, u32[]{:S(2)}) copy-start(s32[128,2]{0,1:T(2,128)} %param.16) | copy-start | bytes 3076
  18.8 5.2 %copy-start.8 = (f32[256,256]{1,0:T(8,128)S(1)}, f32[256,256]{1,0:T(8,128)}, u32[]{:S(2)}) copy-start(f32[256,256]{1,0:T(8,128)} %constant.6.clone.mix_ref) | copy-start | bytes 786436
  18.8 5.2 %collective-permute-start.2 = (f32[8,128]{1,0:T(8,128)S(1)}, f32[8,128]{1,0:T(8,128)S(1)}, u32[]{:S(2)}, u32[]{:S(2)}) collective-permute-start(f32[8,128]{1,0:T(8,128)S(1)} %max.13.turn_ref), channel_id=1, source_target_pairs={{0,16},{1,17},{2,18},{3,19},{4,20},{5,21},{6,22},{7,23},{8,24},{9,... | collective-permute-start | bytes 12296 | tf_op jit(solution)/shard_map/ppermute | solution.py:437
  24.0 3.6 %collective-permute-start.3 = (f32[8,128]{1,0:T(8,128)S(1)}, f32[8,128]{1,0:T(8,128)S(1)}, u32[]{:S(2)}, u32[]{:S(2)}) collective-permute-start(f32[8,128]{1,0:T(8,128)S(1)} %max.14.turn_ref), channel_id=1, source_target_pairs={{0,8},{1,9},{2,10},{3,11},{4,12},{5,13},{6,14},{7,15},{8,0},{9,1},... | collective-permute-start | bytes 12296 | tf_op jit(solution)/shard_map/ppermute | solution.py:437
  24.0 6.3 %copy-start.9 = (f32[256,64]{1,0:T(8,128)S(1)}, f32[256,64]{1,0:T(8,128)}, u32[]{:S(2)}) copy-start(f32[256,64]{1,0:T(8,128)} %constant.8.clone.back_ref) | copy-start | bytes 196612
  24.0 6.3 %copy-start.10 = (f32[256,64]{1,0:T(8,128)S(1)}, f32[256,64]{1,0:T(8,128)}, u32[]{:S(2)}) copy-start(f32[256,64]{1,0:T(8,128)} %constant.7.clone.project_ref) | copy-start | bytes 196612
  27.6 5.6 %collective-permute-start.8 = (f32[8,128]{1,0:T(8,128)S(1)}, f32[8,128]{1,0:T(8,128)S(1)}, u32[]{:S(2)}, u32[]{:S(2)}) collective-permute-start(f32[8,128]{1,0:T(8,128)S(1)} %max.15.turn_ref), channel_id=1, source_target_pairs={{0,4},{1,5},{2,6},{3,7},{4,0},{5,1},{6,2},{7,3},{8,12},{9,13},{10,... | collective-permute-start | bytes 12296 | tf_op jit(solution)/shard_map/ppermute | solution.py:437
  33.2 9.1 %copy-start.4 = (f32[128]{0:T(128)S(1)}, f32[128]{0:T(128)}, u32[]{:S(2)}) copy-start(f32[128]{0:T(128)} %param.12) | copy-start | bytes 1540
  33.2 9.1 %copy-start.5 = (f32[5,512,128]{2,1,0:T(8,128)S(1)}, f32[5,512,128]{2,1,0:T(8,128)}, u32[]{:S(2)}) copy-start(f32[5,512,128]{2,1,0:T(8,128)} %register_ref.1) | copy-start | bytes 3932164
  34.0 10.3 %collective-permute-start.9 = (f32[24,640]{1,0:T(8,128)S(1)}, f32[24,640]{1,0:T(8,128)S(1)}, u32[]{:S(2)}, u32[]{:S(2)}) collective-permute-start(f32[24,640]{1,0:T(8,128)S(1)} %get-tuple-element.31), channel_id=1, source_target_pairs={{0,1},{1,0},{2,3},{3,2},{4,5},{5,4},{6,7},{7,6},{8,9},{9,8},{10,11... | collective-permute-start | bytes 184328 | tf_op jit(solution)/shard_map/ppermute | solution.py:477
  34.1 10.2 %collective-permute-start.10 = (f32[24,640]{1,0:T(8,128)S(1)}, f32[24,640]{1,0:T(8,128)S(1)}, u32[]{:S(2)}, u32[]{:S(2)}) collective-permute-start(f32[24,640]{1,0:T(8,128)S(1)} %get-tuple-element.32), channel_id=1, source_target_pairs={{0,127},{1,2},{2,1},{3,4},{4,3},{5,6},{6,5},{7,8},{8,7},{9,10},{10... | collective-permute-start | bytes 184328 | tf_op jit(solution)/shard_map/ppermute | solution.py:477
  39.8 4.5 %collective-permute-start.11 = (f32[24,640]{1,0:T(8,128)S(1)}, f32[24,640]{1,0:T(8,128)S(1)}, u32[]{:S(2)}, u32[]{:S(2)}) collective-permute-start(f32[24,640]{1,0:T(8,128)S(1)} %get-tuple-element.33), channel_id=1, source_target_pairs={{0,2},{1,3},{2,0},{3,1},{4,6},{5,7},{6,4},{7,5},{8,10},{9,11},{10,... | collective-permute-start | bytes 184328 | tf_op jit(solution)/shard_map/ppermute | solution.py:477
  39.8 9.7 %collective-permute-start.12 = (f32[24,640]{1,0:T(8,128)S(1)}, f32[24,640]{1,0:T(8,128)S(1)}, u32[]{:S(2)}, u32[]{:S(2)}) collective-permute-start(f32[24,640]{1,0:T(8,128)S(1)} %get-tuple-element.34), channel_id=1, source_target_pairs={{0,126},{1,127},{2,4},{3,5},{4,2},{5,3},{6,8},{7,9},{8,6},{9,7},{1... | collective-permute-start | bytes 184328 | tf_op jit(solution)/shard_map/ppermute | solution.py:477
  41.1 8.4 %collective-permute-start.13 = (f32[24,640]{1,0:T(8,128)S(1)}, f32[24,640]{1,0:T(8,128)S(1)}, u32[]{:S(2)}, u32[]{:S(2)}) collective-permute-start(f32[24,640]{1,0:T(8,128)S(1)} %get-tuple-element.35), channel_id=1, source_target_pairs={{0,64},{1,65},{2,66},{3,67},{4,68},{5,69},{6,70},{7,71},{8,72},{9,... | collective-permute-start | bytes 184328 | tf_op jit(solution)/shard_map/ppermute | solution.py:477
  42.2 7.3 %copy-start.1 = (f32[5,512,128]{2,1,0:T(8,128)S(1)}, f32[5,512,128]{2,1,0:T(8,128)}, u32[]{:S(2)}) copy-start(f32[5,512,128]{2,1,0:T(8,128)} %state_ref.9) | copy-start | bytes 3932164
  42.2 7.3 %copy-start.3 = (s32[128,16]{0,1:T(8,128)S(1)}, s32[128,16]{0,1:T(8,128)}, u32[]{:S(2)}) copy-start(s32[128,16]{0,1:T(8,128)} %param.14) | copy-start | bytes 24580

commit v3 on v2

--- a/solution.py
+++ b/solution.py
@@ -77,14 +77,17 @@
 def pairings(devices):
     index = np.arange(devices)
     low = index % 4 < 2
-    partners = [
-        index ^ 1,
-        np.where(index % 2 == 1, index + 1, index - 1) % devices,
-        np.where(low, index + 2, index - 2) % devices,
-        np.where(low, index - 2, index + 2) % devices,
-        (index + devices // 2) % devices,
-    ]
-    return [[(int(d), int(p)) for d, p in enumerate(side)] for side in partners]
+    y = index // 8 % 4
+    partners = dict(
+        chip=index ^ 1,
+        pair=np.where(low, index + 2, index - 2) % devices,
+        next=np.where(low, index - 2, index + 2) % devices,
+        far=(index + devices // 2) % devices,
+        y_first=index ^ 8,
+        y_second=index + 8 * (np.where(y % 2 == 1, y + 1, y - 1) % 4 - y),
+        z_first=index ^ 32,
+    )
+    return {name: [(int(d), int(p)) for d, p in enumerate(side)] for name, side in partners.items()}
 
 
 def partner_of(me, devices):
@@ -100,6 +103,17 @@
     mid = rest.astype(BF16)
     low = (rest - mid.astype(F32)).astype(BF16)
     return high, mid, low
+
+
+def split2(value):
+    high = value.astype(BF16)
+    return high, (value - high.astype(F32)).astype(BF16)
+
+
+def stack_terms(matrix):
+    high = matrix.astype(BF16)
+    mid = (matrix - high.astype(np.float32)).astype(BF16)
+    return jnp.asarray(np.concatenate([high, high, mid, mid], axis=1))
 
 
 def iota(shape, dim):
@@ -141,9 +155,9 @@
         ref[field, place, :] = ref[field, place, :] + value
 
 
-def out_columns(send_ref, partners):
+def out_columns(slots_ref, partners):
     lane = iota((WIDTH, ELEMS), 1)
-    slots = send_ref[...]
+    slots = slots_ref[...]
     columns = [
         jnp.sum(jnp.where(lane == partners[peer], slots, 0), axis=1, keepdims=True) for peer in range(PEERS)
     ]
@@ -172,8 +186,7 @@
     return one_hot(ref_rows(mortar_ref, face_ref) == target)
 
 
-def send_kernel(devices, state_ref, count_ref, send_ref, m0, m1, m2, m3, m4, split_ref, fast_ref):
-    partners = partner_of(lax.axis_index("sfc"), devices)
+def table_kernel(state_ref, split_ref, speed_ref):
     fastest = jnp.zeros((8, ELEMS), F32)
     for a in range(8):
         part = slice(64 * a, 64 * a + 64)
@@ -183,8 +196,7 @@
         press = (GAMMA - 1.0) * (energy - 0.5 * square * inverse)
         speed = jnp.sqrt(square) * inverse + jnp.sqrt(GAMMA * press * inverse)
         fastest = jnp.maximum(fastest, jnp.max(speed.reshape(8, 8, ELEMS), axis=0))
-    fastest = jnp.where(iota((8, ELEMS), 1) < count_ref[0], fastest, 0.0)
-    fast_ref[...] = fastest
+    speed_ref[...] = fastest
     for face in range(6):
         lanes = slice(face * ELEMS, (face + 1) * ELEMS)
         for field in range(5):
@@ -195,16 +207,49 @@
     face = iota((16, SLOTS), 1) // ELEMS
     sign = jnp.where(face % 2 == 1, F32(1.0), F32(-1.0))
     split_ref[3 * ROWS : 3 * ROWS + 16, :] = jnp.where(row == face // 2, sign, 0.0).astype(BF16)
-    chosen = one_hot(out_columns(send_ref, partners) == iota((ELEMS, SLOTS), 1))
+
+
+def send_kernel(
+    devices, split_ref, speed_ref, count_ref, slots_ref, metric_ref, chip_ref, raw_ref, fast_ref, scale_ref
+):
+    partners = partner_of(lax.axis_index("sfc"), devices)
+    live = iota((8, ELEMS), 1) < count_ref[0]
+    scale_ref[...] = jnp.where(live, COURANT * metric_ref[...], 0.0)
+    fastest = jnp.max(jnp.where(live, speed_ref[...], 0.0), axis=0, keepdims=True)
+    fastest = jnp.max(fastest, axis=1, keepdims=True)
+    fast_ref[...] = jnp.broadcast_to(fastest, (8, ELEMS))
+    chosen = one_hot(out_columns(slots_ref, partners) == iota((ELEMS, SLOTS), 1))
     picked = dot_nt(split_ref[...], chosen)
     rows = jnp.concatenate(
-        [thirds(picked, ROWS), picked[3 * ROWS : 3 * ROWS + 16], jnp.zeros((48, ELEMS), F32)], axis=0
+        [thirds(picked, ROWS), picked[3 * ROWS : 3 * ROWS + 16], jnp.broadcast_to(fastest, (48, ELEMS))], axis=0
     )
     message = rows.T
-    for peer, ref in enumerate((m0, m1, m2, m3, m4)):
-        ref[0:WIDTH, :] = message[peer * WIDTH : (peer + 1) * WIDTH]
-        ref[WIDTH : WIDTH + 8, 0:ELEMS] = fastest
-        ref[WIDTH : WIDTH + 8, ELEMS:] = jnp.zeros((8, 256), F32)
+    chip_ref[...] = message[0 : 2 * WIDTH]
+    raw_ref[...] = message[2 * WIDTH : 5 * WIDTH]
+
+
+def pair_kernel(raw_ref, chip_ref, fast_ref, pair_ref, next_ref, best_ref):
+    best = jnp.maximum(fast_ref[...], chip_ref[0:8, 256:384])
+    best_ref[...] = best
+    for k, ref in enumerate((pair_ref, next_ref)):
+        ref[0:WIDTH, :] = raw_ref[k * WIDTH : (k + 1) * WIDTH, :]
+        ref[WIDTH : 2 * WIDTH, :] = chip_ref[WIDTH : 2 * WIDTH, :]
+    pair_ref[0:8, 256:384] = jnp.where(iota((8, ELEMS), 1) < 80, raw_ref[0:8, 256:384], best)
+
+
+def far_kernel(turn_ref, raw_ref, pair_ref, fast_ref, far_ref, best_ref):
+    best = jnp.maximum(fast_ref[...], pair_ref[0:8, 256:384])
+    best_ref[...] = best
+    far_ref[...] = raw_ref[2 * WIDTH : 3 * WIDTH, :]
+    far_ref[0:8, 256:384] = jnp.where(iota((8, ELEMS), 1) < 80, raw_ref[2 * WIDTH : 2 * WIDTH + 8, 256:384], best)
+
+
+def gather_blocks(devices, chip_ref, pair_ref, next_ref, far_ref, columns):
+    place = lax.axis_index("sfc") % 4
+    first = slice(0, WIDTH)
+    second = slice(WIDTH, 2 * WIDTH)
+    passed = jnp.where((place == 0) | (place == 3), next_ref[second, columns], pair_ref[second, columns])
+    return [chip_ref[first, columns], passed, pair_ref[first, columns], next_ref[first, columns], far_ref[first, columns]]
 
 
 def axis_flux(state_ref, axis, ref):
@@ -254,11 +299,14 @@
     lax.fori_loop(0, 5, body, 0)
 
 
-def third_kernel(turn_ref, state_ref, before_ref, split_ref, mortar_ref, face_ref, mix_ref, gather_ref, volume_ref, flux):
-    axis_flux(state_ref, 2, flux)
+def gather_kernel(split_ref, mortar_ref, face_ref, gather_ref):
     picked = jnp.dot(split_ref[...], own_choice(mortar_ref, face_ref), preferred_element_type=F32)
     gather_ref[0:ROWS, :] = thirds(picked, ROWS)
     gather_ref[ROWS : ROWS + 16, :] = picked[3 * ROWS : 3 * ROWS + 16]
+
+
+def third_kernel(turn_ref, state_ref, before_ref, mix_ref, volume_ref, flux):
+    axis_flux(state_ref, 2, flux)
     for half in range(2):
         part = slice(256 * half, 256 * half + 256)
         mixed = jnp.dot(
@@ -296,20 +344,22 @@
 
 
 def by_child(matrix_ref, values):
+    high, mid = split2(jnp.concatenate(values, axis=1))
     stack = jnp.dot(
-        matrix_ref[...], jnp.concatenate(values, axis=1), precision=HIGHEST, preferred_element_type=F32
+        matrix_ref[...], jnp.concatenate([high, mid, high, mid], axis=0), preferred_element_type=F32
     )
     return [child_select(stack, index) for index in range(len(values))]
 
 
 def face_kernel(
-    devices, turn_ref, gather_ref, i0, i1, i2, i3, i4, mortar_ref, face_ref, project_ref, back_ref, corr_ref, pool_ref
+    devices, turn_ref, gather_ref, i0, i2, i3, i4, mortar_ref, face_ref, project_ref, back_ref,
+    corr_ref, chip_ref, raw_ref, pool_ref
 ):
     partners = partner_of(lax.axis_index("sfc"), devices)
-    incoming = (i0, i1, i2, i3, i4)
+    incoming = gather_blocks(devices, i0, i2, i3, i4, slice(0, 384))
     remote = remote_choice(mortar_ref, face_ref, partners)
     arrived = jnp.concatenate(
-        [ref[0:WIDTH, :] for ref in incoming] + [jnp.zeros((ELEMS - PEERS * WIDTH, 384), F32)], axis=0
+        incoming + [jnp.zeros((ELEMS - PEERS * WIDTH, 384), F32)], axis=0
     ).T
     high, mid, low = split3(arrived[:ROWS])
     picked = jnp.dot(
@@ -343,26 +393,29 @@
         corr_ref[more, 128:256] = jump
         corr_ref[rows, 384:512] = -even - right_f[k]
         corr_ref[more, 384:512] = -jump
-
-
-def reply_kernel(devices, corr_ref, mortar_ref, face_ref, turn_ref, last_ref, m0, m1, m2, m3, m4, fast_ref):
-    partners = partner_of(lax.axis_index("sfc"), devices)
-    remote = remote_choice(mortar_ref, face_ref, partners)
-    fast = jnp.maximum(turn_ref[...], last_ref[...])
-    fast_ref[...] = fast
     back = sum(dot_nt(part, remote) for part in split3(corr_ref[...])).T
-    for peer, ref in enumerate((m0, m1, m2, m3, m4)):
-        ref[0:WIDTH, :] = back[peer * WIDTH : (peer + 1) * WIDTH]
-        ref[WIDTH : WIDTH + 8, 0:ELEMS] = fast
-        ref[WIDTH : WIDTH + 8, ELEMS:] = jnp.zeros((8, 512), F32)
+    chip_ref[...] = back[0 : 2 * WIDTH]
+    raw_ref[...] = back[2 * WIDTH : 5 * WIDTH]
+
+
+def reply_kernel(turn_ref, last_ref, raw_ref, chip_ref, pair_ref, next_ref, far_ref, best_ref):
+    best = jnp.maximum(turn_ref[...], last_ref[...])
+    best_ref[...] = best
+    pair_ref[0:WIDTH, 0 : 2 * ROWS] = raw_ref[0:WIDTH, :]
+    next_ref[0:WIDTH, 0 : 2 * ROWS] = raw_ref[WIDTH : 2 * WIDTH, :]
+    far_ref[:, 0 : 2 * ROWS] = raw_ref[2 * WIDTH : 3 * WIDTH, :]
+    for ref in (pair_ref, next_ref):
+        ref[WIDTH : 2 * WIDTH, 0 : 2 * ROWS] = chip_ref[WIDTH : 2 * WIDTH, :]
+    for ref in (pair_ref, next_ref, far_ref):
+        for k in range(ref.shape[0] // 8):
+            ref[8 * k : 8 * k + 8, 2 * ROWS :] = best
 
 
 def lift_kernel(
-    turn_ref, corr_ref, mortar_ref, face_ref, volume_ref, register_ref, metric_ref, count_ref, steady_ref, rate_ref
+    turn_ref, corr_ref, mortar_ref, face_ref, volume_ref, register_ref, scale_ref, steady_ref, rate_ref
 ):
     chosen = own_choice(mortar_ref, face_ref)
-    live = iota((1, ELEMS), 1) < count_ref[0]
-    scale = jnp.where(live, COURANT * metric_ref[...], 0.0)
+    scale = scale_ref[0:1, :]
     for field in range(5):
         steady_ref[field] = SECTION_A * register_ref[field]
         rate_ref[field] = -scale * volume_ref[field]
@@ -379,45 +432,55 @@
 
 
 def finish_kernel(
-    devices, steady_ref, rate_ref, state_ref, i0, i1, i2, i3, i4, fast_ref, send_ref, metric_ref, count_ref,
-    state_out, register_out
+    devices, steady_ref, rate_ref, state_ref, i0, i2, i3, i4, fast_ref, slots_ref, scale_ref,
+    state_hbm, register_hbm, state_out, register_out, sems
 ):
     partners = partner_of(lax.axis_index("sfc"), devices)
     fast = fast_ref[...]
-    for ref in (i0, i1, i2, i3):
-        fast = jnp.maximum(fast, ref[WIDTH : WIDTH + 8, 0:ELEMS])
+    for ref in (i2, i3, i4):
+        fast = jnp.maximum(fast, ref[0:8, 2 * ROWS :])
+    fast = jnp.where(iota((8, ELEMS), 1) < 80, 0.0, fast)
     lam = jnp.max(jnp.max(fast, axis=0, keepdims=True), axis=1, keepdims=True)
     inverse = 1.0 / lam
-    live = iota((1, ELEMS), 1) < count_ref[0]
-    lift = jnp.where(live, -LIFT * COURANT * metric_ref[...], 0.0) * inverse
-    chosen = one_hot(out_columns(send_ref, partners) == iota((ELEMS, SLOTS), 1))
+    lift = -LIFT * scale_ref[0:1, :] * inverse
+    chosen = one_hot(out_columns(slots_ref, partners) == iota((ELEMS, SLOTS), 1))
     arrived = jnp.concatenate(
-        [ref[0:WIDTH, 0:ROWS] + lam * ref[0:WIDTH, ROWS : 2 * ROWS] for ref in (i0, i1, i2, i3, i4)]
+        [
+            block[:, 0:ROWS] + lam * block[:, ROWS : 2 * ROWS]
+            for block in gather_blocks(devices, i0, i2, i3, i4, slice(0, 2 * ROWS))
+        ]
         + [jnp.zeros((ELEMS - PEERS * WIDTH, ROWS), F32)],
         axis=0,
     ).T
-    layers = sum(jnp.dot(part, chosen, preferred_element_type=F32) for part in split3(arrived))
+    parts = jnp.concatenate(split3(arrived), axis=0)
+    layers = thirds(jnp.dot(parts, chosen, preferred_element_type=F32), ROWS)
+    copies = []
     for field in range(5):
         register_out[field] = steady_ref[field] + inverse * rate_ref[field]
-    for face in range(6):
-        lanes = slice(face * ELEMS, (face + 1) * ELEMS)
-        for field in range(5):
+        for face in range(6):
+            lanes = slice(face * ELEMS, (face + 1) * ELEMS)
             add_layer(register_out, field, face, lift * layers[64 * field : 64 * field + 64, lanes])
-    for field in range(5):
+        copies.append(pltpu.make_async_copy(register_out.at[field], register_hbm.at[field], sems.at[2 * field]))
+        copies[-1].start()
         state_out[field] = state_ref[field] + SECTION_B * register_out[field]
+        copies.append(pltpu.make_async_copy(state_out.at[field], state_hbm.at[field], sems.at[2 * field + 1]))
+        copies[-1].start()
+    for copy in copies:
+        copy.wait()
 
 
 VMEM = pl.BlockSpec(memory_space=pltpu.VMEM)
 SMEM = pl.BlockSpec(memory_space=pltpu.SMEM)
-
-
-def call(kernel, name, outs, specs, cost, scratch=()):
+HBM = pl.BlockSpec(memory_space=pltpu.HBM)
+
+
+def call(kernel, name, outs, specs, cost, scratch=(), out_specs=None):
     return pl.pallas_call(
         kernel,
         name=name,
         out_shape=[jax.ShapeDtypeStruct(shape, dtype) for shape, dtype in outs],
         in_specs=specs,
-        out_specs=[VMEM] * len(outs),
+        out_specs=out_specs or [VMEM] * len(outs),
         scratch_shapes=list(scratch),
         compiler_params=pltpu.CompilerParams(vmem_limit_bytes=40 * 1024 * 1024),
         cost_estimate=pl.CostEstimate(flops=cost[0], bytes_accessed=cost[1], transcendentals=0),
@@ -433,56 +496,67 @@
     cube = (5, 512, ELEMS)
     flux = [pltpu.VMEM(cube, F32)]
 
-    def exchange(value, shift):
-        return lax.ppermute(value, "sfc", [(d, d ^ shift) for d in range(devices)])
-
-    first = call(
-        functools.partial(send_kernel, devices), "send",
-        [((WIDTH + 8, 384), F32)] * 5 + [((3 * ROWS + 16, SLOTS), BF16), ((8, ELEMS), F32)],
-        [VMEM, SMEM, VMEM], (200_000_000, 3_000_000),
-    )(state, counts, sends)
-    messages, split, fast = first[:5], first[5], first[6]
-    far = lax.ppermute(messages[4], "sfc", pairs[4])
-    near = [lax.ppermute(message, "sfc", pair) for message, pair in zip(messages[:4], pairs[:4])]
-    fast = jnp.maximum(fast, far[WIDTH : WIDTH + 8, 0:ELEMS])
-    came = exchange(fast, 32)
+    def exchange(value, name):
+        return lax.ppermute(value, "sfc", pairs[name])
+
+    one, two, three = [((k * WIDTH, 384), F32) for k in (1, 2, 3)]
+    row = ((8, ELEMS), F32)
+    split, speed = call(
+        table_kernel, "table", [((3 * ROWS + 16, SLOTS), BF16), row], [VMEM], (100_000_000, 3_000_000)
+    )(state)
+    chip, raw, fast, scale = call(
+        functools.partial(send_kernel, devices), "send", [two, three, row, row], [VMEM] * 2 + [SMEM] + [VMEM] * 2,
+        (200_000_000, 2_000_000),
+    )(split, speed, counts, sends, metric)
+    chip = exchange(chip, "chip")
+    pair, onward, fast = call(pair_kernel, "pair", [two, two, row], [VMEM] * 3, (0, 200_000))(raw, chip, fast)
+    onward = exchange(onward, "next")
+    pair = exchange(pair, "pair")
+    (gathered,) = call(
+        gather_kernel, "gather", [((ROWS + 16, 512), F32)], [VMEM] * 3, (1_000_000_000, 2_000_000)
+    )(split, mortars, faces)
+    far, fast = call(far_kernel, "far", [one, row], [VMEM] * 4, (0, 200_000))(gathered, raw, pair, fast)
+    far = exchange(far, "far")
+    fast = jnp.maximum(fast, far[0:8, 256:384])
+    came = exchange(fast, "y_first")
     (volume,) = call(
         functools.partial(first_kernel, deriv), "volume_first", [(cube, F32)], [VMEM] * 2,
         (1_000_000_000, 2_600_000), flux,
     )(fast, state)
     fast = jnp.maximum(fast, came)
-    came = exchange(fast, 16)
+    came = exchange(fast, "y_second")
+    corrections, chip, raw = call(
+        functools.partial(face_kernel, devices), "faces",
+        [((2 * ROWS, 512), F32), ((2 * WIDTH, 2 * ROWS), F32), ((3 * WIDTH, 2 * ROWS), F32)],
+        [VMEM] * 10, (1_000_000_000, 3_000_000), [pltpu.VMEM((ROWS, 512), F32)],
+    )(fast, gathered, chip, pair, onward, far, mortars, faces, stack_terms(project), stack_terms(back))
+    fast = jnp.maximum(fast, came)
+    came = exchange(fast, "z_first")
+    chip = exchange(chip, "chip")
     (volume,) = call(
         functools.partial(second_kernel, deriv), "volume_second", [(cube, F32)], [VMEM] * 3,
         (1_000_000_000, 3_900_000), flux,
     )(fast, state, volume)
-    fast = jnp.maximum(fast, came)
-    came = exchange(fast, 8)
-    gathered, volume = call(
-        third_kernel, "volume_third_gather", [((ROWS + 16, 512), F32), (cube, F32)], [VMEM] * 7,
-        (2_000_000_000, 6_000_000), flux,
-    )(fast, state, volume, split, mortars, faces, jnp.asarray(mix))
-    fast = jnp.maximum(fast, came)
-    came = exchange(fast, 4)
-    (corrections,) = call(
-        functools.partial(face_kernel, devices), "faces", [((2 * ROWS, 512), F32)], [VMEM] * 11,
-        (1_000_000_000, 3_000_000), [pltpu.VMEM((ROWS, 512), F32)],
-    )(fast, gathered, *near, far, mortars, faces, jnp.asarray(project), jnp.asarray(back))
-    second = call(
-        functools.partial(reply_kernel, devices), "reply",
-        [((WIDTH + 8, 2 * ROWS), F32)] * 5 + [((8, ELEMS), F32)],
-        [VMEM] * 5, (500_000_000, 2_000_000),
-    )(corrections, mortars, faces, fast, came)
-    replies, fast = second[:5], second[5]
-    returned = [lax.ppermute(reply, "sfc", pair) for reply, pair in zip(replies, pairs)]
+    wide = 2 * ROWS + ELEMS
+    pair, onward, far, fast = call(
+        reply_kernel, "reply",
+        [((2 * WIDTH, wide), F32)] * 2 + [((WIDTH, wide), F32), row], [VMEM] * 4, (0, 500_000),
+    )(fast, came, raw, chip)
+    onward = exchange(onward, "next")
+    far = exchange(far, "far")
+    pair = exchange(pair, "pair")
+    (volume,) = call(
+        third_kernel, "volume_third", [(cube, F32)], [VMEM] * 4, (1_000_000_000, 6_000_000), flux,
+    )(fast, state, volume, jnp.asarray(mix))
     steady, rate = call(
-        lift_kernel, "lift", [(cube, F32)] * 2, [VMEM] * 7 + [SMEM], (1_500_000_000, 6_000_000)
-    )(fast, corrections, mortars, faces, volume, register, metric, counts)
+        lift_kernel, "lift", [(cube, F32)] * 2, [VMEM] * 7, (1_500_000_000, 6_000_000)
+    )(fast, corrections, mortars, faces, volume, register, scale)
     return tuple(
         call(
             functools.partial(finish_kernel, devices), "finish", [(cube, F32)] * 2,
-            [VMEM] * 11 + [SMEM], (200_000_000, 6_000_000),
-        )(steady, rate, state, *returned, fast, sends, metric, counts)
+            [VMEM] * 10, (200_000_000, 6_000_000),
+            [pltpu.VMEM(cube, F32)] * 2 + [pltpu.SemaphoreType.DMA((10,))], [HBM] * 2,
+        )(steady, rate, state, chip, pair, onward, far, fast, sends, scale)
     )
 
 

time: 52.2 us -> 46.1 us (0.88)
  starting transfers between devices: 23.7 us -> 19.3 us
  Pallas kernels: 13.2 us -> 12.1 us
  local copies, waits for them, and re-layouts: 2.05 us -> 1.48 us
    ppermute x14 -> x11, starting transfers between devices: 23.7 us -> 19.3 us  [exchange(): return lax.ppermute(value, 'sfc', pairs[name])]
    pallas_call x1, Pallas kernels: 2.78 us -> 2.1 us  [per_device(): call(functools.partial(face_kernel, devices), 'faces', [((2 * ROWS, 512),...]
    unnamed x22 -> x20, local copies, waits for them, and re-layouts: 2.05 us -> 1.48 us
    pallas_call x4 -> x8, Pallas kernels: 6.28 us -> 6 us  [the longest x1 2.06 us: per_device(): call(lift_kernel, 'lift', [(cube, F32)] * 2, [VMEM] * 7, (1500000000, 600...]
    ppermute x14 -> x11, waiting for transfers between devices: 11.5 us -> 11.6 us  [exchange(): return lax.ppermute(value, 'sfc', pairs[name])]
  transfers between devices with their start and end apart: 14 -> 11, of which waited for: 4 -> 6; matrix products, arithmetic and copies ran while one was open for 0% -> 0% of each run, Pallas kernels for 17% -> 18%
where the time goes in v3:
time: 46.1 us; the launch traced here: 45.9 us
  starting transfers between devices  19.3 us (42%)
  Pallas kernels  12.1 us (26%)
  waiting for transfers between devices  11.6 us (25%)
  local copies, waits for them, and re-layouts  1.48 us (3%)
  between operations  1.45 us (3%)
    ppermute x11, starting transfers between devices, exchange(): return lax.ppermute(value, 'sfc', pairs[name])  19.3 us
    ppermute x11, waiting for transfers between devices, exchange(): return lax.ppermute(value, 'sfc', pairs[name])  11.6 us
    pallas_call x1, Pallas kernels, per_device(): call(functools.partial(finish_kernel, devices), 'finish', [(cube, F32)] *...  2.33 us
    pallas_call x1, Pallas kernels, per_device(): call(functools.partial(face_kernel, devices), 'faces', [((2 * ROWS, 512),...  2.1 us
    pallas_call x1, Pallas kernels, per_device(): call(lift_kernel, 'lift', [(cube, F32)] * 2, [VMEM] * 7, (1500000000, 600...  2.06 us
    pallas_call x1, Pallas kernels, per_device(): call(third_kernel, 'volume_third', [(cube, F32)], [VMEM] * 4, (1000000000...  1.61 us
    unnamed x20, local copies, waits for them, and re-layouts  1.48 us
    pallas_call x1, Pallas kernels, per_device(): call(gather_kernel, 'gather', [((ROWS + 16, 512), F32)], [VMEM] * 3, (100...  1.01 us
  transfers between devices with their start and end apart: 11, of which 6 were waited for; matrix products, arithmetic and copies ran while one was open for 0% of the time, Pallas kernels for 18%

profile of v3, /device:TPU:0, one launch (start us, length us, event | category | flops | bytes accessed | tf_op | source)
XLA Modules:
  0.0 45.9 jit_solution(5292574111790437756)
XLA Ops:
  1.3 0.0 copy-start
  1.3 1.3 %copy-done = f32[5,512,128]{2,1,0:T(8,128)S(1)} copy-done((f32[5,512,128]{2,1,0:T(8,128)S(1)}, f32[5,512,128]{2,1,0:T(8,128)}, u32[]{:S(2)}) %copy-start) | copy-done | bytes 1310744
  2.6 0.5 %table.1 = (bf16[976,768]{1,0:T(8,128)(2,1)S(1)}, f32[8,128]{1,0:T(8,128)S(1)}) custom-call(f32[5,512,128]{2,1,0:T(8,128)S(1)} %copy-done), custom_call_target="tpu_custom_call" | custom-call | flops 100000000 | bytes 3000000 | tf_op jit(solution)/shard_map/table/pallas_call | solution.py:504
  3.2 0.1 copy-done.3
  3.3 0.8 %send.1 = (f32[32,384]{1,0:T(8,128)S(1)}, f32[48,384]{1,0:T(8,128)S(1)}, f32[8,128]{1,0:T(8,128)S(1)}, f32[8,128]{1,0:T(8,128)S(1)}) custom-call(bf16[976,768]{1,0:T(8,128)(2,1)S(1)} %get-tuple-element.22.split_ref, f32[8,128]{1,0:T(8,128)S(1)} %get-tuple-element.23.speed_ref, s32[1]{0:T(128)S(6)} %copy.12.count_ref, s32[16,128]{1,0:T(8,128)S(1)} %bitcast.4, ...), custom_call_target="tpu_custom_call" | custom-call | flops 200000000 | bytes 2000000 | tf_op jit(solution)/shard_map/send/pallas_call | solution.py:507
  4.1 0.1 collective-permute-start
  4.2 1.2 %collective-permute-done.chip_ref.i0 = f32[32,384]{1,0:T(8,128)S(1)} collective-permute-done((f32[32,384]{1,0:T(8,128)S(1)}, f32[32,384]{1,0:T(8,128)S(1)}, u32[]{:S(2)}, u32[]{:S(2)}) %collective-permute-start) | collective-permute-done | bytes 49184 | tf_op jit(solution)/shard_map/ppermute | solution.py:500
  5.4 1.7 %collective-permute-start.1 = (f32[32,384]{1,0:T(8,128)S(1)}, f32[32,384]{1,0:T(8,128)S(1)}, u32[]{:S(2)}, u32[]{:S(2)}) collective-permute-start(f32[32,384]{1,0:T(8,128)S(1)} %get-tuple-element.27), channel_id=1, source_target_pairs={{0,2},{1,3},{2,0},{3,1},{4,6},{5,7},{6,4},{7,5},{8,10},{9,11},{10,... | collective-permute-start | bytes 147464 | tf_op jit(solution)/shard_map/ppermute | solution.py:500
  7.1 1.0 %gather.1.turn_ref.gather_ref = f32[336,512]{1,0:T(8,128)S(1)} custom-call(bf16[976,768]{1,0:T(8,128)(2,1)S(1)} %get-tuple-element.22.split_ref, s32[5,32]{1,0:T(8,128)S(1)} %bitcast.7, s32[2,128]{1,0:T(2,128)S(1)} %bitcast.10), custom_call_target="tpu_custom_call" | custom-call | flops 1000000000 | bytes 2000000 | tf_op jit(solution)/shard_map/gather/pallas_call | solution.py:515
  8.1 1.5 %collective-permute-done.1.pair_ref.i2 = f32[32,384]{1,0:T(8,128)S(1)} collective-permute-done((f32[32,384]{1,0:T(8,128)S(1)}, f32[32,384]{1,0:T(8,128)S(1)}, u32[]{:S(2)}, u32[]{:S(2)}) %collective-permute-start.1) | collective-permute-done | bytes 49184 | tf_op jit(solution)/shard_map/ppermute | solution.py:500
  9.6 4.0 %collective-permute-start.2 = (f32[16,384]{1,0:T(8,128)S(1)}, f32[16,384]{1,0:T(8,128)S(1)}, u32[]{:S(2)}, u32[]{:S(2)}) collective-permute-start(f32[16,384]{1,0:T(8,128)S(1)} %get-tuple-element.30), channel_id=1, source_target_pairs={{0,64},{1,65},{2,66},{3,67},{4,68},{5,69},{6,70},{7,71},{8,72},{9,... | collective-permute-start | bytes 73736 | tf_op jit(solution)/shard_map/ppermute | solution.py:500
  13.6 5.4 %collective-permute-start.6 = (f32[32,384]{1,0:T(8,128)S(1)}, f32[32,384]{1,0:T(8,128)S(1)}, u32[]{:S(2)}, u32[]{:S(2)}) collective-permute-start(f32[32,384]{1,0:T(8,128)S(1)} %get-tuple-element.31), channel_id=1, source_target_pairs={{0,126},{1,127},{2,4},{3,5},{4,2},{5,3},{6,8},{7,9},{8,6},{9,7},{1... | collective-permute-start | bytes 147464 | tf_op jit(solution)/shard_map/ppermute | solution.py:500
  18.9 0.0 collective-permute-done.2.i4
  18.9 0.1 collective-permute-start.3
  19.0 0.8 %volume_first.1.before_ref = f32[5,512,128]{2,1,0:T(8,128)S(1)} custom-call(f32[8,128]{1,0:T(8,128)S(1)} %slice_maximum_fusion.turn_ref, f32[5,512,128]{2,1,0:T(8,128)S(1)} %copy-done.1), custom_call_target="tpu_custom_call" | custom-call | flops 1000000000 | bytes 2600000 | tf_op jit(solution)/shard_map/volume_first/pallas_call | solution.py:522
  19.9 2.8 %collective-permute-done.3 = f32[8,128]{1,0:T(8,128)S(1)} collective-permute-done((f32[8,128]{1,0:T(8,128)S(1)}, f32[8,128]{1,0:T(8,128)S(1)}, u32[]{:S(2)}, u32[]{:S(2)}) %collective-permute-start.3) | collective-permute-done | bytes 4128 | tf_op jit(solution)/shard_map/ppermute | solution.py:500
  22.6 0.6 %collective-permute-start.4 = (f32[8,128]{1,0:T(8,128)S(1)}, f32[8,128]{1,0:T(8,128)S(1)}, u32[]{:S(2)}, u32[]{:S(2)}) collective-permute-start(f32[8,128]{1,0:T(8,128)S(1)} %max.10.turn_ref), channel_id=1, source_target_pairs={{0,24},{1,25},{2,26},{3,27},{4,28},{5,29},{6,30},{7,31},{8,16},{9,... | collective-permute-start | bytes 12296 | tf_op jit(solution)/shard_map/ppermute | solution.py:500
  23.2 0.0 collective-permute-done.6.i3
  23.2 2.1 %faces.1 = (f32[640,512]{1,0:T(8,128)S(1)}, f32[32,640]{1,0:T(8,128)S(1)}, f32[48,640]{1,0:T(8,128)S(1)}) custom-call(f32[8,128]{1,0:T(8,128)S(1)} %max.10.turn_ref, f32[336,512]{1,0:T(8,128)S(1)} %gather.1.turn_ref.gather_ref, f32[32,384]{1,0:T(8,128)S(1)} %collective-permute-done.chip_ref.i0, f32[32,384]{1,0:T(8,128)S(1)} %collective-permute-done.1.pair_ref.i2, ...), custom_call_target="tpu_custom_call" | custom-call | flops 1000000000 | bytes 3000000 | tf_op jit(solution)/shard_map/faces/pallas_call | solution.py:528
  25.3 0.1 collective-permute-start.7
  25.4 2.0 %collective-permute-done.4 = f32[8,128]{1,0:T(8,128)S(1)} collective-permute-done((f32[8,128]{1,0:T(8,128)S(1)}, f32[8,128]{1,0:T(8,128)S(1)}, u32[]{:S(2)}, u32[]{:S(2)}) %collective-permute-start.4) | collective-permute-done | bytes 4128 | tf_op jit(solution)/shard_map/ppermute | solution.py:500
  27.4 1.3 %collective-permute-start.5 = (f32[8,128]{1,0:T(8,128)S(1)}, f32[8,128]{1,0:T(8,128)S(1)}, u32[]{:S(2)}, u32[]{:S(2)}) collective-permute-start(f32[8,128]{1,0:T(8,128)S(1)} %max.11.turn_ref), channel_id=1, source_target_pairs={{0,32},{1,33},{2,34},{3,35},{4,36},{5,37},{6,38},{7,39},{8,40},{9,... | collective-permute-start | bytes 12296 | tf_op jit(solution)/shard_map/ppermute | solution.py:500
  28.8 0.9 %volume_second.1.before_ref = f32[5,512,128]{2,1,0:T(8,128)S(1)} custom-call(f32[8,128]{1,0:T(8,128)S(1)} %max.11.turn_ref, f32[5,512,128]{2,1,0:T(8,128)S(1)} %copy-done.1, f32[5,512,128]{2,1,0:T(8,128)S(1)} %volume_first.1.before_ref), custom_call_target="tpu_custom_call" | custom-call | flops 1000000000 | bytes 3900000 | tf_op jit(solution)/shard_map/volume_second/pallas_call | solution.py:536
  29.6 1.4 %collective-permute-done.5.last_ref = f32[8,128]{1,0:T(8,128)S(1)} collective-permute-done((f32[8,128]{1,0:T(8,128)S(1)}, f32[8,128]{1,0:T(8,128)S(1)}, u32[]{:S(2)}, u32[]{:S(2)}) %collective-permute-start.5) | collective-permute-done | bytes 4128 | tf_op jit(solution)/shard_map/ppermute | solution.py:500
  31.0 0.0 collective-permute-done.7.chip_ref.i0
  31.1 2.5 %collective-permute-start.10 = (f32[16,768]{1,0:T(8,128)S(1)}, f32[16,768]{1,0:T(8,128)S(1)}, u32[]{:S(2)}, u32[]{:S(2)}) collective-permute-start(f32[16,768]{1,0:T(8,128)S(1)} %get-tuple-element.41), channel_id=1, source_target_pairs={{0,64},{1,65},{2,66},{3,67},{4,68},{5,69},{6,70},{7,71},{8,72},{9,... | collective-permute-start | bytes 147464 | tf_op jit(solution)/shard_map/ppermute | solution.py:500
  33.5 3.7 %collective-permute-start.9 = (f32[32,768]{1,0:T(8,128)S(1)}, f32[32,768]{1,0:T(8,128)S(1)}, u32[]{:S(2)}, u32[]{:S(2)}) collective-permute-start(f32[32,768]{1,0:T(8,128)S(1)} %get-tuple-element.40), channel_id=1, source_target_pairs={{0,126},{1,127},{2,4},{3,5},{4,2},{5,3},{6,8},{7,9},{8,6},{9,7},{1... | collective-permute-start | bytes 294920 | tf_op jit(solution)/shard_map/ppermute | solution.py:500
  37.2 1.6 %volume_third.1.volume_ref = f32[5,512,128]{2,1,0:T(8,128)S(1)} custom-call(f32[8,128]{1,0:T(8,128)S(1)} %get-tuple-element.34.turn_ref.fast_ref, f32[5,512,128]{2,1,0:T(8,128)S(1)} %copy-done.1, f32[5,512,128]{2,1,0:T(8,128)S(1)} %volume_second.1.before_ref, f32[256,256]{1,0:T(8,128)S(1)} %copy-done.2), custom_call_target="tpu_custom_call" | custom-call | flops 1000000000 | bytes 6000000 | tf_op jit(solution)/shard_map/volume_third/pallas_call | solution.py:548
  38.9 2.1 %lift.1 = (f32[5,512,128]{2,1,0:T(8,128)S(1)}, f32[5,512,128]{2,1,0:T(8,128)S(1)}) custom-call(f32[8,128]{1,0:T(8,128)S(1)} %get-tuple-element.34.turn_ref.fast_ref, f32[640,512]{1,0:T(8,128)S(1)} %get-tuple-element.35.corr_ref, s32[5,32]{1,0:T(8,128)S(1)} %bitcast.9, s32[2,128]{1,0:T(2,128)S(1)} %bitcast.12, f32[5,512,128]{2,1,0:T(8,128)S(1)} %volume_third.1.volume_ref, ...), custom_call_target="tpu_custom_call" | custom-call | flops 1500000000 | bytes 6000000 | tf_op jit(solution)/shard_map/lift/pallas_call | solution.py:551
  40.9 0.0 collective-permute-done.8.i2
  40.9 2.6 %collective-permute-done.9.i3 = f32[32,768]{1,0:T(8,128)S(1)} collective-permute-done((f32[32,768]{1,0:T(8,128)S(1)}, f32[32,768]{1,0:T(8,128)S(1)}, u32[]{:S(2)}, u32[]{:S(2)}) %collective-permute-start.9) | collective-permute-done | bytes 98336 | tf_op jit(solution)/shard_map/ppermute | solution.py:500
  43.6 2.3 %finish.1 = (f32[5,512,128]{2,1,0:T(8,128)}, f32[5,512,128]{2,1,0:T(8,128)}) custom-call(f32[5,512,128]{2,1,0:T(8,128)S(1)} %get-tuple-element.37.steady_ref, f32[5,512,128]{2,1,0:T(8,128)S(1)} %get-tuple-element.38.rate_ref, f32[5,512,128]{2,1,0:T(8,128)S(1)} %copy-done.1, f32[32,640]{1,0:T(8,128)S(1)} %collective-permute-done.7.chip_ref.i0, ...), custom_call_target="tpu_custom_call" | custom-call | flops 200000000 | bytes 6000000 | tf_op jit(solution)/shard_map/finish/pallas_call | solution.py:555
  (25 shorter events, 0.1 us)
Async XLA Ops:
  0.6 2.5 %copy-start.4 = (f32[128]{0:T(128)S(1)}, f32[128]{0:T(128)}, u32[]{:S(2)}) copy-start(f32[128]{0:T(128)} %param.12) | copy-start | bytes 1540
  1.3 1.3 %copy-start = (f32[5,512,128]{2,1,0:T(8,128)S(1)}, f32[5,512,128]{2,1,0:T(8,128)}, u32[]{:S(2)}) copy-start(f32[5,512,128]{2,1,0:T(8,128)} %state_ref.9) | copy-start | bytes 3932164
  2.6 0.7 %copy-start.3 = (s32[128,16]{0,1:T(8,128)S(1)}, s32[128,16]{0,1:T(8,128)}, u32[]{:S(2)}) copy-start(s32[128,16]{0,1:T(8,128)} %param.14) | copy-start | bytes 24580
  2.6 4.4 %copy-start.6 = (s32[32,5]{0,1:T(8,128)S(1)}, s32[32,5]{0,1:T(8,128)}, u32[]{:S(2)}) copy-start(s32[32,5]{0,1:T(8,128)} %param.15) | copy-start | bytes 1924
  2.6 4.4 %copy-start.7 = (s32[128,2]{0,1:T(2,128)S(1)}, s32[128,2]{0,1:T(2,128)}, u32[]{:S(2)}) copy-start(s32[128,2]{0,1:T(2,128)} %param.16) | copy-start | bytes 3076
  4.1 1.3 %collective-permute-start = (f32[32,384]{1,0:T(8,128)S(1)}, f32[32,384]{1,0:T(8,128)S(1)}, u32[]{:S(2)}, u32[]{:S(2)}) collective-permute-start(f32[32,384]{1,0:T(8,128)S(1)} %get-tuple-element.25), channel_id=1, source_target_pairs={{0,1},{1,0},{2,3},{3,2},{4,5},{5,4},{6,7},{7,6},{8,9},{9,8},{10,11... | collective-permute-start | bytes 147464 | tf_op jit(solution)/shard_map/ppermute | solution.py:500
  5.4 4.2 %collective-permute-start.1 = (f32[32,384]{1,0:T(8,128)S(1)}, f32[32,384]{1,0:T(8,128)S(1)}, u32[]{:S(2)}, u32[]{:S(2)}) collective-permute-start(f32[32,384]{1,0:T(8,128)S(1)} %get-tuple-element.27), channel_id=1, source_target_pairs={{0,2},{1,3},{2,0},{3,1},{4,6},{5,7},{6,4},{7,5},{8,10},{9,11},{10,... | collective-permute-start | bytes 147464 | tf_op jit(solution)/shard_map/ppermute | solution.py:500
  7.1 11.9 %copy-start.1 = (f32[5,512,128]{2,1,0:T(8,128)S(1)}, f32[5,512,128]{2,1,0:T(8,128)}, u32[]{:S(2)}) copy-start(f32[5,512,128]{2,1,0:T(8,128)} %state_ref.9) | copy-start | bytes 3932164
  9.6 9.3 %collective-permute-start.2 = (f32[16,384]{1,0:T(8,128)S(1)}, f32[16,384]{1,0:T(8,128)S(1)}, u32[]{:S(2)}, u32[]{:S(2)}) collective-permute-start(f32[16,384]{1,0:T(8,128)S(1)} %get-tuple-element.30), channel_id=1, source_target_pairs={{0,64},{1,65},{2,66},{3,67},{4,68},{5,69},{6,70},{7,71},{8,72},{9,... | collective-permute-start | bytes 73736 | tf_op jit(solution)/shard_map/ppermute | solution.py:500
  13.6 9.7 %collective-permute-start.6 = (f32[32,384]{1,0:T(8,128)S(1)}, f32[32,384]{1,0:T(8,128)S(1)}, u32[]{:S(2)}, u32[]{:S(2)}) collective-permute-start(f32[32,384]{1,0:T(8,128)S(1)} %get-tuple-element.31), channel_id=1, source_target_pairs={{0,126},{1,127},{2,4},{3,5},{4,2},{5,3},{6,8},{7,9},{8,6},{9,7},{1... | collective-permute-start | bytes 147464 | tf_op jit(solution)/shard_map/ppermute | solution.py:500
  18.9 4.3 %copy-start.8 = (bf16[256,256]{1,0:T(8,128)(2,1)S(1)}, bf16[256,256]{1,0:T(8,128)(2,1)}, u32[]{:S(2)}) copy-start(bf16[256,256]{1,0:T(8,128)(2,1)} %constant.7.clone.back_ref) | copy-start | bytes 393220
  18.9 4.3 %copy-start.9 = (bf16[256,256]{1,0:T(8,128)(2,1)S(1)}, bf16[256,256]{1,0:T(8,128)(2,1)}, u32[]{:S(2)}) copy-start(bf16[256,256]{1,0:T(8,128)(2,1)} %constant.6.clone.project_ref) | copy-start | bytes 393220
  18.9 3.7 %collective-permute-start.3 = (f32[8,128]{1,0:T(8,128)S(1)}, f32[8,128]{1,0:T(8,128)S(1)}, u32[]{:S(2)}, u32[]{:S(2)}) collective-permute-start(f32[8,128]{1,0:T(8,128)S(1)} %slice_maximum_fusion.turn_ref), channel_id=1, source_target_pairs={{0,8},{1,9},{2,10},{3,11},{4,12},{5,13},{6,14},{7,15},{8,0},{9,1},... | collective-permute-start | bytes 12296 | tf_op jit(solution)/shard_map/ppermute | solution.py:500
  22.6 4.8 %collective-permute-start.4 = (f32[8,128]{1,0:T(8,128)S(1)}, f32[8,128]{1,0:T(8,128)S(1)}, u32[]{:S(2)}, u32[]{:S(2)}) collective-permute-start(f32[8,128]{1,0:T(8,128)S(1)} %max.10.turn_ref), channel_id=1, source_target_pairs={{0,24},{1,25},{2,26},{3,27},{4,28},{5,29},{6,30},{7,31},{8,16},{9,... | collective-permute-start | bytes 12296 | tf_op jit(solution)/shard_map/ppermute | solution.py:500
  25.3 5.7 %collective-permute-start.7 = (f32[32,640]{1,0:T(8,128)S(1)}, f32[32,640]{1,0:T(8,128)S(1)}, u32[]{:S(2)}, u32[]{:S(2)}) collective-permute-start(f32[32,640]{1,0:T(8,128)S(1)} %get-tuple-element.33), channel_id=1, source_target_pairs={{0,1},{1,0},{2,3},{3,2},{4,5},{5,4},{6,7},{7,6},{8,9},{9,8},{10,11... | collective-permute-start | bytes 245768 | tf_op jit(solution)/shard_map/ppermute | solution.py:500
  27.4 9.8 %copy-start.2 = (f32[256,256]{1,0:T(8,128)S(1)}, f32[256,256]{1,0:T(8,128)}, u32[]{:S(2)}) copy-start(f32[256,256]{1,0:T(8,128)} %constant.8.clone.mix_ref) | copy-start | bytes 786436
  27.4 3.6 %collective-permute-start.5 = (f32[8,128]{1,0:T(8,128)S(1)}, f32[8,128]{1,0:T(8,128)S(1)}, u32[]{:S(2)}, u32[]{:S(2)}) collective-permute-start(f32[8,128]{1,0:T(8,128)S(1)} %max.11.turn_ref), channel_id=1, source_target_pairs={{0,32},{1,33},{2,34},{3,35},{4,36},{5,37},{6,38},{7,39},{8,40},{9,... | collective-permute-start | bytes 12296 | tf_op jit(solution)/shard_map/ppermute | solution.py:500
  31.1 9.8 %collective-permute-start.10 = (f32[16,768]{1,0:T(8,128)S(1)}, f32[16,768]{1,0:T(8,128)S(1)}, u32[]{:S(2)}, u32[]{:S(2)}) collective-permute-start(f32[16,768]{1,0:T(8,128)S(1)} %get-tuple-element.41), channel_id=1, source_target_pairs={{0,64},{1,65},{2,66},{3,67},{4,68},{5,69},{6,70},{7,71},{8,72},{9,... | collective-permute-start | bytes 147464 | tf_op jit(solution)/shard_map/ppermute | solution.py:500
  33.5 7.4 %collective-permute-start.8 = (f32[32,768]{1,0:T(8,128)S(1)}, f32[32,768]{1,0:T(8,128)S(1)}, u32[]{:S(2)}, u32[]{:S(2)}) collective-permute-start(f32[32,768]{1,0:T(8,128)S(1)} %get-tuple-element.39), channel_id=1, source_target_pairs={{0,2},{1,3},{2,0},{3,1},{4,6},{5,7},{6,4},{7,5},{8,10},{9,11},{10,... | collective-permute-start | bytes 294920 | tf_op jit(solution)/shard_map/ppermute | solution.py:500
  33.5 10.0 %collective-permute-start.9 = (f32[32,768]{1,0:T(8,128)S(1)}, f32[32,768]{1,0:T(8,128)S(1)}, u32[]{:S(2)}, u32[]{:S(2)}) collective-permute-start(f32[32,768]{1,0:T(8,128)S(1)} %get-tuple-element.40), channel_id=1, source_target_pairs={{0,126},{1,127},{2,4},{3,5},{4,2},{5,3},{6,8},{7,9},{8,6},{9,7},{1... | collective-permute-start | bytes 294920 | tf_op jit(solution)/shard_map/ppermute | solution.py:500
  37.2 1.6 %copy-start.5 = (f32[5,512,128]{2,1,0:T(8,128)S(1)}, f32[5,512,128]{2,1,0:T(8,128)}, u32[]{:S(2)}) copy-start(f32[5,512,128]{2,1,0:T(8,128)} %register_ref.1) | copy-start | bytes 3932164

commit v4 on v3

--- a/solution.py
+++ b/solution.py
@@ -83,9 +83,9 @@
         pair=np.where(low, index + 2, index - 2) % devices,
         next=np.where(low, index - 2, index + 2) % devices,
         far=(index + devices // 2) % devices,
-        y_first=index ^ 8,
-        y_second=index + 8 * (np.where(y % 2 == 1, y + 1, y - 1) % 4 - y),
-        z_first=index ^ 32,
+        y_first=index ^ 9,
+        y_second=(index + 8 * (np.where(y % 2 == 1, y + 1, y - 1) % 4 - y)) ^ 1,
+        z_first=index ^ 33,
     )
     return {name: [(int(d), int(p)) for d, p in enumerate(side)] for name, side in partners.items()}
 
@@ -210,15 +210,16 @@
 
 
 def send_kernel(
-    devices, split_ref, speed_ref, count_ref, slots_ref, metric_ref, chip_ref, raw_ref, fast_ref, scale_ref
+    devices, split_ref, speed_ref, count_ref, slots_ref, metric_ref, chip_ref, raw_ref, fast_ref, scale_ref, chosen_ref
 ):
     partners = partner_of(lax.axis_index("sfc"), devices)
-    live = iota((8, ELEMS), 1) < count_ref[0]
+    live = iota((8, ELEMS), 1) < count_ref[...]
     scale_ref[...] = jnp.where(live, COURANT * metric_ref[...], 0.0)
     fastest = jnp.max(jnp.where(live, speed_ref[...], 0.0), axis=0, keepdims=True)
     fastest = jnp.max(fastest, axis=1, keepdims=True)
     fast_ref[...] = jnp.broadcast_to(fastest, (8, ELEMS))
     chosen = one_hot(out_columns(slots_ref, partners) == iota((ELEMS, SLOTS), 1))
+    chosen_ref[...] = chosen
     picked = dot_nt(split_ref[...], chosen)
     rows = jnp.concatenate(
         [thirds(picked, ROWS), picked[3 * ROWS : 3 * ROWS + 16], jnp.broadcast_to(fastest, (48, ELEMS))], axis=0
@@ -228,20 +229,21 @@
     raw_ref[...] = message[2 * WIDTH : 5 * WIDTH]
 
 
-def pair_kernel(raw_ref, chip_ref, fast_ref, pair_ref, next_ref, best_ref):
+def relay_kernel(raw_ref, chip_ref, fast_ref, next_ref, far_ref, best_ref):
     best = jnp.maximum(fast_ref[...], chip_ref[0:8, 256:384])
     best_ref[...] = best
-    for k, ref in enumerate((pair_ref, next_ref)):
-        ref[0:WIDTH, :] = raw_ref[k * WIDTH : (k + 1) * WIDTH, :]
-        ref[WIDTH : 2 * WIDTH, :] = chip_ref[WIDTH : 2 * WIDTH, :]
-    pair_ref[0:8, 256:384] = jnp.where(iota((8, ELEMS), 1) < 80, raw_ref[0:8, 256:384], best)
-
-
-def far_kernel(turn_ref, raw_ref, pair_ref, fast_ref, far_ref, best_ref):
-    best = jnp.maximum(fast_ref[...], pair_ref[0:8, 256:384])
-    best_ref[...] = best
+    next_ref[0:WIDTH, :] = raw_ref[WIDTH : 2 * WIDTH, :]
+    next_ref[WIDTH : 2 * WIDTH, :] = chip_ref[WIDTH : 2 * WIDTH, :]
     far_ref[...] = raw_ref[2 * WIDTH : 3 * WIDTH, :]
     far_ref[0:8, 256:384] = jnp.where(iota((8, ELEMS), 1) < 80, raw_ref[2 * WIDTH : 2 * WIDTH + 8, 256:384], best)
+
+
+def pair_kernel(turn_ref, raw_ref, chip_ref, far_ref, fast_ref, pair_ref, best_ref):
+    best = jnp.maximum(fast_ref[...], far_ref[0:8, 256:384])
+    best_ref[...] = best
+    pair_ref[0:WIDTH, :] = raw_ref[0:WIDTH, :]
+    pair_ref[WIDTH : 2 * WIDTH, :] = chip_ref[WIDTH : 2 * WIDTH, :]
+    pair_ref[0:8, 256:384] = jnp.where(iota((8, ELEMS), 1) < 80, raw_ref[0:8, 256:384], best)
 
 
 def gather_blocks(devices, chip_ref, pair_ref, next_ref, far_ref, columns):
@@ -403,10 +405,10 @@
     best_ref[...] = best
     pair_ref[0:WIDTH, 0 : 2 * ROWS] = raw_ref[0:WIDTH, :]
     next_ref[0:WIDTH, 0 : 2 * ROWS] = raw_ref[WIDTH : 2 * WIDTH, :]
-    far_ref[:, 0 : 2 * ROWS] = raw_ref[2 * WIDTH : 3 * WIDTH, :]
+    far_ref[...] = raw_ref[2 * WIDTH : 3 * WIDTH, :]
     for ref in (pair_ref, next_ref):
         ref[WIDTH : 2 * WIDTH, 0 : 2 * ROWS] = chip_ref[WIDTH : 2 * WIDTH, :]
-    for ref in (pair_ref, next_ref, far_ref):
+    for ref in (pair_ref, next_ref):
         for k in range(ref.shape[0] // 8):
             ref[8 * k : 8 * k + 8, 2 * ROWS :] = best
 
@@ -431,19 +433,23 @@
             )
 
 
+def lift_rows(parts, lift):
+    total = parts[0:64] + parts[64:128]
+    return [lift * total[:, face * ELEMS : (face + 1) * ELEMS] for face in range(6)]
+
+
 def finish_kernel(
-    devices, steady_ref, rate_ref, state_ref, i0, i2, i3, i4, fast_ref, slots_ref, scale_ref,
+    devices, steady_ref, rate_ref, state_ref, i0, i3, i4, i2, fast_ref, chosen_ref, scale_ref,
     state_hbm, register_hbm, state_out, register_out, sems
 ):
-    partners = partner_of(lax.axis_index("sfc"), devices)
     fast = fast_ref[...]
-    for ref in (i2, i3, i4):
+    for ref in (i2, i3):
         fast = jnp.maximum(fast, ref[0:8, 2 * ROWS :])
     fast = jnp.where(iota((8, ELEMS), 1) < 80, 0.0, fast)
     lam = jnp.max(jnp.max(fast, axis=0, keepdims=True), axis=1, keepdims=True)
     inverse = 1.0 / lam
     lift = -LIFT * scale_ref[0:1, :] * inverse
-    chosen = one_hot(out_columns(slots_ref, partners) == iota((ELEMS, SLOTS), 1))
+    chosen = chosen_ref[...]
     arrived = jnp.concatenate(
         [
             block[:, 0:ROWS] + lam * block[:, ROWS : 2 * ROWS]
@@ -452,14 +458,15 @@
         + [jnp.zeros((ELEMS - PEERS * WIDTH, ROWS), F32)],
         axis=0,
     ).T
-    parts = jnp.concatenate(split3(arrived), axis=0)
-    layers = thirds(jnp.dot(parts, chosen, preferred_element_type=F32), ROWS)
+    high, mid = split2(arrived)
     copies = []
     for field in range(5):
+        rows = slice(64 * field, 64 * field + 64)
+        parts = jnp.dot(jnp.concatenate([high[rows], mid[rows]], axis=0), chosen, preferred_element_type=F32)
+        layers = lift_rows(parts, lift)
         register_out[field] = steady_ref[field] + inverse * rate_ref[field]
         for face in range(6):
-            lanes = slice(face * ELEMS, (face + 1) * ELEMS)
-            add_layer(register_out, field, face, lift * layers[64 * field : 64 * field + 64, lanes])
+            add_layer(register_out, field, face, layers[face])
         copies.append(pltpu.make_async_copy(register_out.at[field], register_hbm.at[field], sems.at[2 * field]))
         copies[-1].start()
         state_out[field] = state_ref[field] + SECTION_B * register_out[field]
@@ -470,7 +477,6 @@
 
 
 VMEM = pl.BlockSpec(memory_space=pltpu.VMEM)
-SMEM = pl.BlockSpec(memory_space=pltpu.SMEM)
 HBM = pl.BlockSpec(memory_space=pltpu.HBM)
 
 
@@ -504,20 +510,20 @@
     split, speed = call(
         table_kernel, "table", [((3 * ROWS + 16, SLOTS), BF16), row], [VMEM], (100_000_000, 3_000_000)
     )(state)
-    chip, raw, fast, scale = call(
-        functools.partial(send_kernel, devices), "send", [two, three, row, row], [VMEM] * 2 + [SMEM] + [VMEM] * 2,
+    chip, raw, fast, scale, chosen = call(
+        functools.partial(send_kernel, devices), "send", [two, three, row, row, ((ELEMS, SLOTS), BF16)], [VMEM] * 5,
         (200_000_000, 2_000_000),
-    )(split, speed, counts, sends, metric)
+    )(split, speed, counts.reshape(1, 1), sends, metric)
     chip = exchange(chip, "chip")
-    pair, onward, fast = call(pair_kernel, "pair", [two, two, row], [VMEM] * 3, (0, 200_000))(raw, chip, fast)
+    onward, far, fast = call(relay_kernel, "relay", [two, one, row], [VMEM] * 3, (0, 200_000))(raw, chip, fast)
+    far = exchange(far, "far")
     onward = exchange(onward, "next")
-    pair = exchange(pair, "pair")
     (gathered,) = call(
         gather_kernel, "gather", [((ROWS + 16, 512), F32)], [VMEM] * 3, (1_000_000_000, 2_000_000)
     )(split, mortars, faces)
-    far, fast = call(far_kernel, "far", [one, row], [VMEM] * 4, (0, 200_000))(gathered, raw, pair, fast)
-    far = exchange(far, "far")
-    fast = jnp.maximum(fast, far[0:8, 256:384])
+    pair, fast = call(pair_kernel, "pair", [two, row], [VMEM] * 5, (0, 200_000))(gathered, raw, chip, far, fast)
+    pair = exchange(pair, "pair")
+    fast = jnp.maximum(fast, pair[0:8, 256:384])
     came = exchange(fast, "y_first")
     (volume,) = call(
         functools.partial(first_kernel, deriv), "volume_first", [(cube, F32)], [VMEM] * 2,
@@ -540,7 +546,7 @@
     wide = 2 * ROWS + ELEMS
     pair, onward, far, fast = call(
         reply_kernel, "reply",
-        [((2 * WIDTH, wide), F32)] * 2 + [((WIDTH, wide), F32), row], [VMEM] * 4, (0, 500_000),
+        [((2 * WIDTH, wide), F32)] * 2 + [((WIDTH, 2 * ROWS), F32), row], [VMEM] * 4, (0, 500_000),
     )(fast, came, raw, chip)
     onward = exchange(onward, "next")
     far = exchange(far, "far")
@@ -556,7 +562,7 @@
             functools.partial(finish_kernel, devices), "finish", [(cube, F32)] * 2,
             [VMEM] * 10, (200_000_000, 6_000_000),
             [pltpu.VMEM(cube, F32)] * 2 + [pltpu.SemaphoreType.DMA((10,))], [HBM] * 2,
-        )(steady, rate, state, chip, pair, onward, far, fast, sends, scale)
+        )(steady, rate, state, chip, onward, far, pair, fast, chosen, scale)
     )
 
 

time: 46.1 us -> 43.3 us (0.939)
  waiting for transfers between devices: 11.6 us -> 10.3 us
  starting transfers between devices: 19.3 us -> 18.1 us
    ppermute x11, waiting for transfers between devices: 11.6 us -> 10.3 us  [exchange(): return lax.ppermute(value, 'sfc', pairs[name])]
    ppermute x11, starting transfers between devices: 19.3 us -> 18.1 us  [exchange(): return lax.ppermute(value, 'sfc', pairs[name])]
  transfers between devices with their start and end apart: 11 -> 11, of which waited for: 6 -> 6; matrix products, arithmetic and copies ran while one was open for 0% -> 0% of each run, Pallas kernels for 18% -> 20%
where the time goes in v4:
time: 43.3 us; the launch traced here: 43.1 us
  starting transfers between devices  18.1 us (42%)
  Pallas kernels  11.8 us (27%)
  waiting for transfers between devices  10.3 us (24%)
  local copies, waits for them, and re-layouts  1.48 us (3%)
  between operations  1.46 us (3%)
    ppermute x11, starting transfers between devices, exchange(): return lax.ppermute(value, 'sfc', pairs[name])  18.1 us
    ppermute x11, waiting for transfers between devices, exchange(): return lax.ppermute(value, 'sfc', pairs[name])  10.3 us
    pallas_call x1, Pallas kernels, per_device(): call(functools.partial(face_kernel, devices), 'faces', [((2 * ROWS, 512),...  2.1 us
    pallas_call x1, Pallas kernels, per_device(): call(lift_kernel, 'lift', [(cube, F32)] * 2, [VMEM] * 7, (1500000000, 600...  2.03 us
    pallas_call x1, Pallas kernels, per_device(): call(functools.partial(finish_kernel, devices), 'finish', [(cube, F32)] *...  2.03 us
    pallas_call x1, Pallas kernels, per_device(): call(third_kernel, 'volume_third', [(cube, F32)], [VMEM] * 4, (1000000000...  1.61 us
    unnamed x20, local copies, waits for them, and re-layouts  1.48 us
    pallas_call x1, Pallas kernels, per_device(): call(gather_kernel, 'gather', [((ROWS + 16, 512), F32)], [VMEM] * 3, (100...  1.01 us
  transfers between devices with their start and end apart: 11, of which 6 were waited for; matrix products, arithmetic and copies ran while one was open for 0% of the time, Pallas kernels for 20%

profile of v4, /device:TPU:0, one launch (start us, length us, event | category | flops | bytes accessed | tf_op | source)
XLA Modules:
  0.0 43.1 jit_solution(8076263662958909309)
XLA Ops:
  1.3 0.0 copy-start
  1.3 1.3 %copy-done = f32[5,512,128]{2,1,0:T(8,128)S(1)} copy-done((f32[5,512,128]{2,1,0:T(8,128)S(1)}, f32[5,512,128]{2,1,0:T(8,128)}, u32[]{:S(2)}) %copy-start) | copy-done | bytes 1310744
  2.6 0.5 %table.1 = (bf16[976,768]{1,0:T(8,128)(2,1)S(1)}, f32[8,128]{1,0:T(8,128)S(1)}) custom-call(f32[5,512,128]{2,1,0:T(8,128)S(1)} %copy-done), custom_call_target="tpu_custom_call" | custom-call | flops 100000000 | bytes 3000000 | tf_op jit(solution)/shard_map/table/pallas_call | solution.py:510
  3.2 0.1 copy-done.3
  3.3 0.8 %send.1 = (f32[32,384]{1,0:T(8,128)S(1)}, f32[48,384]{1,0:T(8,128)S(1)}, f32[8,128]{1,0:T(8,128)S(1)}, f32[8,128]{1,0:T(8,128)S(1)}, bf16[128,768]{1,0:T(8,128)(2,1)S(1)}) custom-call(bf16[976,768]{1,0:T(8,128)(2,1)S(1)} %get-tuple-element.23.split_ref, f32[8,128]{1,0:T(8,128)S(1)} %get-tuple-element.24.speed_ref, s32[1,1]{1,0:T(1,128)} %bitcast.5.count_ref, ...), custom_call_target="tpu_custom_call" | custom-call | flops 200000000 | bytes 2000000 | tf_op jit(solution)/shard_map/send/pallas_call | solution.py:513
  4.1 0.1 collective-permute-start
  4.2 1.2 %collective-permute-done.chip_ref.i0 = f32[32,384]{1,0:T(8,128)S(1)} collective-permute-done((f32[32,384]{1,0:T(8,128)S(1)}, f32[32,384]{1,0:T(8,128)S(1)}, u32[]{:S(2)}, u32[]{:S(2)}) %collective-permute-start) | collective-permute-done | bytes 49184 | tf_op jit(solution)/shard_map/ppermute | solution.py:506
  5.4 4.0 %collective-permute-start.1 = (f32[16,384]{1,0:T(8,128)S(1)}, f32[16,384]{1,0:T(8,128)S(1)}, u32[]{:S(2)}, u32[]{:S(2)}) collective-permute-start(f32[16,384]{1,0:T(8,128)S(1)} %get-tuple-element.28), channel_id=1, source_target_pairs={{0,64},{1,65},{2,66},{3,67},{4,68},{5,69},{6,70},{7,71},{8,72},{9,... | collective-permute-start | bytes 73736 | tf_op jit(solution)/shard_map/ppermute | solution.py:506
  9.5 1.0 %gather.1.turn_ref.gather_ref = f32[336,512]{1,0:T(8,128)S(1)} custom-call(bf16[976,768]{1,0:T(8,128)(2,1)S(1)} %get-tuple-element.23.split_ref, s32[5,32]{1,0:T(8,128)S(1)} %bitcast.8, s32[2,128]{1,0:T(2,128)S(1)} %bitcast.11), custom_call_target="tpu_custom_call" | custom-call | flops 1000000000 | bytes 2000000 | tf_op jit(solution)/shard_map/gather/pallas_call | solution.py:521
  10.5 0.8 %collective-permute-done.1.far_ref.i4 = f32[16,384]{1,0:T(8,128)S(1)} collective-permute-done((f32[16,384]{1,0:T(8,128)S(1)}, f32[16,384]{1,0:T(8,128)S(1)}, u32[]{:S(2)}, u32[]{:S(2)}) %collective-permute-start.1) | collective-permute-done | bytes 24608 | tf_op jit(solution)/shard_map/ppermute | solution.py:506
  11.3 1.5 %collective-permute-start.2 = (f32[32,384]{1,0:T(8,128)S(1)}, f32[32,384]{1,0:T(8,128)S(1)}, u32[]{:S(2)}, u32[]{:S(2)}) collective-permute-start(f32[32,384]{1,0:T(8,128)S(1)} %get-tuple-element.31), channel_id=1, source_target_pairs={{0,2},{1,3},{2,0},{3,1},{4,6},{5,7},{6,4},{7,5},{8,10},{9,11},{10,... | collective-permute-start | bytes 147464 | tf_op jit(solution)/shard_map/ppermute | solution.py:506
  12.7 7.7 %collective-permute-start.6 = (f32[32,384]{1,0:T(8,128)S(1)}, f32[32,384]{1,0:T(8,128)S(1)}, u32[]{:S(2)}, u32[]{:S(2)}) collective-permute-start(f32[32,384]{1,0:T(8,128)S(1)} %get-tuple-element.32), channel_id=1, source_target_pairs={{0,126},{1,127},{2,4},{3,5},{4,2},{5,3},{6,8},{7,9},{8,6},{9,7},{1... | collective-permute-start | bytes 147464 | tf_op jit(solution)/shard_map/ppermute | solution.py:506
  20.4 0.0 collective-permute-done.2.i2
  20.4 0.1 collective-permute-start.3
  20.5 0.8 %volume_first.1.before_ref = f32[5,512,128]{2,1,0:T(8,128)S(1)} custom-call(f32[8,128]{1,0:T(8,128)S(1)} %slice_maximum_fusion.turn_ref, f32[5,512,128]{2,1,0:T(8,128)S(1)} %copy-done.1), custom_call_target="tpu_custom_call" | custom-call | flops 1000000000 | bytes 2600000 | tf_op jit(solution)/shard_map/volume_first/pallas_call | solution.py:528
  21.4 2.2 %collective-permute-done.3 = f32[8,128]{1,0:T(8,128)S(1)} collective-permute-done((f32[8,128]{1,0:T(8,128)S(1)}, f32[8,128]{1,0:T(8,128)S(1)}, u32[]{:S(2)}, u32[]{:S(2)}) %collective-permute-start.3) | collective-permute-done | bytes 4128 | tf_op jit(solution)/shard_map/ppermute | solution.py:506
  23.6 0.0 collective-permute-start.4
  23.6 0.0 collective-permute-done.6.i3
  23.6 2.1 %faces.1 = (f32[640,512]{1,0:T(8,128)S(1)}, f32[32,640]{1,0:T(8,128)S(1)}, f32[48,640]{1,0:T(8,128)S(1)}) custom-call(f32[8,128]{1,0:T(8,128)S(1)} %max.10.turn_ref, f32[336,512]{1,0:T(8,128)S(1)} %gather.1.turn_ref.gather_ref, f32[32,384]{1,0:T(8,128)S(1)} %collective-permute-done.chip_ref.i0, f32[32,384]{1,0:T(8,128)S(1)} %collective-permute-done.2.i2, ...), custom_call_target="tpu_custom_call" | custom-call | flops 1000000000 | bytes 3000000 | tf_op jit(solution)/shard_map/faces/pallas_call | solution.py:534
  25.7 0.1 collective-permute-start.7
  25.8 2.0 %collective-permute-done.4 = f32[8,128]{1,0:T(8,128)S(1)} collective-permute-done((f32[8,128]{1,0:T(8,128)S(1)}, f32[8,128]{1,0:T(8,128)S(1)}, u32[]{:S(2)}, u32[]{:S(2)}) %collective-permute-start.4) | collective-permute-done | bytes 4128 | tf_op jit(solution)/shard_map/ppermute | solution.py:506
  27.8 0.0 collective-permute-start.5
  27.8 0.9 %volume_second.1.before_ref = f32[5,512,128]{2,1,0:T(8,128)S(1)} custom-call(f32[8,128]{1,0:T(8,128)S(1)} %max.11.turn_ref, f32[5,512,128]{2,1,0:T(8,128)S(1)} %copy-done.1, f32[5,512,128]{2,1,0:T(8,128)S(1)} %volume_first.1.before_ref), custom_call_target="tpu_custom_call" | custom-call | flops 1000000000 | bytes 3900000 | tf_op jit(solution)/shard_map/volume_second/pallas_call | solution.py:542
  28.7 2.2 %collective-permute-done.5.last_ref = f32[8,128]{1,0:T(8,128)S(1)} collective-permute-done((f32[8,128]{1,0:T(8,128)S(1)}, f32[8,128]{1,0:T(8,128)S(1)}, u32[]{:S(2)}, u32[]{:S(2)}) %collective-permute-start.5) | collective-permute-done | bytes 4128 | tf_op jit(solution)/shard_map/ppermute | solution.py:506
  30.8 0.0 collective-permute-done.7.chip_ref.i0
  30.9 0.1 collective-permute-start.9
  31.0 4.5 %collective-permute-start.8 = (f32[32,768]{1,0:T(8,128)S(1)}, f32[32,768]{1,0:T(8,128)S(1)}, u32[]{:S(2)}, u32[]{:S(2)}) collective-permute-start(f32[32,768]{1,0:T(8,128)S(1)} %get-tuple-element.40), channel_id=1, source_target_pairs={{0,126},{1,127},{2,4},{3,5},{4,2},{5,3},{6,8},{7,9},{8,6},{9,7},{1... | collective-permute-start | bytes 294920 | tf_op jit(solution)/shard_map/ppermute | solution.py:506
  35.5 1.6 %volume_third.1.volume_ref = f32[5,512,128]{2,1,0:T(8,128)S(1)} custom-call(f32[8,128]{1,0:T(8,128)S(1)} %get-tuple-element.35.turn_ref.fast_ref, f32[5,512,128]{2,1,0:T(8,128)S(1)} %copy-done.1, f32[5,512,128]{2,1,0:T(8,128)S(1)} %volume_second.1.before_ref, f32[256,256]{1,0:T(8,128)S(1)} %copy-done.2), custom_call_target="tpu_custom_call" | custom-call | flops 1000000000 | bytes 6000000 | tf_op jit(solution)/shard_map/volume_third/pallas_call | solution.py:554
  37.1 2.0 %lift.1 = (f32[5,512,128]{2,1,0:T(8,128)S(1)}, f32[5,512,128]{2,1,0:T(8,128)S(1)}) custom-call(f32[8,128]{1,0:T(8,128)S(1)} %get-tuple-element.35.turn_ref.fast_ref, f32[640,512]{1,0:T(8,128)S(1)} %get-tuple-element.36.corr_ref, s32[5,32]{1,0:T(8,128)S(1)} %bitcast.10, s32[2,128]{1,0:T(2,128)S(1)} %bitcast.13, f32[5,512,128]{2,1,0:T(8,128)S(1)} %volume_third.1.volume_ref, ...), custom_call_target="tpu_custom_call" | custom-call | flops 1500000000 | bytes 6000000 | tf_op jit(solution)/shard_map/lift/pallas_call | solution.py:557
  39.2 1.9 %collective-permute-done.8.i3 = f32[32,768]{1,0:T(8,128)S(1)} collective-permute-done((f32[32,768]{1,0:T(8,128)S(1)}, f32[32,768]{1,0:T(8,128)S(1)}, u32[]{:S(2)}, u32[]{:S(2)}) %collective-permute-start.8) | collective-permute-done | bytes 98336 | tf_op jit(solution)/shard_map/ppermute | solution.py:506
  41.1 0.0 collective-permute-done.10.i2
  41.1 2.0 %finish.1 = (f32[5,512,128]{2,1,0:T(8,128)}, f32[5,512,128]{2,1,0:T(8,128)}) custom-call(f32[5,512,128]{2,1,0:T(8,128)S(1)} %get-tuple-element.38.steady_ref, f32[5,512,128]{2,1,0:T(8,128)S(1)} %get-tuple-element.39.rate_ref, f32[5,512,128]{2,1,0:T(8,128)S(1)} %copy-done.1, f32[32,640]{1,0:T(8,128)S(1)} %collective-permute-done.7.chip_ref.i0, ...), custom_call_target="tpu_custom_call" | custom-call | flops 200000000 | bytes 6000000 | tf_op jit(solution)/shard_map/finish/pallas_call | solution.py:561
  (25 shorter events, 0.1 us)
Async XLA Ops:
  0.6 2.5 %copy-start.4 = (f32[128]{0:T(128)S(1)}, f32[128]{0:T(128)}, u32[]{:S(2)}) copy-start(f32[128]{0:T(128)} %param.12) | copy-start | bytes 1540
  1.3 1.3 %copy-start = (f32[5,512,128]{2,1,0:T(8,128)S(1)}, f32[5,512,128]{2,1,0:T(8,128)}, u32[]{:S(2)}) copy-start(f32[5,512,128]{2,1,0:T(8,128)} %state_ref.9) | copy-start | bytes 3932164
  2.6 0.7 %copy-start.3 = (s32[128,16]{0,1:T(8,128)S(1)}, s32[128,16]{0,1:T(8,128)}, u32[]{:S(2)}) copy-start(s32[128,16]{0,1:T(8,128)} %param.14) | copy-start | bytes 24580
  2.6 6.8 %copy-start.6 = (s32[32,5]{0,1:T(8,128)S(1)}, s32[32,5]{0,1:T(8,128)}, u32[]{:S(2)}) copy-start(s32[32,5]{0,1:T(8,128)} %param.15) | copy-start | bytes 1924
  2.6 6.8 %copy-start.7 = (s32[128,2]{0,1:T(2,128)S(1)}, s32[128,2]{0,1:T(2,128)}, u32[]{:S(2)}) copy-start(s32[128,2]{0,1:T(2,128)} %param.16) | copy-start | bytes 3076
  4.1 1.3 %collective-permute-start = (f32[32,384]{1,0:T(8,128)S(1)}, f32[32,384]{1,0:T(8,128)S(1)}, u32[]{:S(2)}, u32[]{:S(2)}) collective-permute-start(f32[32,384]{1,0:T(8,128)S(1)} %get-tuple-element.26), channel_id=1, source_target_pairs={{0,1},{1,0},{2,3},{3,2},{4,5},{5,4},{6,7},{7,6},{8,9},{9,8},{10,11... | collective-permute-start | bytes 147464 | tf_op jit(solution)/shard_map/ppermute | solution.py:506
  5.4 5.8 %collective-permute-start.1 = (f32[16,384]{1,0:T(8,128)S(1)}, f32[16,384]{1,0:T(8,128)S(1)}, u32[]{:S(2)}, u32[]{:S(2)}) collective-permute-start(f32[16,384]{1,0:T(8,128)S(1)} %get-tuple-element.28), channel_id=1, source_target_pairs={{0,64},{1,65},{2,66},{3,67},{4,68},{5,69},{6,70},{7,71},{8,72},{9,... | collective-permute-start | bytes 73736 | tf_op jit(solution)/shard_map/ppermute | solution.py:506
  9.5 11.1 %copy-start.1 = (f32[5,512,128]{2,1,0:T(8,128)S(1)}, f32[5,512,128]{2,1,0:T(8,128)}, u32[]{:S(2)}) copy-start(f32[5,512,128]{2,1,0:T(8,128)} %state_ref.9) | copy-start | bytes 3932164
  11.3 9.2 %collective-permute-start.2 = (f32[32,384]{1,0:T(8,128)S(1)}, f32[32,384]{1,0:T(8,128)S(1)}, u32[]{:S(2)}, u32[]{:S(2)}) collective-permute-start(f32[32,384]{1,0:T(8,128)S(1)} %get-tuple-element.31), channel_id=1, source_target_pairs={{0,2},{1,3},{2,0},{3,1},{4,6},{5,7},{6,4},{7,5},{8,10},{9,11},{10,... | collective-permute-start | bytes 147464 | tf_op jit(solution)/shard_map/ppermute | solution.py:506
  12.7 10.8 %collective-permute-start.6 = (f32[32,384]{1,0:T(8,128)S(1)}, f32[32,384]{1,0:T(8,128)S(1)}, u32[]{:S(2)}, u32[]{:S(2)}) collective-permute-start(f32[32,384]{1,0:T(8,128)S(1)} %get-tuple-element.32), channel_id=1, source_target_pairs={{0,126},{1,127},{2,4},{3,5},{4,2},{5,3},{6,8},{7,9},{8,6},{9,7},{1... | collective-permute-start | bytes 147464 | tf_op jit(solution)/shard_map/ppermute | solution.py:506
  20.4 3.1 %copy-start.8 = (bf16[256,256]{1,0:T(8,128)(2,1)S(1)}, bf16[256,256]{1,0:T(8,128)(2,1)}, u32[]{:S(2)}) copy-start(bf16[256,256]{1,0:T(8,128)(2,1)} %constant.7.clone.back_ref) | copy-start | bytes 393220
  20.4 3.1 %copy-start.9 = (bf16[256,256]{1,0:T(8,128)(2,1)S(1)}, bf16[256,256]{1,0:T(8,128)(2,1)}, u32[]{:S(2)}) copy-start(bf16[256,256]{1,0:T(8,128)(2,1)} %constant.6.clone.project_ref) | copy-start | bytes 393220
  20.4 3.1 %collective-permute-start.3 = (f32[8,128]{1,0:T(8,128)S(1)}, f32[8,128]{1,0:T(8,128)S(1)}, u32[]{:S(2)}, u32[]{:S(2)}) collective-permute-start(f32[8,128]{1,0:T(8,128)S(1)} %slice_maximum_fusion.turn_ref), channel_id=1, source_target_pairs={{0,9},{1,8},{2,11},{3,10},{4,13},{5,12},{6,15},{7,14},{8,1},{9,0},... | collective-permute-start | bytes 12296 | tf_op jit(solution)/shard_map/ppermute | solution.py:506
  23.6 4.2 %collective-permute-start.4 = (f32[8,128]{1,0:T(8,128)S(1)}, f32[8,128]{1,0:T(8,128)S(1)}, u32[]{:S(2)}, u32[]{:S(2)}) collective-permute-start(f32[8,128]{1,0:T(8,128)S(1)} %max.10.turn_ref), channel_id=1, source_target_pairs={{0,25},{1,24},{2,27},{3,26},{4,29},{5,28},{6,31},{7,30},{8,17},{9,... | collective-permute-start | bytes 12296 | tf_op jit(solution)/shard_map/ppermute | solution.py:506
  25.7 5.2 %collective-permute-start.7 = (f32[32,640]{1,0:T(8,128)S(1)}, f32[32,640]{1,0:T(8,128)S(1)}, u32[]{:S(2)}, u32[]{:S(2)}) collective-permute-start(f32[32,640]{1,0:T(8,128)S(1)} %get-tuple-element.34), channel_id=1, source_target_pairs={{0,1},{1,0},{2,3},{3,2},{4,5},{5,4},{6,7},{7,6},{8,9},{9,8},{10,11... | collective-permute-start | bytes 245768 | tf_op jit(solution)/shard_map/ppermute | solution.py:506
  27.8 7.7 %copy-start.2 = (f32[256,256]{1,0:T(8,128)S(1)}, f32[256,256]{1,0:T(8,128)}, u32[]{:S(2)}) copy-start(f32[256,256]{1,0:T(8,128)} %constant.8.clone.mix_ref) | copy-start | bytes 786436
  27.8 3.0 %collective-permute-start.5 = (f32[8,128]{1,0:T(8,128)S(1)}, f32[8,128]{1,0:T(8,128)S(1)}, u32[]{:S(2)}, u32[]{:S(2)}) collective-permute-start(f32[8,128]{1,0:T(8,128)S(1)} %max.11.turn_ref), channel_id=1, source_target_pairs={{0,33},{1,32},{2,35},{3,34},{4,37},{5,36},{6,39},{7,38},{8,41},{9,... | collective-permute-start | bytes 12296 | tf_op jit(solution)/shard_map/ppermute | solution.py:506
  30.9 8.3 %collective-permute-start.9 = (f32[16,640]{1,0:T(8,128)S(1)}, f32[16,640]{1,0:T(8,128)S(1)}, u32[]{:S(2)}, u32[]{:S(2)}) collective-permute-start(f32[16,640]{1,0:T(8,128)S(1)} %get-tuple-element.41), channel_id=1, source_target_pairs={{0,64},{1,65},{2,66},{3,67},{4,68},{5,69},{6,70},{7,71},{8,72},{9,... | collective-permute-start | bytes 122888 | tf_op jit(solution)/shard_map/ppermute | solution.py:506
  31.0 10.1 %collective-permute-start.8 = (f32[32,768]{1,0:T(8,128)S(1)}, f32[32,768]{1,0:T(8,128)S(1)}, u32[]{:S(2)}, u32[]{:S(2)}) collective-permute-start(f32[32,768]{1,0:T(8,128)S(1)} %get-tuple-element.40), channel_id=1, source_target_pairs={{0,126},{1,127},{2,4},{3,5},{4,2},{5,3},{6,8},{7,9},{8,6},{9,7},{1... | collective-permute-start | bytes 294920 | tf_op jit(solution)/shard_map/ppermute | solution.py:506
  35.5 5.6 %collective-permute-start.10 = (f32[32,768]{1,0:T(8,128)S(1)}, f32[32,768]{1,0:T(8,128)S(1)}, u32[]{:S(2)}, u32[]{:S(2)}) collective-permute-start(f32[32,768]{1,0:T(8,128)S(1)} %get-tuple-element.42), channel_id=1, source_target_pairs={{0,2},{1,3},{2,0},{3,1},{4,6},{5,7},{6,4},{7,5},{8,10},{9,11},{10,... | collective-permute-start | bytes 294920 | tf_op jit(solution)/shard_map/ppermute | solution.py:506
  35.5 1.6 %copy-start.5 = (f32[5,512,128]{2,1,0:T(8,128)S(1)}, f32[5,512,128]{2,1,0:T(8,128)}, u32[]{:S(2)}) copy-start(f32[5,512,128]{2,1,0:T(8,128)} %register_ref.1) | copy-start | bytes 3932164

commit v5 on v4

--- a/solution.py
+++ b/solution.py
@@ -97,14 +97,6 @@
     return [lax.rem(me + step + devices, devices) for step in steps]
 
 
-def split3(value):
-    high = value.astype(BF16)
-    rest = value - high.astype(F32)
-    mid = rest.astype(BF16)
-    low = (rest - mid.astype(F32)).astype(BF16)
-    return high, mid, low
-
-
 def split2(value):
     high = value.astype(BF16)
     return high, (value - high.astype(F32)).astype(BF16)
@@ -128,8 +120,8 @@
     return jnp.where(mask, F32(1.0), F32(0.0)).astype(BF16)
 
 
-def thirds(value, size):
-    return value[:size] + value[size : 2 * size] + value[2 * size : 3 * size]
+def halves(value, size):
+    return value[:size] + value[size : 2 * size]
 
 
 def face_layer(ref, field, face):
@@ -200,13 +192,13 @@
     for face in range(6):
         lanes = slice(face * ELEMS, (face + 1) * ELEMS)
         for field in range(5):
-            parts = split3(face_layer(state_ref, field, face))
-            for term in range(3):
+            parts = split2(face_layer(state_ref, field, face))
+            for term in range(2):
                 split_ref[term * ROWS + field * 64 : term * ROWS + field * 64 + 64, lanes] = parts[term]
     row = iota((16, SLOTS), 0)
     face = iota((16, SLOTS), 1) // ELEMS
     sign = jnp.where(face % 2 == 1, F32(1.0), F32(-1.0))
-    split_ref[3 * ROWS : 3 * ROWS + 16, :] = jnp.where(row == face // 2, sign, 0.0).astype(BF16)
+    split_ref[2 * ROWS : 2 * ROWS + 16, :] = jnp.where(row == face // 2, sign, 0.0).astype(BF16)
 
 
 def send_kernel(
@@ -222,7 +214,7 @@
     chosen_ref[...] = chosen
     picked = dot_nt(split_ref[...], chosen)
     rows = jnp.concatenate(
-        [thirds(picked, ROWS), picked[3 * ROWS : 3 * ROWS + 16], jnp.broadcast_to(fastest, (48, ELEMS))], axis=0
+        [halves(picked, ROWS), picked[2 * ROWS : 2 * ROWS + 16], jnp.broadcast_to(fastest, (48, ELEMS))], axis=0
     )
     message = rows.T
     chip_ref[...] = message[0 : 2 * WIDTH]
@@ -303,8 +295,8 @@
 
 def gather_kernel(split_ref, mortar_ref, face_ref, gather_ref):
     picked = jnp.dot(split_ref[...], own_choice(mortar_ref, face_ref), preferred_element_type=F32)
-    gather_ref[0:ROWS, :] = thirds(picked, ROWS)
-    gather_ref[ROWS : ROWS + 16, :] = picked[3 * ROWS : 3 * ROWS + 16]
+    gather_ref[0:ROWS, :] = halves(picked, ROWS)
+    gather_ref[ROWS : ROWS + 16, :] = picked[2 * ROWS : 2 * ROWS + 16]
 
 
 def third_kernel(turn_ref, state_ref, before_ref, mix_ref, volume_ref, flux):
@@ -363,14 +355,14 @@
     arrived = jnp.concatenate(
         incoming + [jnp.zeros((ELEMS - PEERS * WIDTH, 384), F32)], axis=0
     ).T
-    high, mid, low = split3(arrived[:ROWS])
+    high, mid = split2(arrived[:ROWS])
     picked = jnp.dot(
-        jnp.concatenate([high, mid, low, arrived[ROWS : ROWS + 16].astype(BF16)], axis=0),
+        jnp.concatenate([high, mid, arrived[ROWS : ROWS + 16].astype(BF16)], axis=0),
         remote,
         preferred_element_type=F32,
     )
-    pool_ref[0:ROWS, :] = gather_ref[0:ROWS, :] + thirds(picked, ROWS)
-    normals = gather_ref[ROWS : ROWS + 8, :] + picked[3 * ROWS : 3 * ROWS + 8]
+    pool_ref[0:ROWS, :] = gather_ref[0:ROWS, :] + halves(picked, ROWS)
+    normals = gather_ref[ROWS : ROWS + 8, :] + picked[2 * ROWS : 2 * ROWS + 8]
     sides = []
     for side in range(4):
         lanes = slice(side * ELEMS, (side + 1) * ELEMS)
@@ -395,7 +387,7 @@
         corr_ref[more, 128:256] = jump
         corr_ref[rows, 384:512] = -even - right_f[k]
         corr_ref[more, 384:512] = -jump
-    back = sum(dot_nt(part, remote) for part in split3(corr_ref[...])).T
+    back = sum(dot_nt(part, remote) for part in split2(corr_ref[...])).T
     chip_ref[...] = back[0 : 2 * WIDTH]
     raw_ref[...] = back[2 * WIDTH : 5 * WIDTH]
 
@@ -421,7 +413,7 @@
     for field in range(5):
         steady_ref[field] = SECTION_A * register_ref[field]
         rate_ref[field] = -scale * volume_ref[field]
-    parts = split3(corr_ref[...])
+    parts = split2(corr_ref[...])
     layers = sum(dot_nt(part, chosen) for part in parts)
     lift = -LIFT * scale
     for face in range(6):
@@ -508,7 +500,7 @@
     one, two, three = [((k * WIDTH, 384), F32) for k in (1, 2, 3)]
     row = ((8, ELEMS), F32)
     split, speed = call(
-        table_kernel, "table", [((3 * ROWS + 16, SLOTS), BF16), row], [VMEM], (100_000_000, 3_000_000)
+        table_kernel, "table", [((2 * ROWS + 16, SLOTS), BF16), row], [VMEM], (100_000_000, 3_000_000)
     )(state)
     chip, raw, fast, scale, chosen = call(
         functools.partial(send_kernel, devices), "send", [two, three, row, row, ((ELEMS, SLOTS), BF16)], [VMEM] * 5,

time: 43.3 us -> 43.2 us (level)
  waiting for transfers between devices: 10.3 us -> 12.3 us
  Pallas kernels: 11.8 us -> 10.2 us
  starting transfers between devices: 18.1 us -> 17.5 us
    ppermute x11, waiting for transfers between devices: 10.3 us -> 12.3 us  [exchange(): return lax.ppermute(value, 'sfc', pairs[name])]
    pallas_call x1, Pallas kernels: 2.1 us -> 1.49 us  [per_device(): call(functools.partial(face_kernel, devices), 'faces', [((2 * ROWS, 512),...]
    ppermute x11, starting transfers between devices: 18.1 us -> 17.5 us  [exchange(): return lax.ppermute(value, 'sfc', pairs[name])]
    pallas_call x1, Pallas kernels: 2.03 us -> 1.48 us  [per_device(): call(lift_kernel, 'lift', [(cube, F32)] * 2, [VMEM] * 7, (1500000000, 600...]
  transfers between devices with their start and end apart: 11 -> 11, of which waited for: 6 -> 6; matrix products, arithmetic and copies ran while one was open for 0% -> 0% of each run, Pallas kernels for 20% -> 16%
where the time goes in v5:
time: 43.2 us; the launch traced here: 43 us
  starting transfers between devices  17.5 us (41%)
  waiting for transfers between devices  12.3 us (28%)
  Pallas kernels  10.2 us (24%)
  local copies, waits for them, and re-layouts  1.58 us (4%)
  between operations  1.48 us (3%)
    ppermute x11, starting transfers between devices, exchange(): return lax.ppermute(value, 'sfc', pairs[name])  17.5 us
    ppermute x11, waiting for transfers between devices, exchange(): return lax.ppermute(value, 'sfc', pairs[name])  12.3 us
    pallas_call x1, Pallas kernels, per_device(): call(functools.partial(finish_kernel, devices), 'finish', [(cube, F32)] *...  2.03 us
    pallas_call x1, Pallas kernels, per_device(): call(third_kernel, 'volume_third', [(cube, F32)], [VMEM] * 4, (1000000000...  1.61 us
    unnamed x20, local copies, waits for them, and re-layouts  1.58 us
    pallas_call x1, Pallas kernels, per_device(): call(functools.partial(face_kernel, devices), 'faces', [((2 * ROWS, 512),...  1.49 us
    pallas_call x1, Pallas kernels, per_device(): call(lift_kernel, 'lift', [(cube, F32)] * 2, [VMEM] * 7, (1500000000, 600...  1.48 us
    pallas_call x1, Pallas kernels, per_device(): call(functools.partial(second_kernel, deriv), 'volume_second', [(cube, F3...  0.87 us
  transfers between devices with their start and end apart: 11, of which 6 were waited for; matrix products, arithmetic and copies ran while one was open for 0% of the time, Pallas kernels for 16%

profile of v5, /device:TPU:0, one launch (start us, length us, event | category | flops | bytes accessed | tf_op | source)
XLA Modules:
  0.0 43.0 jit_solution(4457397837355210372)
XLA Ops:
  1.3 0.0 copy-start
  1.3 1.3 %copy-done = f32[5,512,128]{2,1,0:T(8,128)S(1)} copy-done((f32[5,512,128]{2,1,0:T(8,128)S(1)}, f32[5,512,128]{2,1,0:T(8,128)}, u32[]{:S(2)}) %copy-start) | copy-done | bytes 1310744
  2.6 0.4 %table.1 = (bf16[656,768]{1,0:T(8,128)(2,1)S(1)}, f32[8,128]{1,0:T(8,128)S(1)}) custom-call(f32[5,512,128]{2,1,0:T(8,128)S(1)} %copy-done), custom_call_target="tpu_custom_call" | custom-call | flops 100000000 | bytes 3000000 | tf_op jit(solution)/shard_map/table/pallas_call | solution.py:502
  3.1 0.2 copy-done.3
  3.3 0.6 %send.1 = (f32[32,384]{1,0:T(8,128)S(1)}, f32[48,384]{1,0:T(8,128)S(1)}, f32[8,128]{1,0:T(8,128)S(1)}, f32[8,128]{1,0:T(8,128)S(1)}, bf16[128,768]{1,0:T(8,128)(2,1)S(1)}) custom-call(bf16[656,768]{1,0:T(8,128)(2,1)S(1)} %get-tuple-element.23.split_ref, f32[8,128]{1,0:T(8,128)S(1)} %get-tuple-element.24.speed_ref, s32[1,1]{1,0:T(1,128)} %bitcast.5.count_ref, ...), custom_call_target="tpu_custom_call" | custom-call | flops 200000000 | bytes 2000000 | tf_op jit(solution)/shard_map/send/pallas_call | solution.py:505
  4.0 0.1 collective-permute-start
  4.1 1.2 %collective-permute-done.chip_ref.i0 = f32[32,384]{1,0:T(8,128)S(1)} collective-permute-done((f32[32,384]{1,0:T(8,128)S(1)}, f32[32,384]{1,0:T(8,128)S(1)}, u32[]{:S(2)}, u32[]{:S(2)}) %collective-permute-start) | collective-permute-done | bytes 49184 | tf_op jit(solution)/shard_map/ppermute | solution.py:498
  5.3 4.0 %collective-permute-start.1 = (f32[16,384]{1,0:T(8,128)S(1)}, f32[16,384]{1,0:T(8,128)S(1)}, u32[]{:S(2)}, u32[]{:S(2)}) collective-permute-start(f32[16,384]{1,0:T(8,128)S(1)} %get-tuple-element.28), channel_id=1, source_target_pairs={{0,64},{1,65},{2,66},{3,67},{4,68},{5,69},{6,70},{7,71},{8,72},{9,... | collective-permute-start | bytes 73736 | tf_op jit(solution)/shard_map/ppermute | solution.py:498
  9.3 0.8 %gather.1.turn_ref.gather_ref = f32[336,512]{1,0:T(8,128)S(1)} custom-call(bf16[656,768]{1,0:T(8,128)(2,1)S(1)} %get-tuple-element.23.split_ref, s32[5,32]{1,0:T(8,128)S(1)} %bitcast.8, s32[2,128]{1,0:T(2,128)S(1)} %bitcast.11), custom_call_target="tpu_custom_call" | custom-call | flops 1000000000 | bytes 2000000 | tf_op jit(solution)/shard_map/gather/pallas_call | solution.py:513
  10.1 1.0 %collective-permute-done.1.far_ref.i4 = f32[16,384]{1,0:T(8,128)S(1)} collective-permute-done((f32[16,384]{1,0:T(8,128)S(1)}, f32[16,384]{1,0:T(8,128)S(1)}, u32[]{:S(2)}, u32[]{:S(2)}) %collective-permute-start.1) | collective-permute-done | bytes 24608 | tf_op jit(solution)/shard_map/ppermute | solution.py:498
  11.2 1.5 %collective-permute-start.2 = (f32[32,384]{1,0:T(8,128)S(1)}, f32[32,384]{1,0:T(8,128)S(1)}, u32[]{:S(2)}, u32[]{:S(2)}) collective-permute-start(f32[32,384]{1,0:T(8,128)S(1)} %get-tuple-element.31), channel_id=1, source_target_pairs={{0,2},{1,3},{2,0},{3,1},{4,6},{5,7},{6,4},{7,5},{8,10},{9,11},{10,... | collective-permute-start | bytes 147464 | tf_op jit(solution)/shard_map/ppermute | solution.py:498
  12.6 7.7 %collective-permute-start.6 = (f32[32,384]{1,0:T(8,128)S(1)}, f32[32,384]{1,0:T(8,128)S(1)}, u32[]{:S(2)}, u32[]{:S(2)}) collective-permute-start(f32[32,384]{1,0:T(8,128)S(1)} %get-tuple-element.32), channel_id=1, source_target_pairs={{0,126},{1,127},{2,4},{3,5},{4,2},{5,3},{6,8},{7,9},{8,6},{9,7},{1... | collective-permute-start | bytes 147464 | tf_op jit(solution)/shard_map/ppermute | solution.py:498
  20.3 0.0 collective-permute-done.2.i2
  20.3 0.1 collective-permute-start.3
  20.4 0.8 %volume_first.1.before_ref = f32[5,512,128]{2,1,0:T(8,128)S(1)} custom-call(f32[8,128]{1,0:T(8,128)S(1)} %slice_maximum_fusion.turn_ref, f32[5,512,128]{2,1,0:T(8,128)S(1)} %copy-done.1), custom_call_target="tpu_custom_call" | custom-call | flops 1000000000 | bytes 2600000 | tf_op jit(solution)/shard_map/volume_first/pallas_call | solution.py:520
  21.3 2.2 %collective-permute-done.3 = f32[8,128]{1,0:T(8,128)S(1)} collective-permute-done((f32[8,128]{1,0:T(8,128)S(1)}, f32[8,128]{1,0:T(8,128)S(1)}, u32[]{:S(2)}, u32[]{:S(2)}) %collective-permute-start.3) | collective-permute-done | bytes 4128 | tf_op jit(solution)/shard_map/ppermute | solution.py:498
  23.4 0.0 collective-permute-done.6.i3
  23.5 1.5 %faces.1 = (f32[640,512]{1,0:T(8,128)S(1)}, f32[32,640]{1,0:T(8,128)S(1)}, f32[48,640]{1,0:T(8,128)S(1)}) custom-call(f32[8,128]{1,0:T(8,128)S(1)} %max.10.turn_ref, f32[336,512]{1,0:T(8,128)S(1)} %gather.1.turn_ref.gather_ref, f32[32,384]{1,0:T(8,128)S(1)} %collective-permute-done.chip_ref.i0, f32[32,384]{1,0:T(8,128)S(1)} %collective-permute-done.2.i2, ...), custom_call_target="tpu_custom_call" | custom-call | flops 1000000000 | bytes 3000000 | tf_op jit(solution)/shard_map/faces/pallas_call | solution.py:526
  25.0 0.1 collective-permute-start.7
  25.1 2.6 %collective-permute-done.4 = f32[8,128]{1,0:T(8,128)S(1)} collective-permute-done((f32[8,128]{1,0:T(8,128)S(1)}, f32[8,128]{1,0:T(8,128)S(1)}, u32[]{:S(2)}, u32[]{:S(2)}) %collective-permute-start.4) | collective-permute-done | bytes 4128 | tf_op jit(solution)/shard_map/ppermute | solution.py:498
  27.7 0.0 collective-permute-start.5
  27.7 0.9 %volume_second.1.before_ref = f32[5,512,128]{2,1,0:T(8,128)S(1)} custom-call(f32[8,128]{1,0:T(8,128)S(1)} %max.11.turn_ref, f32[5,512,128]{2,1,0:T(8,128)S(1)} %copy-done.1, f32[5,512,128]{2,1,0:T(8,128)S(1)} %volume_first.1.before_ref), custom_call_target="tpu_custom_call" | custom-call | flops 1000000000 | bytes 3900000 | tf_op jit(solution)/shard_map/volume_second/pallas_call | solution.py:534
  28.6 2.2 %collective-permute-done.5.last_ref = f32[8,128]{1,0:T(8,128)S(1)} collective-permute-done((f32[8,128]{1,0:T(8,128)S(1)}, f32[8,128]{1,0:T(8,128)S(1)}, u32[]{:S(2)}, u32[]{:S(2)}) %collective-permute-start.5) | collective-permute-done | bytes 4128 | tf_op jit(solution)/shard_map/ppermute | solution.py:498
  30.7 0.0 collective-permute-done.7.chip_ref.i0
  30.8 0.1 collective-permute-start.9
  30.8 3.9 %collective-permute-start.8 = (f32[32,768]{1,0:T(8,128)S(1)}, f32[32,768]{1,0:T(8,128)S(1)}, u32[]{:S(2)}, u32[]{:S(2)}) collective-permute-start(f32[32,768]{1,0:T(8,128)S(1)} %get-tuple-element.40), channel_id=1, source_target_pairs={{0,126},{1,127},{2,4},{3,5},{4,2},{5,3},{6,8},{7,9},{8,6},{9,7},{1... | collective-permute-start | bytes 294920 | tf_op jit(solution)/shard_map/ppermute | solution.py:498
  34.8 0.0 collective-permute-start.10
  34.8 1.6 %volume_third.1.volume_ref = f32[5,512,128]{2,1,0:T(8,128)S(1)} custom-call(f32[8,128]{1,0:T(8,128)S(1)} %get-tuple-element.35.turn_ref.fast_ref, f32[5,512,128]{2,1,0:T(8,128)S(1)} %copy-done.1, f32[5,512,128]{2,1,0:T(8,128)S(1)} %volume_second.1.before_ref, f32[256,256]{1,0:T(8,128)S(1)} %copy-done.2), custom_call_target="tpu_custom_call" | custom-call | flops 1000000000 | bytes 6000000 | tf_op jit(solution)/shard_map/volume_third/pallas_call | solution.py:546
  36.4 1.5 %lift.1 = (f32[5,512,128]{2,1,0:T(8,128)S(1)}, f32[5,512,128]{2,1,0:T(8,128)S(1)}) custom-call(f32[8,128]{1,0:T(8,128)S(1)} %get-tuple-element.35.turn_ref.fast_ref, f32[640,512]{1,0:T(8,128)S(1)} %get-tuple-element.36.corr_ref, s32[5,32]{1,0:T(8,128)S(1)} %bitcast.10, s32[2,128]{1,0:T(2,128)S(1)} %bitcast.13, f32[5,512,128]{2,1,0:T(8,128)S(1)} %volume_third.1.volume_ref, ...), custom_call_target="tpu_custom_call" | custom-call | flops 1500000000 | bytes 6000000 | tf_op jit(solution)/shard_map/lift/pallas_call | solution.py:549
  37.9 0.0 collective-permute-done.9.i4
  37.9 3.1 %collective-permute-done.8.i3 = f32[32,768]{1,0:T(8,128)S(1)} collective-permute-done((f32[32,768]{1,0:T(8,128)S(1)}, f32[32,768]{1,0:T(8,128)S(1)}, u32[]{:S(2)}, u32[]{:S(2)}) %collective-permute-start.8) | collective-permute-done | bytes 98336 | tf_op jit(solution)/shard_map/ppermute | solution.py:498
  41.0 2.0 %finish.1 = (f32[5,512,128]{2,1,0:T(8,128)}, f32[5,512,128]{2,1,0:T(8,128)}) custom-call(f32[5,512,128]{2,1,0:T(8,128)S(1)} %get-tuple-element.38.steady_ref, f32[5,512,128]{2,1,0:T(8,128)S(1)} %get-tuple-element.39.rate_ref, f32[5,512,128]{2,1,0:T(8,128)S(1)} %copy-done.1, f32[32,640]{1,0:T(8,128)S(1)} %collective-permute-done.7.chip_ref.i0, ...), custom_call_target="tpu_custom_call" | custom-call | flops 200000000 | bytes 6000000 | tf_op jit(solution)/shard_map/finish/pallas_call | solution.py:553
  (25 shorter events, 0.1 us)
Async XLA Ops:
  0.6 2.5 %copy-start.4 = (f32[128]{0:T(128)S(1)}, f32[128]{0:T(128)}, u32[]{:S(2)}) copy-start(f32[128]{0:T(128)} %param.12) | copy-start | bytes 1540
  0.6 8.7 %copy-start.7 = (s32[128,2]{0,1:T(2,128)S(1)}, s32[128,2]{0,1:T(2,128)}, u32[]{:S(2)}) copy-start(s32[128,2]{0,1:T(2,128)} %param.16) | copy-start | bytes 3076
  1.3 1.3 %copy-start = (f32[5,512,128]{2,1,0:T(8,128)S(1)}, f32[5,512,128]{2,1,0:T(8,128)}, u32[]{:S(2)}) copy-start(f32[5,512,128]{2,1,0:T(8,128)} %state_ref.9) | copy-start | bytes 3932164
  2.6 0.7 %copy-start.3 = (s32[128,16]{0,1:T(8,128)S(1)}, s32[128,16]{0,1:T(8,128)}, u32[]{:S(2)}) copy-start(s32[128,16]{0,1:T(8,128)} %param.14) | copy-start | bytes 24580
  2.6 6.7 %copy-start.6 = (s32[32,5]{0,1:T(8,128)S(1)}, s32[32,5]{0,1:T(8,128)}, u32[]{:S(2)}) copy-start(s32[32,5]{0,1:T(8,128)} %param.15) | copy-start | bytes 1924
  4.0 1.3 %collective-permute-start = (f32[32,384]{1,0:T(8,128)S(1)}, f32[32,384]{1,0:T(8,128)S(1)}, u32[]{:S(2)}, u32[]{:S(2)}) collective-permute-start(f32[32,384]{1,0:T(8,128)S(1)} %get-tuple-element.26), channel_id=1, source_target_pairs={{0,1},{1,0},{2,3},{3,2},{4,5},{5,4},{6,7},{7,6},{8,9},{9,8},{10,11... | collective-permute-start | bytes 147464 | tf_op jit(solution)/shard_map/ppermute | solution.py:498
  5.3 5.8 %collective-permute-start.1 = (f32[16,384]{1,0:T(8,128)S(1)}, f32[16,384]{1,0:T(8,128)S(1)}, u32[]{:S(2)}, u32[]{:S(2)}) collective-permute-start(f32[16,384]{1,0:T(8,128)S(1)} %get-tuple-element.28), channel_id=1, source_target_pairs={{0,64},{1,65},{2,66},{3,67},{4,68},{5,69},{6,70},{7,71},{8,72},{9,... | collective-permute-start | bytes 73736 | tf_op jit(solution)/shard_map/ppermute | solution.py:498
  9.3 11.1 %copy-start.1 = (f32[5,512,128]{2,1,0:T(8,128)S(1)}, f32[5,512,128]{2,1,0:T(8,128)}, u32[]{:S(2)}) copy-start(f32[5,512,128]{2,1,0:T(8,128)} %state_ref.9) | copy-start | bytes 3932164
  11.2 9.2 %collective-permute-start.2 = (f32[32,384]{1,0:T(8,128)S(1)}, f32[32,384]{1,0:T(8,128)S(1)}, u32[]{:S(2)}, u32[]{:S(2)}) collective-permute-start(f32[32,384]{1,0:T(8,128)S(1)} %get-tuple-element.31), channel_id=1, source_target_pairs={{0,2},{1,3},{2,0},{3,1},{4,6},{5,7},{6,4},{7,5},{8,10},{9,11},{10,... | collective-permute-start | bytes 147464 | tf_op jit(solution)/shard_map/ppermute | solution.py:498
  12.6 10.8 %collective-permute-start.6 = (f32[32,384]{1,0:T(8,128)S(1)}, f32[32,384]{1,0:T(8,128)S(1)}, u32[]{:S(2)}, u32[]{:S(2)}) collective-permute-start(f32[32,384]{1,0:T(8,128)S(1)} %get-tuple-element.32), channel_id=1, source_target_pairs={{0,126},{1,127},{2,4},{3,5},{4,2},{5,3},{6,8},{7,9},{8,6},{9,7},{1... | collective-permute-start | bytes 147464 | tf_op jit(solution)/shard_map/ppermute | solution.py:498
  20.3 3.1 %copy-start.8 = (bf16[256,256]{1,0:T(8,128)(2,1)S(1)}, bf16[256,256]{1,0:T(8,128)(2,1)}, u32[]{:S(2)}) copy-start(bf16[256,256]{1,0:T(8,128)(2,1)} %constant.7.clone.back_ref) | copy-start | bytes 393220
  20.3 3.1 %copy-start.9 = (bf16[256,256]{1,0:T(8,128)(2,1)S(1)}, bf16[256,256]{1,0:T(8,128)(2,1)}, u32[]{:S(2)}) copy-start(bf16[256,256]{1,0:T(8,128)(2,1)} %constant.6.clone.project_ref) | copy-start | bytes 393220
  20.3 3.1 %collective-permute-start.3 = (f32[8,128]{1,0:T(8,128)S(1)}, f32[8,128]{1,0:T(8,128)S(1)}, u32[]{:S(2)}, u32[]{:S(2)}) collective-permute-start(f32[8,128]{1,0:T(8,128)S(1)} %slice_maximum_fusion.turn_ref), channel_id=1, source_target_pairs={{0,9},{1,8},{2,11},{3,10},{4,13},{5,12},{6,15},{7,14},{8,1},{9,0},... | collective-permute-start | bytes 12296 | tf_op jit(solution)/shard_map/ppermute | solution.py:498
  23.4 4.2 %collective-permute-start.4 = (f32[8,128]{1,0:T(8,128)S(1)}, f32[8,128]{1,0:T(8,128)S(1)}, u32[]{:S(2)}, u32[]{:S(2)}) collective-permute-start(f32[8,128]{1,0:T(8,128)S(1)} %max.10.turn_ref), channel_id=1, source_target_pairs={{0,25},{1,24},{2,27},{3,26},{4,29},{5,28},{6,31},{7,30},{8,17},{9,... | collective-permute-start | bytes 12296 | tf_op jit(solution)/shard_map/ppermute | solution.py:498
  25.0 5.8 %collective-permute-start.7 = (f32[32,640]{1,0:T(8,128)S(1)}, f32[32,640]{1,0:T(8,128)S(1)}, u32[]{:S(2)}, u32[]{:S(2)}) collective-permute-start(f32[32,640]{1,0:T(8,128)S(1)} %get-tuple-element.34), channel_id=1, source_target_pairs={{0,1},{1,0},{2,3},{3,2},{4,5},{5,4},{6,7},{7,6},{8,9},{9,8},{10,11... | collective-permute-start | bytes 245768 | tf_op jit(solution)/shard_map/ppermute | solution.py:498
  27.7 7.1 %copy-start.2 = (f32[256,256]{1,0:T(8,128)S(1)}, f32[256,256]{1,0:T(8,128)}, u32[]{:S(2)}) copy-start(f32[256,256]{1,0:T(8,128)} %constant.8.clone.mix_ref) | copy-start | bytes 786436
  27.7 3.0 %collective-permute-start.5 = (f32[8,128]{1,0:T(8,128)S(1)}, f32[8,128]{1,0:T(8,128)S(1)}, u32[]{:S(2)}, u32[]{:S(2)}) collective-permute-start(f32[8,128]{1,0:T(8,128)S(1)} %max.11.turn_ref), channel_id=1, source_target_pairs={{0,33},{1,32},{2,35},{3,34},{4,37},{5,36},{6,39},{7,38},{8,41},{9,... | collective-permute-start | bytes 12296 | tf_op jit(solution)/shard_map/ppermute | solution.py:498
  30.8 7.1 %collective-permute-start.9 = (f32[16,640]{1,0:T(8,128)S(1)}, f32[16,640]{1,0:T(8,128)S(1)}, u32[]{:S(2)}, u32[]{:S(2)}) collective-permute-start(f32[16,640]{1,0:T(8,128)S(1)} %get-tuple-element.41), channel_id=1, source_target_pairs={{0,64},{1,65},{2,66},{3,67},{4,68},{5,69},{6,70},{7,71},{8,72},{9,... | collective-permute-start | bytes 122888 | tf_op jit(solution)/shard_map/ppermute | solution.py:498
  30.8 10.1 %collective-permute-start.8 = (f32[32,768]{1,0:T(8,128)S(1)}, f32[32,768]{1,0:T(8,128)S(1)}, u32[]{:S(2)}, u32[]{:S(2)}) collective-permute-start(f32[32,768]{1,0:T(8,128)S(1)} %get-tuple-element.40), channel_id=1, source_target_pairs={{0,126},{1,127},{2,4},{3,5},{4,2},{5,3},{6,8},{7,9},{8,6},{9,7},{1... | collective-permute-start | bytes 294920 | tf_op jit(solution)/shard_map/ppermute | solution.py:498
  34.8 6.2 %collective-permute-start.10 = (f32[32,768]{1,0:T(8,128)S(1)}, f32[32,768]{1,0:T(8,128)S(1)}, u32[]{:S(2)}, u32[]{:S(2)}) collective-permute-start(f32[32,768]{1,0:T(8,128)S(1)} %get-tuple-element.42), channel_id=1, source_target_pairs={{0,2},{1,3},{2,0},{3,1},{4,6},{5,7},{6,4},{7,5},{8,10},{9,11},{10,... | collective-permute-start | bytes 294920 | tf_op jit(solution)/shard_map/ppermute | solution.py:498
  34.8 1.6 %copy-start.5 = (f32[5,512,128]{2,1,0:T(8,128)S(1)}, f32[5,512,128]{2,1,0:T(8,128)}, u32[]{:S(2)}) copy-start(f32[5,512,128]{2,1,0:T(8,128)} %register_ref.1) | copy-start | bytes 3932164

commit v6 on v5

--- a/solution.py
+++ b/solution.py
@@ -347,7 +347,7 @@
 
 def face_kernel(
     devices, turn_ref, gather_ref, i0, i2, i3, i4, mortar_ref, face_ref, project_ref, back_ref,
-    corr_ref, chip_ref, raw_ref, pool_ref
+    corr_ref, chip_ref, raw_ref, far_ref, pool_ref
 ):
     partners = partner_of(lax.axis_index("sfc"), devices)
     incoming = gather_blocks(devices, i0, i2, i3, i4, slice(0, 384))
@@ -389,15 +389,15 @@
         corr_ref[more, 384:512] = -jump
     back = sum(dot_nt(part, remote) for part in split2(corr_ref[...])).T
     chip_ref[...] = back[0 : 2 * WIDTH]
-    raw_ref[...] = back[2 * WIDTH : 5 * WIDTH]
-
-
-def reply_kernel(turn_ref, last_ref, raw_ref, chip_ref, pair_ref, next_ref, far_ref, best_ref):
+    raw_ref[...] = back[2 * WIDTH : 4 * WIDTH]
+    far_ref[...] = back[4 * WIDTH : 5 * WIDTH]
+
+
+def reply_kernel(turn_ref, last_ref, raw_ref, chip_ref, pair_ref, next_ref, best_ref):
     best = jnp.maximum(turn_ref[...], last_ref[...])
     best_ref[...] = best
     pair_ref[0:WIDTH, 0 : 2 * ROWS] = raw_ref[0:WIDTH, :]
     next_ref[0:WIDTH, 0 : 2 * ROWS] = raw_ref[WIDTH : 2 * WIDTH, :]
-    far_ref[...] = raw_ref[2 * WIDTH : 3 * WIDTH, :]
     for ref in (pair_ref, next_ref):
         ref[WIDTH : 2 * WIDTH, 0 : 2 * ROWS] = chip_ref[WIDTH : 2 * WIDTH, :]
     for ref in (pair_ref, next_ref):
@@ -523,25 +523,28 @@
     )(fast, state)
     fast = jnp.maximum(fast, came)
     came = exchange(fast, "y_second")
-    corrections, chip, raw = call(
+    corrections, chip, raw, far = call(
         functools.partial(face_kernel, devices), "faces",
-        [((2 * ROWS, 512), F32), ((2 * WIDTH, 2 * ROWS), F32), ((3 * WIDTH, 2 * ROWS), F32)],
+        [
+            ((2 * ROWS, 512), F32), ((2 * WIDTH, 2 * ROWS), F32), ((2 * WIDTH, 2 * ROWS), F32),
+            ((WIDTH, 2 * ROWS), F32),
+        ],
         [VMEM] * 10, (1_000_000_000, 3_000_000), [pltpu.VMEM((ROWS, 512), F32)],
     )(fast, gathered, chip, pair, onward, far, mortars, faces, stack_terms(project), stack_terms(back))
     fast = jnp.maximum(fast, came)
     came = exchange(fast, "z_first")
     chip = exchange(chip, "chip")
+    far = exchange(far, "far")
     (volume,) = call(
         functools.partial(second_kernel, deriv), "volume_second", [(cube, F32)], [VMEM] * 3,
         (1_000_000_000, 3_900_000), flux,
     )(fast, state, volume)
     wide = 2 * ROWS + ELEMS
-    pair, onward, far, fast = call(
+    pair, onward, fast = call(
         reply_kernel, "reply",
-        [((2 * WIDTH, wide), F32)] * 2 + [((WIDTH, 2 * ROWS), F32), row], [VMEM] * 4, (0, 500_000),
+        [((2 * WIDTH, wide), F32)] * 2 + [row], [VMEM] * 4, (0, 500_000),
     )(fast, came, raw, chip)
     onward = exchange(onward, "next")
-    far = exchange(far, "far")
     pair = exchange(pair, "pair")
     (volume,) = call(
         third_kernel, "volume_third", [(cube, F32)], [VMEM] * 4, (1_000_000_000, 6_000_000), flux,

time: 43.2 us -> 43.1 us (level)
  waiting for transfers between devices: 12.3 us -> 11 us
  starting transfers between devices: 17.5 us -> 18.7 us
    ppermute x11, waiting for transfers between devices: 12.3 us -> 11 us  [exchange(): return lax.ppermute(value, 'sfc', pairs[name])]
    ppermute x11, starting transfers between devices: 17.5 us -> 18.7 us  [exchange(): return lax.ppermute(value, 'sfc', pairs[name])]
where the time goes in v6:
time: 43.1 us; the launch traced here: 42.9 us
  starting transfers between devices  18.7 us (43%)
  waiting for transfers between devices  11 us (26%)
  Pallas kernels  10.2 us (24%)
  local copies, waits for them, and re-layouts  1.58 us (4%)
  between operations  1.46 us (3%)
    ppermute x11, starting transfers between devices, exchange(): return lax.ppermute(value, 'sfc', pairs[name])  18.7 us
    ppermute x11, waiting for transfers between devices, exchange(): return lax.ppermute(value, 'sfc', pairs[name])  11 us
    pallas_call x1, Pallas kernels, per_device(): call(functools.partial(finish_kernel, devices), 'finish', [(cube, F32)] *...  2.02 us
    pallas_call x1, Pallas kernels, per_device(): call(third_kernel, 'volume_third', [(cube, F32)], [VMEM] * 4, (1000000000...  1.61 us
    unnamed x20, local copies, waits for them, and re-layouts  1.58 us
    pallas_call x1, Pallas kernels, per_device(): call(functools.partial(face_kernel, devices), 'faces', [((2 * ROWS, 512),...  1.49 us
    pallas_call x1, Pallas kernels, per_device(): call(lift_kernel, 'lift', [(cube, F32)] * 2, [VMEM] * 7, (1500000000, 600...  1.48 us
    pallas_call x1, Pallas kernels, per_device(): call(functools.partial(second_kernel, deriv), 'volume_second', [(cube, F3...  0.87 us
  transfers between devices with their start and end apart: 11, of which 6 were waited for; matrix products, arithmetic and copies ran while one was open for 0% of the time, Pallas kernels for 16%

profile of v6, /device:TPU:0, one launch (start us, length us, event | category | flops | bytes accessed | tf_op | source)
XLA Modules:
  0.0 42.9 jit_solution(15905246779449748051)
XLA Ops:
  1.3 0.0 copy-start
  1.3 1.3 %copy-done = f32[5,512,128]{2,1,0:T(8,128)S(1)} copy-done((f32[5,512,128]{2,1,0:T(8,128)S(1)}, f32[5,512,128]{2,1,0:T(8,128)}, u32[]{:S(2)}) %copy-start) | copy-done | bytes 1310744
  2.6 0.4 %table.1 = (bf16[656,768]{1,0:T(8,128)(2,1)S(1)}, f32[8,128]{1,0:T(8,128)S(1)}) custom-call(f32[5,512,128]{2,1,0:T(8,128)S(1)} %copy-done), custom_call_target="tpu_custom_call" | custom-call | flops 100000000 | bytes 3000000 | tf_op jit(solution)/shard_map/table/pallas_call | solution.py:502
  3.1 0.2 copy-done.3
  3.3 0.6 %send.1 = (f32[32,384]{1,0:T(8,128)S(1)}, f32[48,384]{1,0:T(8,128)S(1)}, f32[8,128]{1,0:T(8,128)S(1)}, f32[8,128]{1,0:T(8,128)S(1)}, bf16[128,768]{1,0:T(8,128)(2,1)S(1)}) custom-call(bf16[656,768]{1,0:T(8,128)(2,1)S(1)} %get-tuple-element.23.split_ref, f32[8,128]{1,0:T(8,128)S(1)} %get-tuple-element.24.speed_ref, s32[1,1]{1,0:T(1,128)} %bitcast.5.count_ref, ...), custom_call_target="tpu_custom_call" | custom-call | flops 200000000 | bytes 2000000 | tf_op jit(solution)/shard_map/send/pallas_call | solution.py:505
  4.0 0.1 collective-permute-start
  4.1 1.2 %collective-permute-done.chip_ref.i0 = f32[32,384]{1,0:T(8,128)S(1)} collective-permute-done((f32[32,384]{1,0:T(8,128)S(1)}, f32[32,384]{1,0:T(8,128)S(1)}, u32[]{:S(2)}, u32[]{:S(2)}) %collective-permute-start) | collective-permute-done | bytes 49184 | tf_op jit(solution)/shard_map/ppermute | solution.py:498
  5.3 4.0 %collective-permute-start.1 = (f32[16,384]{1,0:T(8,128)S(1)}, f32[16,384]{1,0:T(8,128)S(1)}, u32[]{:S(2)}, u32[]{:S(2)}) collective-permute-start(f32[16,384]{1,0:T(8,128)S(1)} %get-tuple-element.28), channel_id=1, source_target_pairs={{0,64},{1,65},{2,66},{3,67},{4,68},{5,69},{6,70},{7,71},{8,72},{9,... | collective-permute-start | bytes 73736 | tf_op jit(solution)/shard_map/ppermute | solution.py:498
  9.3 0.8 %gather.1.turn_ref.gather_ref = f32[336,512]{1,0:T(8,128)S(1)} custom-call(bf16[656,768]{1,0:T(8,128)(2,1)S(1)} %get-tuple-element.23.split_ref, s32[5,32]{1,0:T(8,128)S(1)} %bitcast.8, s32[2,128]{1,0:T(2,128)S(1)} %bitcast.11), custom_call_target="tpu_custom_call" | custom-call | flops 1000000000 | bytes 2000000 | tf_op jit(solution)/shard_map/gather/pallas_call | solution.py:513
  10.1 1.0 %collective-permute-done.1.far_ref.i4 = f32[16,384]{1,0:T(8,128)S(1)} collective-permute-done((f32[16,384]{1,0:T(8,128)S(1)}, f32[16,384]{1,0:T(8,128)S(1)}, u32[]{:S(2)}, u32[]{:S(2)}) %collective-permute-start.1) | collective-permute-done | bytes 24608 | tf_op jit(solution)/shard_map/ppermute | solution.py:498
  11.2 1.5 %collective-permute-start.2 = (f32[32,384]{1,0:T(8,128)S(1)}, f32[32,384]{1,0:T(8,128)S(1)}, u32[]{:S(2)}, u32[]{:S(2)}) collective-permute-start(f32[32,384]{1,0:T(8,128)S(1)} %get-tuple-element.31), channel_id=1, source_target_pairs={{0,2},{1,3},{2,0},{3,1},{4,6},{5,7},{6,4},{7,5},{8,10},{9,11},{10,... | collective-permute-start | bytes 147464 | tf_op jit(solution)/shard_map/ppermute | solution.py:498
  12.6 7.7 %collective-permute-start.6 = (f32[32,384]{1,0:T(8,128)S(1)}, f32[32,384]{1,0:T(8,128)S(1)}, u32[]{:S(2)}, u32[]{:S(2)}) collective-permute-start(f32[32,384]{1,0:T(8,128)S(1)} %get-tuple-element.32), channel_id=1, source_target_pairs={{0,126},{1,127},{2,4},{3,5},{4,2},{5,3},{6,8},{7,9},{8,6},{9,7},{1... | collective-permute-start | bytes 147464 | tf_op jit(solution)/shard_map/ppermute | solution.py:498
  20.3 0.0 collective-permute-done.2.i2
  20.3 0.1 collective-permute-start.3
  20.4 0.8 %volume_first.1.before_ref = f32[5,512,128]{2,1,0:T(8,128)S(1)} custom-call(f32[8,128]{1,0:T(8,128)S(1)} %slice_maximum_fusion.turn_ref, f32[5,512,128]{2,1,0:T(8,128)S(1)} %copy-done.1), custom_call_target="tpu_custom_call" | custom-call | flops 1000000000 | bytes 2600000 | tf_op jit(solution)/shard_map/volume_first/pallas_call | solution.py:520
  21.3 2.2 %collective-permute-done.3 = f32[8,128]{1,0:T(8,128)S(1)} collective-permute-done((f32[8,128]{1,0:T(8,128)S(1)}, f32[8,128]{1,0:T(8,128)S(1)}, u32[]{:S(2)}, u32[]{:S(2)}) %collective-permute-start.3) | collective-permute-done | bytes 4128 | tf_op jit(solution)/shard_map/ppermute | solution.py:498
  23.4 0.0 collective-permute-start.4
  23.4 0.0 collective-permute-done.6.i3
  23.5 1.5 %faces.1 = (f32[640,512]{1,0:T(8,128)S(1)}, f32[32,640]{1,0:T(8,128)S(1)}, f32[32,640]{1,0:T(8,128)S(1)}, f32[16,640]{1,0:T(8,128)S(1)}) custom-call(f32[8,128]{1,0:T(8,128)S(1)} %max.10.turn_ref, f32[336,512]{1,0:T(8,128)S(1)} %gather.1.turn_ref.gather_ref, f32[32,384]{1,0:T(8,128)S(1)} %collective-permute-done.chip_ref.i0, ...), custom_call_target="tpu_custom_call" | custom-call | flops 1000000000 | bytes 3000000 | tf_op jit(solution)/shard_map/faces/pallas_call | solution.py:526
  25.0 1.1 %collective-permute-start.9 = (f32[16,640]{1,0:T(8,128)S(1)}, f32[16,640]{1,0:T(8,128)S(1)}, u32[]{:S(2)}, u32[]{:S(2)}) collective-permute-start(f32[16,640]{1,0:T(8,128)S(1)} %get-tuple-element.41), channel_id=1, source_target_pairs={{0,64},{1,65},{2,66},{3,67},{4,68},{5,69},{6,70},{7,71},{8,72},{9,... | collective-permute-start | bytes 122888 | tf_op jit(solution)/shard_map/ppermute | solution.py:498
  26.1 0.2 collective-permute-start.7
  26.2 1.4 %collective-permute-done.4 = f32[8,128]{1,0:T(8,128)S(1)} collective-permute-done((f32[8,128]{1,0:T(8,128)S(1)}, f32[8,128]{1,0:T(8,128)S(1)}, u32[]{:S(2)}, u32[]{:S(2)}) %collective-permute-start.4) | collective-permute-done | bytes 4128 | tf_op jit(solution)/shard_map/ppermute | solution.py:498
  27.7 0.0 collective-permute-start.5
  27.7 0.9 %volume_second.1.before_ref = f32[5,512,128]{2,1,0:T(8,128)S(1)} custom-call(f32[8,128]{1,0:T(8,128)S(1)} %max.11.turn_ref, f32[5,512,128]{2,1,0:T(8,128)S(1)} %copy-done.1, f32[5,512,128]{2,1,0:T(8,128)S(1)} %volume_first.1.before_ref), custom_call_target="tpu_custom_call" | custom-call | flops 1000000000 | bytes 3900000 | tf_op jit(solution)/shard_map/volume_second/pallas_call | solution.py:538
  28.6 2.2 %collective-permute-done.5.last_ref = f32[8,128]{1,0:T(8,128)S(1)} collective-permute-done((f32[8,128]{1,0:T(8,128)S(1)}, f32[8,128]{1,0:T(8,128)S(1)}, u32[]{:S(2)}, u32[]{:S(2)}) %collective-permute-start.5) | collective-permute-done | bytes 4128 | tf_op jit(solution)/shard_map/ppermute | solution.py:498
  30.7 0.0 collective-permute-done.7.chip_ref.i0
  30.8 4.0 %collective-permute-start.8 = (f32[32,768]{1,0:T(8,128)S(1)}, f32[32,768]{1,0:T(8,128)S(1)}, u32[]{:S(2)}, u32[]{:S(2)}) collective-permute-start(f32[32,768]{1,0:T(8,128)S(1)} %get-tuple-element.40), channel_id=1, source_target_pairs={{0,126},{1,127},{2,4},{3,5},{4,2},{5,3},{6,8},{7,9},{8,6},{9,7},{1... | collective-permute-start | bytes 294920 | tf_op jit(solution)/shard_map/ppermute | solution.py:498
  34.8 1.6 %volume_third.1.volume_ref = f32[5,512,128]{2,1,0:T(8,128)S(1)} custom-call(f32[8,128]{1,0:T(8,128)S(1)} %get-tuple-element.35.turn_ref.fast_ref, f32[5,512,128]{2,1,0:T(8,128)S(1)} %copy-done.1, f32[5,512,128]{2,1,0:T(8,128)S(1)} %volume_second.1.before_ref, f32[256,256]{1,0:T(8,128)S(1)} %copy-done.2), custom_call_target="tpu_custom_call" | custom-call | flops 1000000000 | bytes 6000000 | tf_op jit(solution)/shard_map/volume_third/pallas_call | solution.py:549
  36.4 1.5 %lift.1 = (f32[5,512,128]{2,1,0:T(8,128)S(1)}, f32[5,512,128]{2,1,0:T(8,128)S(1)}) custom-call(f32[8,128]{1,0:T(8,128)S(1)} %get-tuple-element.35.turn_ref.fast_ref, f32[640,512]{1,0:T(8,128)S(1)} %get-tuple-element.36.corr_ref, s32[5,32]{1,0:T(8,128)S(1)} %bitcast.10, s32[2,128]{1,0:T(2,128)S(1)} %bitcast.13, f32[5,512,128]{2,1,0:T(8,128)S(1)} %volume_third.1.volume_ref, ...), custom_call_target="tpu_custom_call" | custom-call | flops 1500000000 | bytes 6000000 | tf_op jit(solution)/shard_map/lift/pallas_call | solution.py:552
  37.9 0.0 collective-permute-done.9.i4
  37.9 3.0 %collective-permute-done.8.i3 = f32[32,768]{1,0:T(8,128)S(1)} collective-permute-done((f32[32,768]{1,0:T(8,128)S(1)}, f32[32,768]{1,0:T(8,128)S(1)}, u32[]{:S(2)}, u32[]{:S(2)}) %collective-permute-start.8) | collective-permute-done | bytes 98336 | tf_op jit(solution)/shard_map/ppermute | solution.py:498
  40.9 2.0 %finish.1 = (f32[5,512,128]{2,1,0:T(8,128)}, f32[5,512,128]{2,1,0:T(8,128)}) custom-call(f32[5,512,128]{2,1,0:T(8,128)S(1)} %get-tuple-element.38.steady_ref, f32[5,512,128]{2,1,0:T(8,128)S(1)} %get-tuple-element.39.rate_ref, f32[5,512,128]{2,1,0:T(8,128)S(1)} %copy-done.1, f32[32,640]{1,0:T(8,128)S(1)} %collective-permute-done.7.chip_ref.i0, ...), custom_call_target="tpu_custom_call" | custom-call | flops 200000000 | bytes 6000000 | tf_op jit(solution)/shard_map/finish/pallas_call | solution.py:556
  (25 shorter events, 0.1 us)
Async XLA Ops:
  0.6 2.5 %copy-start.4 = (f32[128]{0:T(128)S(1)}, f32[128]{0:T(128)}, u32[]{:S(2)}) copy-start(f32[128]{0:T(128)} %param.12) | copy-start | bytes 1540
  0.6 8.7 %copy-start.7 = (s32[128,2]{0,1:T(2,128)S(1)}, s32[128,2]{0,1:T(2,128)}, u32[]{:S(2)}) copy-start(s32[128,2]{0,1:T(2,128)} %param.16) | copy-start | bytes 3076
  1.3 1.3 %copy-start = (f32[5,512,128]{2,1,0:T(8,128)S(1)}, f32[5,512,128]{2,1,0:T(8,128)}, u32[]{:S(2)}) copy-start(f32[5,512,128]{2,1,0:T(8,128)} %state_ref.9) | copy-start | bytes 3932164
  2.6 0.7 %copy-start.3 = (s32[128,16]{0,1:T(8,128)S(1)}, s32[128,16]{0,1:T(8,128)}, u32[]{:S(2)}) copy-start(s32[128,16]{0,1:T(8,128)} %param.14) | copy-start | bytes 24580
  2.6 6.7 %copy-start.6 = (s32[32,5]{0,1:T(8,128)S(1)}, s32[32,5]{0,1:T(8,128)}, u32[]{:S(2)}) copy-start(s32[32,5]{0,1:T(8,128)} %param.15) | copy-start | bytes 1924
  4.0 1.3 %collective-permute-start = (f32[32,384]{1,0:T(8,128)S(1)}, f32[32,384]{1,0:T(8,128)S(1)}, u32[]{:S(2)}, u32[]{:S(2)}) collective-permute-start(f32[32,384]{1,0:T(8,128)S(1)} %get-tuple-element.26), channel_id=1, source_target_pairs={{0,1},{1,0},{2,3},{3,2},{4,5},{5,4},{6,7},{7,6},{8,9},{9,8},{10,11... | collective-permute-start | bytes 147464 | tf_op jit(solution)/shard_map/ppermute | solution.py:498
  5.3 5.8 %collective-permute-start.1 = (f32[16,384]{1,0:T(8,128)S(1)}, f32[16,384]{1,0:T(8,128)S(1)}, u32[]{:S(2)}, u32[]{:S(2)}) collective-permute-start(f32[16,384]{1,0:T(8,128)S(1)} %get-tuple-element.28), channel_id=1, source_target_pairs={{0,64},{1,65},{2,66},{3,67},{4,68},{5,69},{6,70},{7,71},{8,72},{9,... | collective-permute-start | bytes 73736 | tf_op jit(solution)/shard_map/ppermute | solution.py:498
  9.3 11.1 %copy-start.1 = (f32[5,512,128]{2,1,0:T(8,128)S(1)}, f32[5,512,128]{2,1,0:T(8,128)}, u32[]{:S(2)}) copy-start(f32[5,512,128]{2,1,0:T(8,128)} %state_ref.9) | copy-start | bytes 3932164
  11.2 9.2 %collective-permute-start.2 = (f32[32,384]{1,0:T(8,128)S(1)}, f32[32,384]{1,0:T(8,128)S(1)}, u32[]{:S(2)}, u32[]{:S(2)}) collective-permute-start(f32[32,384]{1,0:T(8,128)S(1)} %get-tuple-element.31), channel_id=1, source_target_pairs={{0,2},{1,3},{2,0},{3,1},{4,6},{5,7},{6,4},{7,5},{8,10},{9,11},{10,... | collective-permute-start | bytes 147464 | tf_op jit(solution)/shard_map/ppermute | solution.py:498
  12.6 10.8 %collective-permute-start.6 = (f32[32,384]{1,0:T(8,128)S(1)}, f32[32,384]{1,0:T(8,128)S(1)}, u32[]{:S(2)}, u32[]{:S(2)}) collective-permute-start(f32[32,384]{1,0:T(8,128)S(1)} %get-tuple-element.32), channel_id=1, source_target_pairs={{0,126},{1,127},{2,4},{3,5},{4,2},{5,3},{6,8},{7,9},{8,6},{9,7},{1... | collective-permute-start | bytes 147464 | tf_op jit(solution)/shard_map/ppermute | solution.py:498
  20.3 3.1 %copy-start.8 = (bf16[256,256]{1,0:T(8,128)(2,1)S(1)}, bf16[256,256]{1,0:T(8,128)(2,1)}, u32[]{:S(2)}) copy-start(bf16[256,256]{1,0:T(8,128)(2,1)} %constant.7.clone.back_ref) | copy-start | bytes 393220
  20.3 3.1 %copy-start.9 = (bf16[256,256]{1,0:T(8,128)(2,1)S(1)}, bf16[256,256]{1,0:T(8,128)(2,1)}, u32[]{:S(2)}) copy-start(bf16[256,256]{1,0:T(8,128)(2,1)} %constant.6.clone.project_ref) | copy-start | bytes 393220
  20.3 3.1 %collective-permute-start.3 = (f32[8,128]{1,0:T(8,128)S(1)}, f32[8,128]{1,0:T(8,128)S(1)}, u32[]{:S(2)}, u32[]{:S(2)}) collective-permute-start(f32[8,128]{1,0:T(8,128)S(1)} %slice_maximum_fusion.turn_ref), channel_id=1, source_target_pairs={{0,9},{1,8},{2,11},{3,10},{4,13},{5,12},{6,15},{7,14},{8,1},{9,0},... | collective-permute-start | bytes 12296 | tf_op jit(solution)/shard_map/ppermute | solution.py:498
  23.4 4.2 %collective-permute-start.4 = (f32[8,128]{1,0:T(8,128)S(1)}, f32[8,128]{1,0:T(8,128)S(1)}, u32[]{:S(2)}, u32[]{:S(2)}) collective-permute-start(f32[8,128]{1,0:T(8,128)S(1)} %max.10.turn_ref), channel_id=1, source_target_pairs={{0,25},{1,24},{2,27},{3,26},{4,29},{5,28},{6,31},{7,30},{8,17},{9,... | collective-permute-start | bytes 12296 | tf_op jit(solution)/shard_map/ppermute | solution.py:498
  25.0 12.9 %collective-permute-start.9 = (f32[16,640]{1,0:T(8,128)S(1)}, f32[16,640]{1,0:T(8,128)S(1)}, u32[]{:S(2)}, u32[]{:S(2)}) collective-permute-start(f32[16,640]{1,0:T(8,128)S(1)} %get-tuple-element.41), channel_id=1, source_target_pairs={{0,64},{1,65},{2,66},{3,67},{4,68},{5,69},{6,70},{7,71},{8,72},{9,... | collective-permute-start | bytes 122888 | tf_op jit(solution)/shard_map/ppermute | solution.py:498
  26.1 4.7 %collective-permute-start.7 = (f32[32,640]{1,0:T(8,128)S(1)}, f32[32,640]{1,0:T(8,128)S(1)}, u32[]{:S(2)}, u32[]{:S(2)}) collective-permute-start(f32[32,640]{1,0:T(8,128)S(1)} %get-tuple-element.34), channel_id=1, source_target_pairs={{0,1},{1,0},{2,3},{3,2},{4,5},{5,4},{6,7},{7,6},{8,9},{9,8},{10,11... | collective-permute-start | bytes 245768 | tf_op jit(solution)/shard_map/ppermute | solution.py:498
  27.7 7.1 %copy-start.2 = (f32[256,256]{1,0:T(8,128)S(1)}, f32[256,256]{1,0:T(8,128)}, u32[]{:S(2)}) copy-start(f32[256,256]{1,0:T(8,128)} %constant.8.clone.mix_ref) | copy-start | bytes 786436
  27.7 3.0 %collective-permute-start.5 = (f32[8,128]{1,0:T(8,128)S(1)}, f32[8,128]{1,0:T(8,128)S(1)}, u32[]{:S(2)}, u32[]{:S(2)}) collective-permute-start(f32[8,128]{1,0:T(8,128)S(1)} %max.11.turn_ref), channel_id=1, source_target_pairs={{0,33},{1,32},{2,35},{3,34},{4,37},{5,36},{6,39},{7,38},{8,41},{9,... | collective-permute-start | bytes 12296 | tf_op jit(solution)/shard_map/ppermute | solution.py:498
  30.8 10.1 %collective-permute-start.8 = (f32[32,768]{1,0:T(8,128)S(1)}, f32[32,768]{1,0:T(8,128)S(1)}, u32[]{:S(2)}, u32[]{:S(2)}) collective-permute-start(f32[32,768]{1,0:T(8,128)S(1)} %get-tuple-element.40), channel_id=1, source_target_pairs={{0,126},{1,127},{2,4},{3,5},{4,2},{5,3},{6,8},{7,9},{8,6},{9,7},{1... | collective-permute-start | bytes 294920 | tf_op jit(solution)/shard_map/ppermute | solution.py:498
  34.8 6.1 %collective-permute-start.10 = (f32[32,768]{1,0:T(8,128)S(1)}, f32[32,768]{1,0:T(8,128)S(1)}, u32[]{:S(2)}, u32[]{:S(2)}) collective-permute-start(f32[32,768]{1,0:T(8,128)S(1)} %get-tuple-element.42), channel_id=1, source_target_pairs={{0,2},{1,3},{2,0},{3,1},{4,6},{5,7},{6,4},{7,5},{8,10},{9,11},{10,... | collective-permute-start | bytes 294920 | tf_op jit(solution)/shard_map/ppermute | solution.py:498
  34.8 1.6 %copy-start.5 = (f32[5,512,128]{2,1,0:T(8,128)S(1)}, f32[5,512,128]{2,1,0:T(8,128)}, u32[]{:S(2)}) copy-start(f32[5,512,128]{2,1,0:T(8,128)} %register_ref.1) | copy-start | bytes 3932164
